TPU v7x, 32 devices: a whole 2x2x4 slice. The times are simulated.
32 devices in a mesh: dp: 16 (over z, y, x), tensor: 2 (over core).
Axes of the slice: x: 2, y: 2, z: 4, core: 2. Of those that a mesh axis runs over, the one named last changes fastest.
Arguments:
- tokens: bfloat16 [4096, 1152], P('dp'), may hold values from -6 to 6
- segment_ids: int32 [4096], P('dp'), may hold values from 0 to 3, as said below
- timesteps: int32 [16, 4], P('dp'), may hold values from 0 to 999
- norm_gain: float32 [2, 2, 1152], replicated, may hold values from 0.5 to 1.5
- norm_bias: float32 [2, 2, 1152], replicated, may hold values from -3 to 3
- token_proj: bfloat16 [2, 3, 1152, 1152], P(None, None, None, 'tensor'), may hold values from -0.1875 to 0.1875
- time_proj: bfloat16 [2, 2, 1152, 1152], P(None, None, None, 'tensor'), may hold values from -0.1875 to 0.1875
- bias_table: float32 [2, 16, 1024], P(None, 'tensor'), may hold values from -4 to 4
- out_proj: bfloat16 [2, 1152, 1152], P(None, 'tensor'), may hold values from -0.1875 to 0.1875
- hidden_in: bfloat16 [2, 1152, 4608], P(None, None, 'tensor'), may hold values from -0.1875 to 0.1875
- hidden_out: bfloat16 [2, 4608, 1152], P(None, 'tensor'), may hold values from -0.09375 to 0.09375
- branch_bias: float32 [2, 2, 1152], replicated, may hold values from -3 to 3
- cotangent: bfloat16 [4096, 1152], P('dp'), may hold values from -6 to 6
Outputs:
- output_tokens: bfloat16 [4096, 1152], P('dp')
- gradient_tokens: bfloat16 [4096, 1152], P('dp')
- gradient_gain: float32 [2, 2, 1152], P(None, None, 'dp')
- gradient_shift: float32 [2, 2, 1152], P(None, None, 'dp')
- gradient_token_proj: float32 [2, 3, 1152, 1152], P(None, None, 'dp', 'tensor')
- gradient_time_proj: float32 [2, 2, 1152, 1152], P(None, None, 'dp', 'tensor')
- gradient_table: float32 [2, 16, 1024], P(None, 'tensor', 'dp')
- gradient_out_proj: float32 [2, 1152, 1152], P(None, ('tensor', 'dp'))
- gradient_hidden_in: float32 [2, 1152, 4608], P(None, 'dp', 'tensor')
- gradient_hidden_out: float32 [2, 4608, 1152], P(None, ('tensor', 'dp'))
- gradient_branch_bias: float32 [2, 2, 1152], P(None, None, 'dp')
Inputs may be any that keep to these rules, and one draw needn't show every extreme that they name: `segment_ids`: within each row of 256 tokens the image slots are numbered 0, 1, 2, ... in order of position. Each aligned block of 256 tokens of a row holds either one image of 16 x 16 latent patches or four images of (8) x (8) patches, each in raster order; some row holds only small images and some row a large one.
All inputs are finite; a program needn't handle non-finite values.
Results may differ from a plain program's by a relative error of at most 0.017.
Values sent between devices are 32-bit elements; how exact they have to be, the bound alone decides.
No kernel may reach another device: no remote copies, remote signals or barrier semaphores. Data moves between devices by JAX's collectives and lax.ppermute only.
A program may use at most 320 MiB of HBM per device.

v0:
```python
import math

import jax
import jax.numpy as jnp
from jax import lax
from jax.sharding import PartitionSpec as P

SIDE = 16


EPSILON = 1e-06
MASKED = -1e30
ROOT_HALF = 0.7071067811865476
SLOPE_NORM = 0.3989422804014327


def layer_norm(stream, gain, shift):
    center = stream - jnp.mean(stream, axis=-1, keepdims=True)
    inverse = lax.rsqrt(jnp.mean(center * center, axis=-1, keepdims=True) + EPSILON)
    normal = center * inverse
    return (normal * gain + shift, normal, inverse)


def norm_backward(normal, inverse, gain, upstream):
    gain_part = jnp.sum(upstream * normal, axis=0)
    shift_part = jnp.sum(upstream, axis=0)
    scaled = upstream * gain
    inner = (
        scaled
        - jnp.mean(scaled, axis=-1, keepdims=True)
        - normal * jnp.mean(scaled * normal, axis=-1, keepdims=True)
    )
    return (inner * inverse, gain_part, shift_part)


def sinusoid(steps, width):
    half = width // 2
    rates = jnp.exp(-math.log(10000.0) * jnp.arange(half, dtype=jnp.float32) / half)
    angles = steps.astype(jnp.float32)[..., None] * rates
    return jnp.concatenate([jnp.cos(angles), jnp.sin(angles)], axis=-1)


def gelu_value(hidden):
    return 0.5 * hidden * (1.0 + lax.erf(hidden * ROOT_HALF))


def gelu_slope(hidden):
    return (
        0.5 * (1.0 + lax.erf(hidden * ROOT_HALF))
        + hidden * jnp.exp(-0.5 * hidden * hidden) * SLOPE_NORM
    )


def block_layout(segment_block):
    span = segment_block.shape[1]
    large = segment_block[:, :1] == segment_block[:, -1:]
    inside = jnp.arange(span, dtype=jnp.int32)[None, :]
    place = jnp.where(large, inside, inside % (span // 4))
    side = jnp.where(large, SIDE, SIDE // 2).astype(jnp.int32)
    grid_row = place // side
    grid_col = place % side
    same = segment_block[:, :, None] == segment_block[:, None, :]
    return (grid_row, grid_col, same)


def position_tables(grid_row, grid_col):
    differences = jnp.arange(2 * SIDE, dtype=jnp.int32)
    grid_cells = jnp.arange(SIDE, dtype=jnp.int32)
    row_pick = (
        grid_row[:, None, None, :] - grid_cells[None, :, None, None] + SIDE
        == differences[None, None, :, None]
    ).astype(jnp.float32)
    col_pick = (
        grid_col[:, None, None, :] - grid_cells[None, :, None, None] + SIDE
        == differences[None, None, :, None]
    ).astype(jnp.float32)
    key_pick = (grid_row[:, None, None, :] == grid_cells[None, :, None, None]) & (
        grid_col[:, None, None, :] == grid_cells[None, None, :, None]
    )
    return (row_pick, col_pick, key_pick)


def position_bias(table, row_pick, col_pick, key_pick_full):
    heads = table.shape[0]
    square = table.reshape(heads, 2 * SIDE, 2 * SIDE)
    by_column = jnp.einsum("hae,bceq->bhcaq", square, col_pick, precision=lax.Precision.HIGHEST)
    by_cell = jnp.einsum("bhcaq,braq->bhrcq", by_column, row_pick, precision=lax.Precision.HIGHEST)
    return jnp.einsum("bhrcq,brck->hbqk", by_cell, key_pick_full, precision=lax.Precision.HIGHEST)


def table_gradient(back_scores, row_pick, col_pick, key_pick_low):
    by_cell = jnp.einsum(
        "hbqk,brck->bhrcq", back_scores, key_pick_low, preferred_element_type=jnp.float32
    )
    by_column = jnp.einsum("bhrcq,braq->bhcaq", by_cell, row_pick, precision=lax.Precision.HIGHEST)
    square = jnp.einsum("bhcaq,bceq->hae", by_column, col_pick, precision=lax.Precision.HIGHEST)
    return square.reshape(square.shape[0], 4 * SIDE * SIDE)


def to_blocks(rows, blocks, heads):
    return rows.reshape(blocks, rows.shape[0] // blocks, heads, rows.shape[1] // heads)


def masked_scores(queries, keys, position, same, scale):
    scores = (
        jnp.einsum("bqhd,bkhd->hbqk", queries, keys, preferred_element_type=jnp.float32) * scale
    )
    scores = scores + position
    return jnp.where(same[None], scores, MASKED)


def local(
    tokens,
    segment_ids,
    timesteps,
    norm_gain,
    norm_bias,
    token_proj,
    time_proj,
    bias_table,
    out_proj,
    hidden_in,
    hidden_out,
    branch_bias,
    cotangent,
):
    count = tokens.shape[0]
    width = tokens.shape[1]
    local_width = token_proj.shape[3]
    local_heads = bias_table.shape[1]
    depth = token_proj.shape[0]
    slots = timesteps.shape[1]
    span = SIDE * SIDE
    blocks = count // span
    scale = 1.0 / math.sqrt(local_width // local_heads)
    grid_row, grid_col, same = block_layout(segment_ids.reshape(blocks, span))
    row_pick, col_pick, key_pick = position_tables(grid_row, grid_col)
    key_pick_full = key_pick.astype(jnp.float32)
    key_pick_low = key_pick.astype(jnp.bfloat16)
    one_hot = segment_ids[:, None] == jnp.arange(slots, dtype=jnp.int32)[None, :]
    one_hot_low = one_hot.astype(jnp.bfloat16)
    one_hot_full = one_hot.astype(jnp.float32)
    embedded = sinusoid(timesteps[0], width).astype(jnp.bfloat16)
    stream = tokens.astype(jnp.float32)
    saved = []
    for layer in range(depth):
        normed, normal_first, inverse_first = layer_norm(
            stream, norm_gain[layer, 0], norm_bias[layer, 0]
        )
        normed_first = normed.astype(jnp.bfloat16)
        per_image = jnp.einsum(
            "sd,jde->jse", embedded, time_proj[layer], preferred_element_type=jnp.float32
        )
        per_token = jnp.einsum(
            "ts,jse->jte", one_hot_full, per_image, precision=lax.Precision.HIGHEST
        )
        projected = jnp.einsum(
            "td,jde->jte", normed_first, token_proj[layer], preferred_element_type=jnp.float32
        )
        query_blocks = to_blocks(
            (projected[0] + per_token[0]).astype(jnp.bfloat16), blocks, local_heads
        )
        key_blocks = to_blocks(projected[1].astype(jnp.bfloat16), blocks, local_heads)
        value_blocks = to_blocks(
            (projected[2] + per_token[1]).astype(jnp.bfloat16), blocks, local_heads
        )
        position = position_bias(bias_table[layer], row_pick, col_pick, key_pick_full)
        masked = masked_scores(query_blocks, key_blocks, position, same, scale)
        peak = jnp.max(masked, axis=-1, keepdims=True)
        expo = jnp.exp(masked - peak)
        total = jnp.sum(expo, axis=-1, keepdims=True)
        weights = expo / total
        held = (peak + jnp.log(total), position)
        attended = jnp.einsum(
            "hbqk,bkhd->bqhd",
            weights.astype(jnp.bfloat16),
            value_blocks,
            preferred_element_type=jnp.float32,
        )
        attended = attended.reshape(count, local_width).astype(jnp.bfloat16)
        partial_attention = jnp.dot(attended, out_proj[layer], preferred_element_type=jnp.float32)
        middle = stream + lax.psum(partial_attention, "tensor") + branch_bias[layer, 0]
        normed, normal_second, inverse_second = layer_norm(
            middle, norm_gain[layer, 1], norm_bias[layer, 1]
        )
        normed_second = normed.astype(jnp.bfloat16)
        hidden = jnp.dot(normed_second, hidden_in[layer], preferred_element_type=jnp.float32)
        activated = gelu_value(hidden).astype(jnp.bfloat16)
        partial_feed = jnp.dot(activated, hidden_out[layer], preferred_element_type=jnp.float32)
        next_stream = middle + lax.psum(partial_feed, "tensor") + branch_bias[layer, 1]
        saved.append(
            (
                normed_first,
                normal_first,
                inverse_first,
                query_blocks,
                key_blocks,
                value_blocks,
                held,
                attended,
                normal_second,
                inverse_second,
                normed_second,
                hidden,
                activated,
            )
        )
        stream = next_stream
    output = stream.astype(jnp.bfloat16)
    upstream = cotangent.astype(jnp.float32)
    collected = [None] * depth
    for layer in reversed(range(depth)):
        (
            normed_first,
            normal_first,
            inverse_first,
            query_blocks,
            key_blocks,
            value_blocks,
            held,
            attended,
            normal_second,
            inverse_second,
            normed_second,
            hidden,
            activated,
        ) = saved[layer]
        back_feed = upstream.astype(jnp.bfloat16)
        feed_bias = jnp.sum(back_feed.astype(jnp.float32), axis=0)
        outer_weight = jnp.einsum(
            "tf,td->fd", activated, back_feed, preferred_element_type=jnp.float32
        )
        back_active = jnp.einsum(
            "td,fd->tf", back_feed, hidden_out[layer], preferred_element_type=jnp.float32
        )
        back_hidden = (back_active * gelu_slope(hidden)).astype(jnp.bfloat16)
        inner_weight = jnp.einsum(
            "td,tf->df", normed_second, back_hidden, preferred_element_type=jnp.float32
        )
        partial_second = jnp.einsum(
            "tf,df->td", back_hidden, hidden_in[layer], preferred_element_type=jnp.float32
        )
        back_second = lax.psum(partial_second, "tensor")
        norm_part, gain_second, shift_second = norm_backward(
            normal_second, inverse_second, norm_gain[layer, 1], back_second
        )
        back_middle = upstream + norm_part
        back_branch = back_middle.astype(jnp.bfloat16)
        attention_bias = jnp.sum(back_branch.astype(jnp.float32), axis=0)
        projection_weight = jnp.einsum(
            "te,td->ed", attended, back_branch, preferred_element_type=jnp.float32
        )
        back_attended = jnp.einsum(
            "td,ed->te", back_branch, out_proj[layer], preferred_element_type=jnp.float32
        ).astype(jnp.bfloat16)
        log_total, position = held
        weights = jnp.exp(
            masked_scores(query_blocks, key_blocks, position, same, scale) - log_total
        )
        back_blocks = to_blocks(back_attended, blocks, local_heads)
        back_weights = jnp.einsum(
            "bqhd,bkhd->hbqk", back_blocks, value_blocks, preferred_element_type=jnp.float32
        )
        back_values = jnp.einsum(
            "hbqk,bqhd->bkhd",
            weights.astype(jnp.bfloat16),
            back_blocks,
            preferred_element_type=jnp.float32,
        ).astype(jnp.bfloat16)
        inner = jnp.sum(weights * back_weights, axis=-1, keepdims=True)
        back_scores = (weights * (back_weights - inner)).astype(jnp.bfloat16)
        table_part = table_gradient(back_scores, row_pick, col_pick, key_pick_low)
        back_queries = (
            jnp.einsum(
                "hbqk,bkhd->bqhd", back_scores, key_blocks, preferred_element_type=jnp.float32
            )
            * scale
        ).astype(jnp.bfloat16)
        back_keys = (
            jnp.einsum(
                "hbqk,bqhd->bkhd", back_scores, query_blocks, preferred_element_type=jnp.float32
            )
            * scale
        ).astype(jnp.bfloat16)
        back_projected = jnp.stack(
            [
                back_queries.reshape(count, local_width),
                back_keys.reshape(count, local_width),
                back_values.reshape(count, local_width),
            ]
        )
        token_weight = jnp.einsum(
            "td,jte->jde", normed_first, back_projected, preferred_element_type=jnp.float32
        )
        per_image_back = jnp.einsum(
            "ts,jte->jse",
            one_hot_low,
            jnp.stack([back_projected[0], back_projected[2]]),
            preferred_element_type=jnp.float32,
        )
        time_weight = jnp.einsum(
            "sd,jse->jde",
            embedded.astype(jnp.float32),
            per_image_back,
            precision=lax.Precision.HIGHEST,
        )
        partial_first = jnp.einsum(
            "jte,jde->td", back_projected, token_proj[layer], preferred_element_type=jnp.float32
        )
        back_first = lax.psum(partial_first, "tensor")
        norm_part, gain_first, shift_first = norm_backward(
            normal_first, inverse_first, norm_gain[layer, 0], back_first
        )
        upstream = back_middle + norm_part
        terms = (
            jnp.stack([gain_first, gain_second]),
            jnp.stack([shift_first, shift_second]),
            token_weight,
            time_weight,
            table_part,
            projection_weight,
            inner_weight,
            outer_weight,
            jnp.stack([attention_bias, feed_bias]),
        )
        collected[layer] = terms
    stacked = tuple(
        (jnp.stack([collected[layer][member] for layer in range(depth)]) for member in range(9))
    )
    reduced = (
        lax.psum_scatter(stacked[0], "dp", scatter_dimension=2, tiled=True),
        lax.psum_scatter(stacked[1], "dp", scatter_dimension=2, tiled=True),
        lax.psum_scatter(stacked[2], "dp", scatter_dimension=2, tiled=True),
        lax.psum_scatter(stacked[3], "dp", scatter_dimension=2, tiled=True),
        lax.psum_scatter(stacked[4], "dp", scatter_dimension=2, tiled=True),
        lax.psum_scatter(stacked[5], "dp", scatter_dimension=1, tiled=True),
        lax.psum_scatter(stacked[6], "dp", scatter_dimension=1, tiled=True),
        lax.psum_scatter(stacked[7], "dp", scatter_dimension=1, tiled=True),
        lax.psum_scatter(stacked[8], "dp", scatter_dimension=2, tiled=True),
    )
    return (
        output,
        upstream.astype(jnp.bfloat16),
        reduced[0],
        reduced[1],
        reduced[2],
        reduced[3],
        reduced[4],
        reduced[5],
        reduced[6],
        reduced[7],
        reduced[8],
    )


def solution(mesh):
    return jax.shard_map(
        local,
        mesh=mesh,
        in_specs=(
            P("dp", None),
            P("dp"),
            P("dp", None),
            P(),
            P(),
            P(None, None, None, "tensor"),
            P(None, None, None, "tensor"),
            P(None, "tensor", None),
            P(None, "tensor", None),
            P(None, None, "tensor"),
            P(None, "tensor", None),
            P(),
            P("dp", None),
        ),
        out_specs=(
            P("dp", None),
            P("dp", None),
            P(None, None, "dp"),
            P(None, None, "dp"),
            P(None, None, "dp", "tensor"),
            P(None, None, "dp", "tensor"),
            P(None, "tensor", "dp"),
            P(None, ("tensor", "dp"), None),
            P(None, "dp", "tensor"),
            P(None, ("tensor", "dp"), None),
            P(None, None, "dp"),
        ),
        check_vma=False,
    )
```

profile of v0, /device:TPU:2, one launch (start us, length us, event | category | flops | bytes accessed | tf_op | source)
XLA Modules:
  0.0 2222.7 jit_solution(16061913283387083197)
XLA Ops:
  26.8 14.4 copy.49
  41.8 65.7 %convolution_bitcast_fusion.7 = f32[8,16,16,256]{2,1,0,3:T(8,128)} fusion(f32[8,16,32,256]{2,1,0,3:T(8,128)} %copy.49, s32[16,256]{0,1:T(8,128)S(1)} %copy.48), kind=kOutput, calls=%fused_computation.19 | convolution fusion | flops 201457664 | bytes 6307840 | tf_op jit(solution)/shard_map/bhcaq,braq->bhrcq/dot_general | solution.py:87
  107.6 27.5 %fusion.229 = (f32[8,256]{1,0:T(8,128)S(1)}, f32[8,1,256,256]{2,3,0,1:T(8,128)S(1)}) fusion(f32[8,16,16,256]{2,1,0,3:T(8,128)} %convolution_bitcast_fusion.7, pred[16,256]{1,0:T(8,128)(4,1)S(1)} %iota_compare_fusion.2, pred[16,256]{1,0:T(8,128)(4,1)S(1)} %iota_compare_fusion.3, f32[8,256,256]{1,2,0:T(8,128)S(1)} %fusion.231, ...), kind=kOutput, calls=%fused_computation.335 | convolution fusion | flops 1612773376 | bytes 6373376 | tf_op jit(solution)/shard_map/bhrcq,brck->hbqk/dot_general | solution.py:88
  146.2 14.3 all-reduce.19.cloned.1.call-done
  168.3 5.3 fusion.18
  175.4 14.4 copy.53
  189.9 66.4 %convolution_bitcast_fusion.6 = f32[8,16,16,256]{2,1,0,3:T(8,128)} fusion(f32[8,16,32,256]{2,1,0,3:T(8,128)} %copy.53, s32[16,256]{0,1:T(8,128)S(1)} %copy.48), kind=kOutput, calls=%fused_computation.18 | convolution fusion | flops 201457664 | bytes 6307840 | tf_op jit(solution)/shard_map/bhcaq,braq->bhrcq/dot_general | solution.py:87
  265.1 22.6 %fusion.230 = (f32[8,256]{1,0:T(8,128)S(1)}, f32[8,1,256,256]{2,3,0,1:T(8,128)S(1)}) fusion(f32[8,16,16,256]{2,1,0,3:T(8,128)S(1)} %copy-done, pred[16,256]{1,0:T(8,128)(4,1)S(1)} %copy-done.79, pred[16,256]{1,0:T(8,128)(4,1)S(1)} %copy-done.82, f32[8,256,256]{1,2,0:T(8,128)S(1)} %fusion.232, pred[256,256]{0,1:T(8,128)(4,1)S(1)} %broadcast_compare_fusion), kind=kOutput, calls=%fused_computation.336 | convolution fusion | flops 1612773376 | bytes 6373376 | tf_op jit(solution)/shard_map/bhrcq,brck->hbqk/dot_general | solution.py:88
  292.1 21.1 all-reduce.23.cloned.1.call-done
  319.9 5.3 fusion.46
  329.2 21.1 all-reduce.25.cloned.1.call-done
  363.9 6.1 fusion.10
  371.7 14.4 copy.69
  391.6 4.8 fusion.49
  397.4 5.3 fusion.20
  402.8 15.2 convolution_bitcast_fusion.4
  417.9 26.1 %fusion.142 = f32[8,32,32]{2,1,0:T(8,128)S(1)} fusion(f32[8,16,32,256]{2,1,0,3:T(8,128)} %convolution_bitcast_fusion.4, s32[16,256]{1,0:T(8,128)S(1)} %subtract_add_fusion), kind=kOutput, calls=%fused_computation.189 | convolution fusion | flops 402784256 | bytes 4243456 | tf_op jit(solution)/shard_map/bhcaq,bceq->hae/dot_general | solution.py:96
  456.0 14.5 copy.66
  470.5 15.1 convolution_bitcast_fusion.5
  485.7 25.8 %fusion.139 = f32[8,32,32]{2,1,0:T(8,128)S(1)} fusion(f32[8,16,32,256]{2,1,0,3:T(8,128)} %convolution_bitcast_fusion.5, s32[16,256]{1,0:T(8,128)S(1)} %subtract_add_fusion), kind=kOutput, calls=%fused_computation.188 | convolution fusion | flops 402784256 | bytes 4243456 | tf_op jit(solution)/shard_map/bhcaq,bceq->hae/dot_general | solution.py:96
  521.7 6.4 copy.71
  539.6 4.7 pad_maximum_fusion.3
  544.4 19.3 copy.64
  565.3 9.3 pad_maximum_fusion.2
  574.6 31.8 %copy.63 = f32[2,3,1152,576]{3,0,1,2:T(2,128)} copy(f32[2,3,1152,576]{2,3,1,0:T(8,128)} %pad_maximum_fusion.2) | data formatting | bytes 31850496 | tf_op jit(solution)/shard_map/stack | solution.py:328
  612.1 7.5 pad_maximum_fusion
  625.3 7.6 pad_maximum_fusion.1
  639.4 73.4 %all-reduce.6 = (f32[2,2,1152]{2,1,0:T(2,128)S(1)}, f32[2,2,1152]{2,1,0:T(2,128)S(1)}, f32[2,2,1152]{2,1,0:T(2,128)S(1)}) all-reduce(f32[2,2,1152]{2,1,0:T(2,128)S(1)} %pad_maximum_fusion.12, f32[2,2,1152]{2,1,0:T(2,128)S(1)} %pad_maximum_fusion.13, ...), channel_id=2, replica_groups=mesh['dp'=16,'tensor'=2] {'dp'}, use_global_device_ids=true, to_apply=%region_34.35.clone | all-reduce | flops 13824 | bytes 110592
  718.3 92.1 %all-reduce.31.cloned.1.call-done = f32[2,576,1152]{2,0,1:T(2,128)} async-done(((f32[2,576,1152]{2,0,1:T(2,128)}), f32[2,576,1152]{2,0,1:T(2,128)}) %all-reduce.31.cloned.1.call-update) | async-done | bytes 5308432
  812.1 764.2 %all-reduce.33.cloned.1.call-done = (f32[2,3,1152,576]{3,0,1,2:T(2,128)}, f32[2,2,1152,576]{3,1,0,2:T(2,128)}) async-done(((f32[2,3,1152,576]{3,0,1,2:T(2,128)}, f32[2,2,1152,576]{3,1,0,2:T(2,128)}), (f32[2,3,1152,576]{3,0,1,2:T(2,128)}, f32[2,2,1152,576]{3,1,0,2:T(2,128)})) %all-reduce.33.cloned.1.call-update) | async-done | bytes 26542096
  1581.3 314.3 %reduce-scatter.9.cloned.1.call-done = f32[2,72,2304]{2,1,0:T(8,128)} async-done(((f32[2,1152,2304]{2,1,0:T(8,128)}), f32[2,72,2304]{2,1,0:T(8,128)}) %reduce-scatter.9.cloned.1.call-update) | async-done | bytes 1327120 | tf_op jit(solution)/shard_map/reduce_scatter | solution.py:337
  1895.5 320.0 %reduce-scatter.11.cloned.1.call-done = f32[2,144,1152]{2,1,0:T(8,128)} async-done(((f32[2,2304,1152]{2,1,0:T(8,128)}), f32[2,144,1152]{2,1,0:T(8,128)}) %reduce-scatter.11.cloned.1.call-update) | async-done | bytes 1327120 | tf_op jit(solution)/shard_map/reduce_scatter | solution.py:338
  (443 shorter events, 147.7 us)
Async XLA Ops:
  7.2 153.3 %all-reduce.19.cloned.1.call-start = ((), (), s32[]{:S(2)}) async-start(), calls=%async_computation.3 | async-start | bytes 2359296 | tf_op jit(solution)/shard_map/psum | solution.py:182
  10.0 97.6 %copy-start.78 = (pred[16,256]{1,0:T(8,128)(4,1)}, pred[16,256]{1,0:T(8,128)(4,1)S(1)}, u32[]{:S(2)}) copy-start(pred[16,256]{1,0:T(8,128)(4,1)S(1)} %iota_compare_fusion.2) | copy-start | bytes 12292
  10.0 97.6 %copy-start.81 = (pred[16,256]{1,0:T(8,128)(4,1)}, pred[16,256]{1,0:T(8,128)(4,1)S(1)}, u32[]{:S(2)}) copy-start(pred[16,256]{1,0:T(8,128)(4,1)S(1)} %iota_compare_fusion.3) | copy-start | bytes 12292
  14.4 125.4 %copy-start.74 = (bf16[4,576]{1,0:T(4,128)(2,1)}, bf16[4,576]{1,0:T(4,128)(2,1)S(1)}, u32[]{:S(2)}) copy-start(bf16[4,576]{1,0:T(4,128)(2,1)S(1)} %get-tuple-element.87) | copy-start | bytes 13828
  14.4 125.4 %copy-start.76 = (bf16[4,576]{1,0:T(4,128)(2,1)}, bf16[4,576]{1,0:T(4,128)(2,1)S(1)}, u32[]{:S(2)}) copy-start(bf16[4,576]{1,0:T(4,128)(2,1)S(1)} %get-tuple-element.88) | copy-start | bytes 13828
  18.4 144.0 %copy-start.64 = (f32[1152]{0:T(1024)}, f32[1152]{0:T(1024)S(1)}, u32[]{:S(2)}) copy-start(f32[1152]{0:T(1024)S(1)} %get-tuple-element.101) | copy-start | bytes 13828
  18.4 334.3 %copy-start.66 = (f32[1152]{0:T(1024)}, f32[1152]{0:T(1024)S(1)}, u32[]{:S(2)}) copy-start(f32[1152]{0:T(1024)S(1)} %get-tuple-element.102) | copy-start | bytes 13828
  18.4 370.6 %copy-start.72 = (f32[1152]{0:T(1024)}, f32[1152]{0:T(1024)S(1)}, u32[]{:S(2)}) copy-start(f32[1152]{0:T(1024)S(1)} %get-tuple-element.99) | copy-start | bytes 13828
  23.0 112.5 %copy-start.45 = (bf16[1,256,576]{1,2,0:T(8,128)(2,1)}, bf16[1,256,576]{1,2,0:T(8,128)(2,1)S(1)}, u32[]{:S(2)}) copy-start(bf16[1,256,576]{1,2,0:T(8,128)(2,1)S(1)} %get-tuple-element.83) | copy-start | bytes 884740
  139.0 117.3 %all-reduce.21.cloned.1.call-start = ((), (), s32[]{:S(2)}) async-start(), calls=%async_computation.4 | async-start | bytes 2359296 | tf_op jit(solution)/shard_map/psum | solution.py:190
  162.2 94.2 %copy-start.3 = (f32[256,1152]{1,0:T(8,128)}, f32[256,1152]{1,0:T(8,128)S(1)}, u32[]{:S(2)}) copy-start(f32[256,1152]{1,0:T(8,128)S(1)} %get-tuple-element.79) | copy-start | bytes 3538948
  173.7 139.6 %all-reduce.23.cloned.1.call-start = ((), (), s32[]{:S(2)}) async-start(), calls=%async_computation.5 | async-start | bytes 2359296 | tf_op jit(solution)/shard_map/psum | solution.py:182
  189.9 66.5 %copy-start.98 = (f32[1152]{0:T(1024)S(1)}, f32[1152]{0:T(1024)}, u32[]{:S(2)}) copy-start(f32[1152]{0:T(1024)} %get-tuple-element.50) | copy-start | bytes 13828
  189.9 68.4 %copy-start.108 = (f32[1152]{0:T(1024)S(1)}, f32[1152]{0:T(1024)}, u32[]{:S(2)}) copy-start(f32[1152]{0:T(1024)} %get-tuple-element.60) | copy-start | bytes 13828
  264.6 23.2 %copy-start.34 = (bf16[1,256,576]{1,2,0:T(8,128)(2,1)}, bf16[1,256,576]{1,2,0:T(8,128)(2,1)S(1)}, u32[]{:S(2)}) copy-start(bf16[1,256,576]{1,2,0:T(8,128)(2,1)S(1)} %get-tuple-element.80) | copy-start | bytes 884740
  264.6 23.5 %copy-start.47 = (bf16[1,256,576]{1,2,0:T(8,128)(2,1)}, bf16[1,256,576]{1,2,0:T(8,128)(2,1)S(1)}, u32[]{:S(2)}) copy-start(bf16[1,256,576]{1,2,0:T(8,128)(2,1)S(1)} %get-tuple-element.81) | copy-start | bytes 884740
  289.1 24.2 %copy-start.55 = (bf16[8,72,256]{2,1,0:T(8,128)(2,1)}, bf16[8,72,256]{2,1,0:T(8,128)(2,1)S(1)}, u32[]{:S(2)}) copy-start(bf16[8,72,256]{2,1,0:T(8,128)(2,1)S(1)} %convolution_convert_fusion.2) | copy-start | bytes 884740
  292.1 58.2 %all-reduce.25.cloned.1.call-start = ((), (), s32[]{:S(2)}) async-start(), calls=%async_computation.6 | async-start | bytes 2359296 | tf_op jit(solution)/shard_map/psum | solution.py:243
  315.1 37.7 %copy-start.91 = (f32[256]{0:T(256)}, f32[256]{0:T(256)S(1)}, u32[]{:S(2)}) copy-start(f32[256]{0:T(256)S(1)} %broadcast_multiply_fusion.8) | copy-start | bytes 3076
  315.4 37.4 %copy-start.110 = (f32[256]{0:T(256)}, f32[256]{0:T(256)S(1)}, u32[]{:S(2)}) copy-start(f32[256]{0:T(256)S(1)} %add_rsqrt_fusion) | copy-start | bytes 3076
  329.1 57.1 %all-reduce.27.cloned.1.call-start = ((), (), s32[]{:S(2)}) async-start(), calls=%async_computation.7 | async-start | bytes 2359296 | tf_op jit(solution)/shard_map/psum | solution.py:310
  362.8 81.9 %all-reduce.29.cloned.1.call-start = ((), (), s32[]{:S(2)}) async-start(), calls=%async_computation.8 | async-start | bytes 2359296 | tf_op jit(solution)/shard_map/psum | solution.py:243
  402.7 233.0 %reduce-scatter.13.cloned.1.call-start = ((), (), s32[]{:S(2)}) async-start(), calls=%async_computation.11 | async-start | bytes 557056
  456.0 57.6 %copy-start.60 = (bf16[8,72,256]{2,1,0:T(8,128)(2,1)}, bf16[8,72,256]{2,1,0:T(8,128)(2,1)S(1)}, u32[]{:S(2)}) copy-start(bf16[8,72,256]{2,1,0:T(8,128)(2,1)S(1)} %fusion.118) | copy-start | bytes 884740
  485.7 25.9 %copy-start.69 = (f32[1,8,1024]{2,1,0:T(8,128)S(1)}, f32[1,8,1024]{2,1,0:T(8,128)}, u32[]{:S(2)}) copy-start(f32[1,8,1024]{2,1,0:T(8,128)} %stack_reshape.31) | copy-start | bytes 98308
  513.6 123.7 %all-reduce.35.cloned.1.call-start = ((), (), s32[]{:S(2)}) async-start(), calls=%async_computation.14 | async-start | bytes 4718592 | tf_op jit(solution)/shard_map/psum | solution.py:190
  518.2 292.1 %all-reduce.31.cloned.1.call-start = ((), (), s32[]{:S(2)}) async-start(), calls=%async_computation.12 | async-start | bytes 10616832
  528.1 1048.2 %all-reduce.33.cloned.1.call-start = ((), (), s32[]{:S(2)}) async-start(), calls=%async_computation.13 | async-start | bytes 58982400
  606.4 1289.1 %reduce-scatter.9.cloned.1.call-start = ((), (), s32[]{:S(2)}) async-start(), calls=%async_computation.9 | async-start | bytes 22560768 | tf_op jit(solution)/shard_map/reduce_scatter | solution.py:337
  619.6 1596.0 %reduce-scatter.11.cloned.1.call-start = ((), (), s32[]{:S(2)}) async-start(), calls=%async_computation.10 | async-start | bytes 22560768 | tf_op jit(solution)/shard_map/reduce_scatter | solution.py:338
  633.0 81.8 %copy-start.95 = (f32[1152]{0:T(1024)S(1)}, f32[1152]{0:T(1024)}, u32[]{:S(2)}) copy-start(f32[1152]{0:T(1024)} %get-tuple-element.49) | copy-start | bytes 13828
  637.3 79.7 %copy-start.16 = (f32[256,1152]{1,0:T(8,128)S(1)}, f32[256,1152]{1,0:T(8,128)}, u32[]{:S(2)}) copy-start(f32[256,1152]{1,0:T(8,128)} %copy-done.14) | copy-start | bytes 3538948
  (116 other events, 504.2 us)
Sparse Core Ops, SparseCore 0:
  139.2 21.2 all-reduce.18
  173.8 20.9 all-reduce.20
  292.2 20.9 all-reduce.22
  329.2 20.9 all-reduce.24
  362.9 20.9 all-reduce.26
  402.8 20.9 all-reduce.28
  513.7 72.9 reduce-scatter.12
  589.2 22.7 all-reduce.34
  618.1 192.1 all-reduce.30
  817.8 758.4 all-reduce.32
  1582.9 312.6 reduce-scatter.8
  1903.0 312.5 reduce-scatter.10
where the time goes:
time: 2230 us; the launch traced here: 2220 us
  waiting for transfers between devices  1550 us (70%)
  matrix products  371 us (17%)
  local copies, waits for them, and re-layouts  147 us (7%)
  blocking collectives  73.4 us (3%)
  other arithmetic  62.8 us (3%)
    unnamed x15, waiting for transfers between devices  857 us
    reduce_scatter x1, waiting for transfers between devices, local(): lax.psum_scatter(stacked[7], 'dp', scatter_dimension=1, tiled=True)  320 us
    reduce_scatter x1, waiting for transfers between devices, local(): lax.psum_scatter(stacked[6], 'dp', scatter_dimension=1, tiled=True)  314 us
    dot_general x2, matrix products, position_bias(): jnp.einsum('bhcaq,braq->bhrcq', by_column, row_pick, precision=lax.Precis...  132 us
    unnamed x1, blocking collectives  73.4 us
    another operation x5, local copies, waits for them, and re-layouts, local(): jnp.stack([collected[layer][member] for layer in range(depth)])  58.3 us
    another operation x4, local copies, waits for them, and re-layouts  57.8 us
    dot_general x2, matrix products, table_gradient(): jnp.einsum('bhcaq,bceq->hae', by_column, col_pick, precision=lax.Precisio...  51.9 us
  transfers between devices with their start and end apart: 12, of which 7 were waited for; matrix products, arithmetic and copies ran while one was open for 13% of the time, Pallas kernels for 0%

commit v1 on v0

v1 whole, which is shorter than its diff:
```python
import functools
import math

import jax
import jax.numpy as jnp
from jax import lax
from jax.experimental import pallas as pl
from jax.experimental.pallas import tpu as pltpu
from jax.sharding import Mesh
from jax.sharding import PartitionSpec as P

SIDE = 16
HALF = 8
IMAGES = 4
EPSILON = 1e-06
MASKED = -1e30
ROOT_HALF = 0.7071067811865476
SLOPE_NORM = 0.3989422804014327
LINES = ("line", "col", "row")


def layer_norm(stream, gain, shift):
    center = stream - jnp.mean(stream, axis=-1, keepdims=True)
    inverse = lax.rsqrt(jnp.mean(center * center, axis=-1, keepdims=True) + EPSILON)
    normal = center * inverse
    return (normal * gain + shift, normal, inverse)


def norm_backward(normal, inverse, gain, upstream):
    gain_part = jnp.sum(upstream * normal, axis=0)
    shift_part = jnp.sum(upstream, axis=0)
    scaled = upstream * gain
    inner = (
        scaled
        - jnp.mean(scaled, axis=-1, keepdims=True)
        - normal * jnp.mean(scaled * normal, axis=-1, keepdims=True)
    )
    return (inner * inverse, gain_part, shift_part)


def sinusoid(steps, feature, width):
    half = width // 2
    rates = jnp.exp(-math.log(10000.0) * (feature % half).astype(jnp.float32) / half)
    angles = steps.astype(jnp.float32)[:, None] * rates[None, :]
    wave = jnp.where(feature[None, :] < half, jnp.cos(angles), jnp.sin(angles))
    return wave.astype(jnp.bfloat16)


def gelu_value(hidden):
    return 0.5 * hidden * (1.0 + lax.erf(hidden * ROOT_HALF))


def gelu_slope(hidden):
    return (
        0.5 * (1.0 + lax.erf(hidden * ROOT_HALF))
        + hidden * jnp.exp(-0.5 * hidden * hidden) * SLOPE_NORM
    )


def matmul(left, right, dims=((1,), (0,))):
    return lax.dot_general(left, right, (dims, ((), ())), preferred_element_type=jnp.float32)


def expand_table(table):
    depth, heads = table.shape[:2]
    reverse = table.reshape(depth, heads, 2 * SIDE, 2 * SIDE)[:, :, ::-1, ::-1]
    wide = jnp.stack(
        [reverse[..., SIDE - 1 - c : 2 * SIDE - 1 - c] for c in range(SIDE)], axis=2
    )
    small = wide[:, :, :HALF, HALF : 3 * HALF, :HALF]
    return (
        wide.reshape(depth, heads, SIDE, 2 * SIDE * SIDE),
        small.reshape(depth, heads, HALF, 2 * HALF * HALF),
    )


def fold_table(wide, small):
    heads = wide.shape[0]
    total = wide.reshape(heads, SIDE, 2 * SIDE, SIDE)
    inner = small.reshape(heads, HALF, 2 * HALF, HALF)
    total = total + jnp.pad(inner, ((0, 0), (0, HALF), (HALF, HALF), (0, HALF)))
    reverse = functools.reduce(
        jnp.add,
        [
            jnp.pad(total[:, c], ((0, 0), (0, 0), (SIDE - 1 - c, 1 + c)))
            for c in range(SIDE)
        ],
    )
    return reverse[:, ::-1, ::-1].reshape(heads, 4 * SIDE * SIDE)


def fill_bias(small_row, wide_ref, small_ref, head, bias):
    span = SIDE * SIDE

    @pl.when(small_row == 0)
    def _():
        wide = wide_ref[head]
        for r in range(SIDE):
            at = SIDE * (SIDE - 1 - r)
            turned = wide if at == 0 else pltpu.roll(wide, 2 * span - at, 1)
            bias[r * SIDE : (r + 1) * SIDE, :] = turned[:, :span]

    @pl.when(small_row != 0)
    def _():
        small = small_ref[head]
        image = lax.broadcasted_iota(jnp.int32, (HALF, span), 1) // (HALF * HALF)
        lane = lax.broadcasted_iota(jnp.int32, small.shape, 1)
        for r in range(HALF):
            at = HALF * (HALF - 1 - r)
            turned = small if at == 0 else pltpu.roll(small, 2 * HALF * HALF - at, 1)
            turned = jnp.where(lane < HALF * HALF, turned, 0.0)
            pair = turned + pltpu.roll(turned, HALF * HALF, 1)
            line = jnp.concatenate([pair, pair], axis=1)
            for i in range(IMAGES):
                start = i * HALF * HALF + r * HALF
                bias[start : start + HALF, :] = jnp.where(image == i, line, MASKED)


def window_of(head, head_dim, width):
    first = head * head_dim // 128 * 128
    last = min(-(-(head + 1) * head_dim // 128) * 128, width)
    return first, last


def softmax_of(queries, keys, bias, scale):
    scores = matmul(queries, keys, ((1,), (1,))) * scale + bias[...]
    expo = jnp.exp(scores - jnp.max(scores, axis=-1, keepdims=True))
    return expo * (1.0 / jnp.sum(expo, axis=-1, keepdims=True))


def forward_kernel(heads, scale, flags, q_ref, k_ref, v_ref, wide_ref, small_ref, out_ref, bias, total):
    width = q_ref.shape[2]
    head_dim = width // heads
    total[...] = jnp.zeros_like(total)
    for head in range(heads):
        first, last = window_of(head, head_dim, width)
        lane = lax.broadcasted_iota(jnp.int32, (q_ref.shape[1], last - first), 1) + first
        mine = (lane >= head * head_dim) & (lane < (head + 1) * head_dim)
        fill_bias(flags[pl.program_id(0)], wide_ref, small_ref, head, bias)
        zero = jnp.zeros((), jnp.bfloat16)
        queries = jnp.where(mine, q_ref[0, :, first:last], zero)
        values = jnp.where(mine, v_ref[0, :, first:last], zero)
        weights = softmax_of(queries, k_ref[0, :, first:last], bias, scale)
        total[:, first:last] += matmul(weights.astype(jnp.bfloat16), values)
    out_ref[0] = total[...].astype(jnp.bfloat16)


def attend(flags, queries, keys, values, wide, small):
    rows, count, width = queries.shape
    heads = wide.shape[0]
    row = pl.BlockSpec((1, count, width), lambda r, f: (r, 0, 0))
    return pl.pallas_call(
        functools.partial(forward_kernel, heads, 1.0 / math.sqrt(width // heads)),
        grid_spec=pltpu.PrefetchScalarGridSpec(
            num_scalar_prefetch=1,
            grid=(rows,),
            in_specs=[
                row,
                row,
                row,
                pl.BlockSpec(wide.shape, lambda r, f: (0, 0, 0)),
                pl.BlockSpec(small.shape, lambda r, f: (0, 0, 0)),
            ],
            out_specs=row,
            scratch_shapes=[
                pltpu.VMEM((count, count), jnp.float32),
                pltpu.VMEM((count, width), jnp.float32),
            ],
        ),
        out_shape=jax.ShapeDtypeStruct(queries.shape, jnp.bfloat16),
        compiler_params=pltpu.CompilerParams(vmem_limit_bytes=32 << 20),
        cost_estimate=pl.CostEstimate(
            flops=rows * heads * count * count * 512,
            bytes_accessed=8 * rows * count * width,
            transcendentals=rows * heads * count * count,
        ),
        name="attend",
    )(flags, queries, keys, values, wide, small)


def backward_kernel(
    heads, scale, with_table, flags, q_ref, k_ref, v_ref, up_ref, wide_ref, small_ref, *rest
):
    outs, (bias, steps) = rest[:-2], rest[-2:]
    span = SIDE * SIDE
    width = q_ref.shape[2]
    head_dim = width // heads
    kind = flags[pl.program_id(0)]
    steps[...] = jnp.zeros_like(steps)
    if with_table:
        wide_out, small_out = outs[4:]

        @pl.when(pl.program_id(0) == 0)
        def _():
            wide_out[...] = jnp.zeros_like(wide_out)
            small_out[...] = jnp.zeros_like(small_out)

    for head in range(heads):
        first, last = window_of(head, head_dim, width)
        lane = lax.broadcasted_iota(jnp.int32, (q_ref.shape[1], last - first), 1) + first
        mine = (lane >= head * head_dim) & (lane < (head + 1) * head_dim)
        fill_bias(kind, wide_ref, small_ref, head, bias)
        zero = jnp.zeros((), jnp.bfloat16)
        queries, keys, values, upstream = (
            jnp.where(mine, ref[0, :, first:last], zero)
            for ref in (q_ref, k_ref, v_ref, up_ref)
        )
        weights = softmax_of(queries, keys, bias, scale)
        low = weights.astype(jnp.bfloat16)
        back_weights = matmul(upstream, values, ((1,), (1,)))
        inner = jnp.sum(weights * back_weights, axis=-1, keepdims=True)
        back_scores = (weights * (back_weights - inner)).astype(jnp.bfloat16)
        steps[0, :, first:last] += matmul(back_scores, keys) * scale
        steps[1, :, first:last] += matmul(back_scores, queries, ((0,), (0,))) * scale
        steps[2, :, first:last] += matmul(low, upstream, ((0,), (0,)))
        if with_table:
            steps[3, :, first:last] += matmul(low, values)
            bias[...] = back_scores.astype(jnp.float32)

            @pl.when(kind == 0)
            def _(head=head):
                total = wide_out[head]
                for r in range(SIDE):
                    part = bias[r * SIDE : (r + 1) * SIDE, :]
                    part = jnp.concatenate([part, jnp.zeros_like(part)], axis=1)
                    at = SIDE * (SIDE - 1 - r)
                    total = total + (part if at == 0 else pltpu.roll(part, at, 1))
                wide_out[head] = total

            @pl.when(kind != 0)
            def _(head=head):
                total = small_out[head]
                block = HALF * HALF
                lane = lax.broadcasted_iota(jnp.int32, total.shape, 1)
                for r in range(HALF):
                    part = functools.reduce(
                        jnp.add,
                        [
                            bias[i * block + r * HALF : i * block + (r + 1) * HALF, :]
                            for i in range(IMAGES)
                        ],
                    )
                    part = part[:, : span // 2] + part[:, span // 2 :]
                    part = jnp.where(lane < block, part + pltpu.roll(part, block, 1), 0.0)
                    at = HALF * (HALF - 1 - r)
                    total = total + (part if at == 0 else pltpu.roll(part, at, 1))
                small_out[head] = total

    for member in range(4 if with_table else 3):
        outs[member][0] = steps[member].astype(jnp.bfloat16)


def attend_back(flags, queries, keys, values, upstream, wide, small, with_table):
    rows, count, width = queries.shape
    heads = wide.shape[0]
    row = pl.BlockSpec((1, count, width), lambda r, f: (r, 0, 0))
    wide_spec = pl.BlockSpec(wide.shape, lambda r, f: (0, 0, 0))
    small_spec = pl.BlockSpec(small.shape, lambda r, f: (0, 0, 0))
    low = jax.ShapeDtypeStruct(queries.shape, jnp.bfloat16)
    members = 4 if with_table else 3
    tables = (
        [
            jax.ShapeDtypeStruct(wide.shape, jnp.float32),
            jax.ShapeDtypeStruct(small.shape, jnp.float32),
        ]
        if with_table
        else []
    )
    return pl.pallas_call(
        functools.partial(
            backward_kernel, heads, 1.0 / math.sqrt(width // heads), with_table
        ),
        grid_spec=pltpu.PrefetchScalarGridSpec(
            num_scalar_prefetch=1,
            grid=(rows,),
            in_specs=[row, row, row, row, wide_spec, small_spec],
            out_specs=[row] * members + ([wide_spec, small_spec] if with_table else []),
            scratch_shapes=[
                pltpu.VMEM((count, count), jnp.float32),
                pltpu.VMEM((4, count, width), jnp.float32),
            ],
        ),
        out_shape=[low] * members + tables,
        compiler_params=pltpu.CompilerParams(vmem_limit_bytes=32 << 20),
        cost_estimate=pl.CostEstimate(
            flops=rows * heads * count * count * 1536,
            bytes_accessed=16 * rows * count * width,
            transcendentals=rows * heads * count * count,
        ),
        name="attend_back",
    )(flags, queries, keys, values, upstream, wide, small)


def swap(value, axis):
    return lax.ppermute(value, axis, [(0, 1), (1, 0)])


def shift(value, line, by=1):
    return lax.ppermute(value, "line", [(i, (i + by) % line) for i in range(line)])


def add_tensor(partial):
    return partial + swap(partial, "tensor")


def narrow_kernel(own_ref, *refs):
    blocks, out_ref = refs[:-1], refs[-1]
    start = 0
    for ref in (own_ref, *blocks):
        out_ref[start : start + ref.shape[0], :] = ref[...].astype(jnp.bfloat16)
        start += ref.shape[0]


def narrow_line(blocks):
    width = blocks[0].shape[1]
    part = 384
    count = sum(block.shape[0] for block in blocks)
    return pl.pallas_call(
        narrow_kernel,
        grid=(width // part,),
        in_specs=[pl.BlockSpec((block.shape[0], part), lambda c: (0, c)) for block in blocks],
        out_specs=pl.BlockSpec((count, part), lambda c: (0, c)),
        out_shape=jax.ShapeDtypeStruct((count, width), jnp.bfloat16),
        compiler_params=pltpu.CompilerParams(vmem_limit_bytes=48 << 20),
        name="narrow_line",
    )(*blocks)


def narrow_plane_kernel(core, own_ref, remote_ref, other_ref, out_ref):
    half = remote_ref.shape[1]
    out_ref[0] = own_ref[...].astype(jnp.bfloat16)

    @pl.when(core[0] == 0)
    def _():
        out_ref[1:, :half] = remote_ref[...].astype(jnp.bfloat16)
        out_ref[1:, half:] = other_ref[...].astype(jnp.bfloat16)

    @pl.when(core[0] != 0)
    def _():
        out_ref[1:, :half] = other_ref[...].astype(jnp.bfloat16)
        out_ref[1:, half:] = remote_ref[...].astype(jnp.bfloat16)


def narrow_plane(own, remote, other):
    count, width = own.shape
    part = 384
    block = pl.BlockSpec((*remote.shape[:2], part), lambda c, core: (0, 0, c))
    return pl.pallas_call(
        narrow_plane_kernel,
        grid_spec=pltpu.PrefetchScalarGridSpec(
            num_scalar_prefetch=1,
            grid=(width // part,),
            in_specs=[pl.BlockSpec((count, part), lambda c, core: (0, c)), block, block],
            out_specs=pl.BlockSpec((4, count, part), lambda c, core: (0, 0, c)),
        ),
        out_shape=jax.ShapeDtypeStruct((4, count, width), jnp.bfloat16),
        compiler_params=pltpu.CompilerParams(vmem_limit_bytes=48 << 20),
        name="narrow_plane",
    )(lax.axis_index("tensor")[None].astype(jnp.int32), own, remote, other)


def half_rows(value):
    half = value.shape[0] // 2
    return lax.dynamic_slice_in_dim(value, lax.axis_index("tensor") * half, half, 0)


def gather_line(value, line):
    current = half_rows(value)
    blocks = []
    for _ in range(line - 1):
        current = shift(current, line)
        blocks += [current, swap(current, "tensor")]
    return narrow_line([value, *blocks])


def gather_plane(value):
    mine = half_rows(value)
    half = mine.shape[0] // 2
    across = swap(mine, "row")
    along = swap(mine, "col")
    corner = jnp.concatenate([swap(along[:half], "row"), swap(across[half:], "col")])
    remote = jnp.stack([across, along, corner])
    other = swap(remote, "tensor")
    return narrow_plane(value, remote, other)


def pick(value, index, axis=0):
    return lax.dynamic_index_in_dim(value, index, axis, keepdims=False)


def scatter_plane(value, axes):
    order, positions = axes
    for name, position in zip(order, positions, strict=True):
        place = lax.axis_index(name)
        value = pick(value, place, position) + swap(pick(value, 1 - place, position), name)
    return value


def scatter_line(value, line):
    place = lax.axis_index("line")
    total = pick(value, (place - 1) % line)
    for step in range(1, line):
        total = pick(value, (place - 1 - step) % line) + shift(total, line)
    return total


def exchange_line(value, line):
    place = lax.axis_index("line")
    slots = [pick(value, place)] + [
        shift(pick(value, (place + by) % line), line, by) for by in range(1, line)
    ]
    turned = jnp.stack([slots[-i % line] for i in range(line)] * 2)
    return lax.dynamic_slice_in_dim(turned, (line - place) % line, line, 0)


def exchange_plane(value):
    col, row = lax.axis_index("col"), lax.axis_index("row")
    place = 2 * col + row
    across = swap(pick(value, place ^ 1), "row")
    along = swap(pick(value, place ^ 2), "col")
    corner = lax.ppermute(
        pick(value, place ^ 3), ("col", "row"), [(0, 3), (3, 0), (1, 2), (2, 1)]
    )
    slots = [pick(value, place), across, along, corner]
    slots = [jnp.where(row == 0, slots[i], slots[i ^ 1]) for i in range(4)]
    return jnp.stack([jnp.where(col == 0, slots[i], slots[i ^ 2]) for i in range(4)])


def feed_gradients(normed, upstream, weight_in, weight_out, line):
    width, units = weight_in.shape
    own = units // line
    start = lax.axis_index("line") * own
    part_in = lax.dynamic_slice_in_dim(weight_in, start, own, 1)
    part_out = lax.dynamic_slice_in_dim(weight_out, start, own, 0)
    hidden = matmul(normed, part_in)
    activated = gelu_value(hidden).astype(jnp.bfloat16)
    back = matmul(upstream, part_out, ((1,), (1,)))
    back_hidden = (back * gelu_slope(hidden)).astype(jnp.bfloat16)
    outer = matmul(activated, upstream, ((0,), (0,)))
    inner = matmul(normed, back_hidden, ((0,), (0,)))
    outer = scatter_plane(outer.reshape(2, 2, own // 4, width), (("col", "row"), (0, 0)))
    inner = inner.reshape(line, 2, 2, width // (4 * line), own)
    inner = scatter_plane(inner, (("row", "col"), (2, 1)))
    inner = exchange_line(inner, line)
    return jnp.moveaxis(inner, 0, 1).reshape(width // (4 * line), units), outer


def place_images(per_image, small_row, count):
    first = jnp.where(small_row[..., None, None] != 0, per_image, per_image[..., :1, :])
    return jnp.repeat(first, count // IMAGES, axis=-2)


def attention_gradients(
    normed, upstream, embedded, kinds, token_weight, time_weight, out_weight, wide, small, line
):
    slots, count, width = normed.shape
    local = token_weight.shape[2]
    heads = wide.shape[0]
    own, own_heads = local // slots, heads // slots
    place = 2 * lax.axis_index("col") + lax.axis_index("row")
    start = place * own
    part = lax.dynamic_slice_in_dim(token_weight, start, own, 2)
    part_time = lax.dynamic_slice_in_dim(time_weight, start, own, 2)
    part_out = lax.dynamic_slice_in_dim(out_weight, start, own, 0)
    part_wide = lax.dynamic_slice_in_dim(wide, place * own_heads, own_heads, 0)
    part_small = lax.dynamic_slice_in_dim(small, place * own_heads, own_heads, 0)
    flat = normed.reshape(slots * count, width)
    flat_up = upstream.reshape(slots * count, width)
    per_image = [
        matmul(embedded, part_time[member]).reshape(slots, IMAGES, own) for member in range(2)
    ]
    per_token = [place_images(member, kinds, count) for member in per_image]
    queries, keys, values = (
        matmul(flat, part[member]).reshape(slots, count, own) for member in range(3)
    )
    back_attended = matmul(flat_up, part_out, ((1,), (1,))).astype(jnp.bfloat16)
    back_queries, back_keys, back_values, attended, back_wide, back_small = attend_back(
        kinds,
        (queries + per_token[0]).astype(jnp.bfloat16),
        keys.astype(jnp.bfloat16),
        (values + per_token[1]).astype(jnp.bfloat16),
        back_attended.reshape(slots, count, own),
        part_wide,
        part_small,
        True,
    )
    projection = matmul(attended.reshape(slots * count, own), flat_up, ((0,), (0,)))
    projection = scatter_line(projection.reshape(line, own // line, width), line)
    projection = lax.ppermute(
        projection,
        LINES,
        [(slots * z + j, line * j + z) for z in range(line) for j in range(slots)],
    )
    token = jnp.stack(
        [
            matmul(flat, member.reshape(slots * count, own), ((0,), (0,)))
            for member in (back_queries, back_keys, back_values)
        ]
    )
    token = token.reshape(3, line, width // line, own)
    token = scatter_line(jnp.moveaxis(token, 1, 0), line)
    token = token.reshape(3, slots, width // (slots * line), own)
    token = exchange_plane(jnp.moveaxis(token, 1, 0))
    token = jnp.moveaxis(token, 0, 2).reshape(3, width // (slots * line), local)
    table = fold_table(back_wide, back_small)
    whole = jnp.zeros((heads, table.shape[1]), jnp.float32)
    whole = lax.dynamic_update_slice_in_dim(whole, table, place * own_heads, 0)
    return token, projection, whole


def local(
    tokens,
    segment_ids,
    timesteps,
    norm_gain,
    norm_bias,
    token_proj,
    time_proj,
    bias_table,
    out_proj,
    hidden_in,
    hidden_out,
    branch_bias,
    cotangent,
    *,
    line,
):
    count, width = tokens.shape
    local_width = token_proj.shape[3]
    depth = token_proj.shape[0]
    heads = bias_table.shape[1]
    n_dp = 4 * line
    line_at = lax.axis_index("line")
    place = 2 * lax.axis_index("col") + lax.axis_index("row")
    kind = segment_ids[-1:]
    info = lax.all_gather(jnp.concatenate([timesteps[0], kind]), LINES)
    near = lax.dynamic_slice_in_dim(info, 4 * line_at, 4, 0)
    slot_of = place ^ jnp.arange(4, dtype=jnp.int32)
    chosen = slot_of[:, None] == jnp.arange(4, dtype=jnp.int32)[None, :]
    near = jnp.sum(jnp.where(chosen[:, :, None], near[None], 0), axis=1)
    kinds = near[:, IMAGES]
    features = jnp.arange(width, dtype=jnp.int32)
    embedded_own = sinusoid(timesteps[0], features, width)
    embedded_near = sinusoid(near[:, :IMAGES].reshape(-1), features, width)
    own_features = width // n_dp
    embedded_all = sinusoid(
        info[:, :IMAGES].reshape(-1),
        (4 * line_at + place) * own_features + jnp.arange(own_features, dtype=jnp.int32),
        width,
    )
    wide, small = expand_table(bias_table)

    stream = tokens.astype(jnp.float32)
    saved = []
    cotangent_full = cotangent.astype(jnp.float32)
    gathered_up = gather_line(cotangent_full, line)
    for layer in range(depth):
        normed, normal_first, inverse_first = layer_norm(
            stream, norm_gain[layer, 0], norm_bias[layer, 0]
        )
        near_first = gather_plane(normed)
        normed_first = normed.astype(jnp.bfloat16)
        per_token = [
            place_images(matmul(embedded_own, time_proj[layer, member]), kind[0], count)
            for member in range(2)
        ]
        queries = (matmul(normed_first, token_proj[layer, 0]) + per_token[0]).astype(jnp.bfloat16)
        keys = matmul(normed_first, token_proj[layer, 1]).astype(jnp.bfloat16)
        values = (matmul(normed_first, token_proj[layer, 2]) + per_token[1]).astype(jnp.bfloat16)
        attended = attend(kind, queries[None], keys[None], values[None], wide[layer], small[layer])
        partial = matmul(attended[0], out_proj[layer])
        middle = stream + add_tensor(partial) + branch_bias[layer, 0]
        normed, normal_second, inverse_second = layer_norm(
            middle, norm_gain[layer, 1], norm_bias[layer, 1]
        )
        line_second = gather_line(normed, line)
        normed_second = normed.astype(jnp.bfloat16)
        hidden = matmul(normed_second, hidden_in[layer])
        activated = gelu_value(hidden).astype(jnp.bfloat16)
        partial = matmul(activated, hidden_out[layer])
        stream = middle + add_tensor(partial) + branch_bias[layer, 1]
        saved.append(
            (
                near_first,
                normal_first,
                inverse_first,
                queries,
                keys,
                values,
                normal_second,
                inverse_second,
                line_second,
                hidden,
            )
        )
    output = stream.astype(jnp.bfloat16)
    upstream = cotangent_full
    collected = [None] * depth
    for layer in reversed(range(depth)):
        (
            near_first,
            normal_first,
            inverse_first,
            queries,
            keys,
            values,
            normal_second,
            inverse_second,
            line_second,
            hidden,
        ) = saved[layer]
        back_feed = upstream.astype(jnp.bfloat16)
        feed_bias = jnp.sum(back_feed.astype(jnp.float32), axis=0)
        if layer < depth - 1:
            gathered_up = gather_line(upstream, line)
        inner_weight, outer_weight = feed_gradients(
            line_second, gathered_up, hidden_in[layer], hidden_out[layer], line
        )
        back_active = matmul(back_feed, hidden_out[layer], ((1,), (1,)))
        back_hidden = (back_active * gelu_slope(hidden)).astype(jnp.bfloat16)
        back_second = add_tensor(matmul(back_hidden, hidden_in[layer], ((1,), (1,))))
        norm_part, gain_second, shift_second = norm_backward(
            normal_second, inverse_second, norm_gain[layer, 1], back_second
        )
        back_middle = upstream + norm_part
        near_branch = gather_plane(back_middle)
        back_branch = back_middle.astype(jnp.bfloat16)
        attention_bias = jnp.sum(back_branch.astype(jnp.float32), axis=0)
        back_attended = matmul(back_branch, out_proj[layer], ((1,), (1,))).astype(jnp.bfloat16)
        back_projected = attend_back(
            kind,
            queries[None],
            keys[None],
            values[None],
            back_attended[None],
            wide[layer],
            small[layer],
            False,
        )
        back_projected = [member[0] for member in back_projected]
        back_first = functools.reduce(
            jnp.add,
            [
                matmul(back_projected[member], token_proj[layer, member], ((1,), (1,)))
                for member in range(3)
            ],
        )
        back_first = add_tensor(back_first)
        norm_part, gain_first, shift_first = norm_backward(
            normal_first, inverse_first, norm_gain[layer, 0], back_first
        )
        upstream = back_middle + norm_part
        token_weight, projection_weight, table = attention_gradients(
            near_first,
            near_branch,
            embedded_near,
            kinds,
            token_proj[layer],
            time_proj[layer],
            out_proj[layer],
            wide[layer],
            small[layer],
            line,
        )
        per_image = jnp.stack([back_projected[0], back_projected[2]]).astype(jnp.float32)
        per_image = jnp.sum(per_image.reshape(2, IMAGES, count // IMAGES, local_width), axis=2)
        first_image = (jnp.arange(IMAGES, dtype=jnp.int32) == 0)[None, :, None]
        per_image = jnp.where(
            kind[0] != 0,
            per_image,
            jnp.where(first_image, jnp.sum(per_image, axis=1, keepdims=True), 0.0),
        )
        per_image = lax.all_gather(per_image, LINES)
        time_weight = jnp.einsum(
            "rsd,rjse->jde",
            embedded_all.astype(jnp.float32).reshape(n_dp, IMAGES, own_features),
            per_image,
            precision=lax.Precision.HIGHEST,
        )
        pieces = [
            jnp.stack([gain_first, gain_second, shift_first, shift_second, attention_bias, feed_bias]),
            table,
        ]
        pieces = [
            jnp.moveaxis(piece.reshape(piece.shape[0], n_dp, -1), 1, 0).reshape(n_dp, -1)
            for piece in pieces
        ]
        pieces = lax.psum_scatter(
            jnp.concatenate(pieces, axis=1), LINES, scatter_dimension=0, tiled=True
        )[0]
        vectors = pieces[: 6 * own_features].reshape(3, 2, own_features)
        table = pieces[6 * own_features :].reshape(heads, -1)
        collected[layer] = (
            vectors[0],
            vectors[1],
            token_weight,
            time_weight,
            table,
            projection_weight,
            inner_weight,
            outer_weight,
            vectors[2],
        )
    stacked = [jnp.stack([terms[member] for terms in collected]) for member in range(9)]
    return (output, upstream.astype(jnp.bfloat16), *stacked)


def solution(mesh):
    line = mesh.shape["dp"] // 4
    fine = Mesh(
        mesh.devices.reshape(line, 2, 2, mesh.shape["tensor"]), (*LINES, "tensor")
    )
    return jax.shard_map(
        functools.partial(local, line=line),
        mesh=fine,
        in_specs=(
            P(LINES, None),
            P(LINES),
            P(LINES, None),
            P(),
            P(),
            P(None, None, None, "tensor"),
            P(None, None, None, "tensor"),
            P(None, "tensor", None),
            P(None, "tensor", None),
            P(None, None, "tensor"),
            P(None, "tensor", None),
            P(),
            P(LINES, None),
        ),
        out_specs=(
            P(LINES, None),
            P(LINES, None),
            P(None, None, LINES),
            P(None, None, LINES),
            P(None, None, LINES, "tensor"),
            P(None, None, LINES, "tensor"),
            P(None, "tensor", LINES),
            P(None, ("tensor", *LINES), None),
            P(None, LINES, "tensor"),
            P(None, ("tensor", *LINES), None),
            P(None, None, LINES),
        ),
        check_vma=False,
    )
```

time: 2230 us -> 1040 us (0.47)
  waiting for transfers between devices: 1550 us -> 281 us
  matrix products: 371 us -> 166 us
  local copies, waits for them, and re-layouts: 147 us -> 230 us
  Pallas kernels: 0 us -> 80.9 us
  starting transfers between devices: 1.29 us -> 74.3 us
  blocking collectives: 73.4 us -> 98.4 us
    unnamed x15 -> x2, waiting for transfers between devices: 857 us -> 104 us
    reduce_scatter x2 -> x0, waiting for transfers between devices: 634 us -> none  [the longest x1 320 us: local(): lax.psum_scatter(stacked[7], 'dp', scatter_dimension=1, tiled=True)]
    dot_general x56 -> x54, matrix products: 371 us -> 166 us  [the longest x52 163 us: matmul(): lax.dot_general(left, right, (dims, ((), ())), preferred_element_type=jnp...]
    ppermute x0 -> x86, waiting for transfers between devices: none -> 177 us  [the longest x30 128 us: shift(): lax.ppermute(value, 'line', [(i, (i + by) % line) for i in range(line)])]
    all_gather x0 -> x2, blocking collectives: none -> 85 us  [local(): per_image = lax.all_gather(per_image, LINES)]
    pallas_call x0 -> x14, Pallas kernels: none -> 80.9 us  [the longest x4 35.8 us: attend_back(): pl.pallas_call(functools.partial(backward_kernel, heads, 1.0 / math.sqrt(...]
    slice x5 -> x53, local copies, waits for them, and re-layouts: 1.97 us -> 80.6 us  [the longest x17 21.4 us: expand_table(): reverse[..., SIDE - 1 - c:2 * SIDE - 1 - c]]
    ppermute x0 -> x86, starting transfers between devices: none -> 74.3 us  [the longest x52 41.7 us: swap(): return lax.ppermute(value, axis, [(0, 1), (1, 0)])]
  transfers between devices with their start and end apart: 12 -> 87, of which waited for: 7 -> 33; matrix products, arithmetic and copies ran while one was open for 13% -> 38% of each run, Pallas kernels for 0% -> 7%
where the time goes in v1:
time: 1040 us; the launch traced here: 1020 us
  waiting for transfers between devices  281 us (27%)
  local copies, waits for them, and re-layouts  230 us (22%)
  matrix products  166 us (16%)
  blocking collectives  98.4 us (9%)
  Pallas kernels  80.9 us (8%)
  other arithmetic  75.1 us (7%)
  starting transfers between devices  74.3 us (7%)
  between operations  18.7 us (2%)
    dot_general x52, matrix products, matmul(): lax.dot_general(left, right, (dims, ((), ())), preferred_element_type=jnp...  163 us
    ppermute x30, waiting for transfers between devices, shift(): lax.ppermute(value, 'line', [(i, (i + by) % line) for i in range(line)])  128 us
    unnamed x2, waiting for transfers between devices  104 us
    all_gather x2, blocking collectives, local(): per_image = lax.all_gather(per_image, LINES)  85 us
    unnamed x400, local copies, waits for them, and re-layouts  42.2 us
    ppermute x52, starting transfers between devices, swap(): return lax.ppermute(value, axis, [(0, 1), (1, 0)])  41.7 us
    ppermute x52, waiting for transfers between devices, swap(): return lax.ppermute(value, axis, [(0, 1), (1, 0)])  37 us
    pallas_call x4, Pallas kernels, attend_back(): pl.pallas_call(functools.partial(backward_kernel, heads, 1.0 / math.sqrt(...  35.8 us
  transfers between devices with their start and end apart: 87, of which 33 were waited for; matrix products, arithmetic and copies ran while one was open for 38% of the time, Pallas kernels for 7%

profile of v1, /device:TPU:2, one launch (start us, length us, event | category | flops | bytes accessed | tf_op | source)
XLA Modules:
  0.0 1024.0 jit_solution(8610337241992027514)
XLA Ops:
  67.8 6.5 attend.2
  91.1 13.4 %all-reduce.34 = s32[80]{0:T(128)S(1)} all-reduce(s32[80]{0:T(128)S(1)} %add_dynamic-update-slice_fusion), channel_id=2, replica_groups=mesh['line'=4,'col'=2,'row'=2,'tensor'=2] {'line','col','row'}, use_global_device_ids=true, to_apply=%add.34 | all-reduce | flops 80 | bytes 640
  118.5 8.7 fusion.326
  127.2 8.8 fusion.325
  137.1 6.6 fusion.327
  159.6 14.2 %collective-permute-done.73.refs_2_ = f32[128,1152]{1,0:T(8,128)} collective-permute-done((f32[128,1152]{1,0:T(8,128)}, f32[128,1152]{1,0:T(8,128)}, u32[]{:S(2)}, u32[]{:S(2)}) %collective-permute-start.73) | collective-permute-done | bytes 589856 | tf_op jit(solution)/shard_map/ppermute | solution.py:299
  173.7 12.5 %collective-permute-done.48.refs_0_ = f32[128,1152]{1,0:T(8,128)S(1)} collective-permute-done((f32[128,1152]{1,0:T(8,128)S(1)}, f32[128,1152]{1,0:T(8,128)S(1)}, u32[]{:S(2)}, u32[]{:S(2)}) %collective-permute-start.48) | collective-permute-done | bytes 589856 | tf_op jit(solution)/shard_map/ppermute | solution.py:299
  192.6 6.3 attend.3
  200.7 10.6 %collective-permute-done.50.refs_2_ = f32[128,1152]{1,0:T(8,128)} collective-permute-done((f32[128,1152]{1,0:T(8,128)S(1)}, f32[128,1152]{1,0:T(8,128)}, u32[]{:S(2)}, u32[]{:S(2)}) %collective-permute-start.50) | collective-permute-done | bytes 589856 | tf_op jit(solution)/shard_map/ppermute | solution.py:299
  244.0 9.3 fusion.4
  289.9 8.2 attend_back.4
  346.3 9.1 fusion.12
  355.4 9.0 fusion.200
  392.5 8.0 attend_back.5
  404.5 44.7 %all_gather.17 = f32[16,2,4,576]{3,2,1,0:T(4,128)S(1)} all-gather(f32[1,2,4,576]{3,2,1,0:T(4,128)S(1)} %get-tuple-element.306), channel_id=1, replica_groups=mesh['line'=4,'col'=2,'row'=2,'tensor'=2] {'line','col','row'}, dimensions={0}, use_global_device_ids=true | all-gather | bytes 313344 | tf_op jit(solution)/shard_map/all_gather | solution.py:673
  449.2 40.3 %all_gather.16 = f32[16,2,4,576]{3,2,1,0:T(4,128)S(1)} all-gather(f32[1,2,4,576]{3,2,1,0:T(4,128)S(1)} %get-tuple-element.305), channel_id=1, replica_groups=mesh['line'=4,'col'=2,'row'=2,'tensor'=2] {'line','col','row'}, dimensions={0}, use_global_device_ids=true | all-gather | bytes 313344 | tf_op jit(solution)/shard_map/all_gather | solution.py:673
  522.8 9.8 attend_back.7
  569.2 8.2 constant_dynamic-slice_fusion.11
  589.6 7.8 collective-permute-done.34
  627.1 7.9 collective-permute-done.80
  636.5 7.4 collective-permute-done.81
  666.1 9.1 fusion.203
  713.3 7.0 collective-permute-done.39
  720.3 9.9 collective-permute-start.11
  735.1 10.6 %collective-permute-done.11 = f32[64,1152]{1,0:T(8,128)} collective-permute-done((f32[64,1152]{1,0:T(8,128)}, f32[64,1152]{1,0:T(8,128)}, u32[]{:S(2)}, u32[]{:S(2)}) %collective-permute-start.11) | collective-permute-done | bytes 294944 | tf_op jit(solution)/shard_map/ppermute | solution.py:295
  765.9 7.5 collective-permute-done.61
  781.9 9.5 collective-permute-done.63
  808.4 9.8 attend_back.6
  831.2 7.1 constant_dynamic-slice_fusion.19
  845.5 104.1 %all-reduce.40.cloned.1.call-done = (f32[16,944]{1,0:T(8,128)}, f32[16,944]{1,0:T(8,128)}) async-done(((f32[16,944]{1,0:T(8,128)}, f32[16,944]{1,0:T(8,128)}), (f32[16,944]{1,0:T(8,128)}, f32[16,944]{1,0:T(8,128)})) %all-reduce.40.cloned.1.call-update) | async-done | bytes 120848
  967.7 12.9 %collective-permute-done.29 = f32[3,288,144]{1,2,0:T(8,128)S(1)} collective-permute-done((f32[3,288,144]{1,2,0:T(8,128)}, f32[3,288,144]{1,2,0:T(8,128)S(1)}, u32[]{:S(2)}, u32[]{:S(2)}) %collective-permute-start.29) | collective-permute-done | bytes 497696 | tf_op jit(solution)/shard_map/ppermute | solution.py:299
  985.9 13.0 %collective-permute-done.30 = f32[3,288,144]{1,2,0:T(8,128)S(1)} collective-permute-done((f32[3,288,144]{1,2,0:T(8,128)S(1)}, f32[3,288,144]{1,2,0:T(8,128)S(1)}, u32[]{:S(2)}, u32[]{:S(2)}) %collective-permute-start.30) | collective-permute-done | bytes 497696 | tf_op jit(solution)/shard_map/ppermute | solution.py:299
  (899 shorter events, 547.5 us)
Async XLA Ops:
  7.2 942.4 %all-reduce.40.cloned.1.call-start = ((), (), s32[]{:S(2)}) async-start(), calls=%async_computation | async-start | bytes 262144
  76.3 67.5 %collective-permute-start = (f32[256,1152]{1,0:T(8,128)S(1)}, f32[256,1152]{1,0:T(8,128)}, u32[]{:S(2)}, u32[]{:S(2)}) collective-permute-start(f32[256,1152]{1,0:T(8,128)S(1)} %fusion.82), channel_id=1, source_target_pairs={{0,1},{1,0},{2,3},{3,2},{4,5},{5,4},{6,7},{7,6},{8,9},{9,8},{10,11... | collective-permute-start | bytes 3538952 | tf_op jit(solution)/shard_map/ppermute | solution.py:295
  78.4 77.1 %collective-permute-start.71 = (f32[128,1152]{1,0:T(8,128)}, f32[128,1152]{1,0:T(8,128)}, u32[]{:S(2)}, u32[]{:S(2)}) collective-permute-start(f32[128,1152]{1,0:T(8,128)} %constant_dynamic-slice_fusion), channel_id=1, source_target_pairs={{0,8},{8,16},{16,24},{24,0},{1,9},{9,17},{17,25},{25,1},{2,10},{10... | collective-permute-start | bytes 1769480 | tf_op jit(solution)/shard_map/ppermute | solution.py:299
  154.7 32.0 %collective-permute-start.1 = (f32[256,1152]{1,0:T(8,128)S(1)}, f32[256,1152]{1,0:T(8,128)S(1)}, u32[]{:S(2)}, u32[]{:S(2)}) collective-permute-start(f32[256,1152]{1,0:T(8,128)S(1)} %fusion.10), channel_id=1, source_target_pairs={{0,1},{1,0},{2,3},{3,2},{4,5},{5,4},{6,7},{7,6},{8,9},{9,8},{10,11... | collective-permute-start | bytes 3538952 | tf_op jit(solution)/shard_map/ppermute | solution.py:295
  159.6 63.5 %collective-permute-start.72 = (f32[128,1152]{1,0:T(8,128)}, f32[128,1152]{1,0:T(8,128)}, u32[]{:S(2)}, u32[]{:S(2)}) collective-permute-start(f32[128,1152]{1,0:T(8,128)} %collective-permute-done.71.refs_0_), channel_id=1, source_target_pairs={{0,1},{1,0},{2,3},{3,2},{4,5},{5,4},{6,7},{7,6},{8,9},{9,8},{10,11... | collective-permute-start | bytes 1769480 | tf_op jit(solution)/shard_map/ppermute | solution.py:295
  226.3 39.3 %collective-permute-start.49 = (f32[128,1152]{1,0:T(8,128)}, f32[128,1152]{1,0:T(8,128)}, u32[]{:S(2)}, u32[]{:S(2)}) collective-permute-start(f32[128,1152]{1,0:T(8,128)} %copy-done.15), channel_id=1, source_target_pairs={{0,1},{1,0},{2,3},{3,2},{4,5},{5,4},{6,7},{7,6},{8,9},{9,8},{10,11... | collective-permute-start | bytes 1769480 | tf_op jit(solution)/shard_map/ppermute | solution.py:295
  232.0 33.7 %collective-permute-start.51 = (f32[128,1152]{1,0:T(8,128)}, f32[128,1152]{1,0:T(8,128)S(1)}, u32[]{:S(2)}, u32[]{:S(2)}) collective-permute-start(f32[128,1152]{1,0:T(8,128)} %collective-permute-done.50.refs_2_), channel_id=1, source_target_pairs={{0,1},{1,0},{2,3},{3,2},{4,5},{5,4},{6,7},{7,6},{8,9},{9,8},{10,11... | collective-permute-start | bytes 1769480 | tf_op jit(solution)/shard_map/ppermute | solution.py:295
  232.2 34.0 %collective-permute-start.53 = (f32[128,1152]{1,0:T(8,128)}, f32[128,1152]{1,0:T(8,128)S(1)}, u32[]{:S(2)}, u32[]{:S(2)}) collective-permute-start(f32[128,1152]{1,0:T(8,128)} %collective-permute-done.52.refs_4_), channel_id=1, source_target_pairs={{0,1},{1,0},{2,3},{3,2},{4,5},{5,4},{6,7},{7,6},{8,9},{9,8},{10,11... | collective-permute-start | bytes 1769480 | tf_op jit(solution)/shard_map/ppermute | solution.py:295
  265.6 40.2 %collective-permute-start.22 = (f32[3,128,1152]{2,1,0:T(8,128)}, f32[3,128,1152]{2,1,0:T(8,128)}, u32[]{:S(2)}, u32[]{:S(2)}) collective-permute-start(f32[3,128,1152]{2,1,0:T(8,128)} %pad_maximum_fusion.2.remote_ref), channel_id=1, source_target_pairs={{0,1},{1,0},{2,3},{3,2},{4,5},{5,4},{6,7},{7,6},{8,9},{9,8},{10,11... | collective-permute-start | bytes 5308424 | tf_op jit(solution)/shard_map/ppermute | solution.py:295
  276.5 55.1 %collective-permute-start.66 = (f32[128,1152]{1,0:T(8,128)}, f32[128,1152]{1,0:T(8,128)}, u32[]{:S(2)}, u32[]{:S(2)}) collective-permute-start(f32[128,1152]{1,0:T(8,128)} %collective-permute-done.65.refs_0_), channel_id=1, source_target_pairs={{0,1},{1,0},{2,3},{3,2},{4,5},{5,4},{6,7},{7,6},{8,9},{9,8},{10,11... | collective-permute-start | bytes 1769480 | tf_op jit(solution)/shard_map/ppermute | solution.py:295
  278.1 53.4 %collective-permute-start.68 = (f32[128,1152]{1,0:T(8,128)}, f32[128,1152]{1,0:T(8,128)}, u32[]{:S(2)}, u32[]{:S(2)}) collective-permute-start(f32[128,1152]{1,0:T(8,128)} %collective-permute-done.67.refs_2_), channel_id=1, source_target_pairs={{0,1},{1,0},{2,3},{3,2},{4,5},{5,4},{6,7},{7,6},{8,9},{9,8},{10,11... | collective-permute-start | bytes 1769480 | tf_op jit(solution)/shard_map/ppermute | solution.py:295
  281.3 32.4 %collective-permute-start.23 = (f32[128,1152]{1,0:T(8,128)}, f32[128,1152]{1,0:T(8,128)}, u32[]{:S(2)}, u32[]{:S(2)}) collective-permute-start(f32[128,1152]{1,0:T(8,128)} %constant_dynamic-slice_fusion.22), channel_id=1, source_target_pairs={{0,2},{2,0},{1,3},{3,1},{4,6},{6,4},{5,7},{7,5},{8,10},{10,8},{9,1... | collective-permute-start | bytes 1769480 | tf_op jit(solution)/shard_map/ppermute | solution.py:295
  283.5 31.8 %collective-permute-start.24 = (f32[128,1152]{1,0:T(8,128)}, f32[128,1152]{1,0:T(8,128)}, u32[]{:S(2)}, u32[]{:S(2)}) collective-permute-start(f32[128,1152]{1,0:T(8,128)} %constant_dynamic-slice_fusion.22), channel_id=1, source_target_pairs={{0,4},{4,0},{1,5},{5,1},{2,6},{6,2},{3,7},{7,3},{8,12},{12,8},{9,1... | collective-permute-start | bytes 1769480 | tf_op jit(solution)/shard_map/ppermute | solution.py:295
  331.1 178.4 %collective-permute-start.27 = (f32[3,128,1152]{2,1,0:T(8,128)}, f32[3,128,1152]{2,1,0:T(8,128)}, u32[]{:S(2)}, u32[]{:S(2)}) collective-permute-start(f32[3,128,1152]{2,1,0:T(8,128)} %pad_maximum_fusion.3.remote_ref), channel_id=1, source_target_pairs={{0,1},{1,0},{2,3},{3,2},{4,5},{5,4},{6,7},{7,6},{8,9},{9,8},{10,11... | collective-permute-start | bytes 5308424 | tf_op jit(solution)/shard_map/ppermute | solution.py:295
  367.1 136.8 %collective-permute-start.77 = (f32[4,2,72,576]{3,2,1,0:T(8,128)}, f32[4,2,72,576]{3,2,1,0:T(8,128)}, u32[]{:S(2)}, u32[]{:S(2)}) collective-permute-start(f32[4,2,72,576]{3,2,1,0:T(8,128)} %dynamic-slice_bitcast_fusion), channel_id=1, source_target_pairs={{0,2},{2,0},{1,3},{3,1},{4,6},{6,4},{5,7},{7,5},{8,10},{10,8},{9,1... | collective-permute-start | bytes 3981320 | tf_op jit(solution)/shard_map/ppermute | solution.py:295
  375.3 131.4 %collective-permute-start.84 = (f32[2,144,1152]{2,1,0:T(8,128)}, f32[2,144,1152]{2,1,0:T(8,128)}, u32[]{:S(2)}, u32[]{:S(2)}) collective-permute-start(f32[2,144,1152]{2,1,0:T(8,128)} %dynamic-slice_bitcast_fusion.2), channel_id=1, source_target_pairs={{0,4},{4,0},{1,5},{5,1},{2,6},{6,2},{3,7},{7,3},{8,12},{12,8},{9,1... | collective-permute-start | bytes 3981320 | tf_op jit(solution)/shard_map/ppermute | solution.py:295
  386.0 197.5 %collective-permute-start.56 = (f32[128,1152]{1,0:T(8,128)}, f32[128,1152]{1,0:T(8,128)}, u32[]{:S(2)}, u32[]{:S(2)}) collective-permute-start(f32[128,1152]{1,0:T(8,128)} %collective-permute-done.54.refs_0_), channel_id=1, source_target_pairs={{0,8},{8,16},{16,24},{24,0},{1,9},{9,17},{17,25},{25,1},{2,10},{10... | collective-permute-start | bytes 1769480 | tf_op jit(solution)/shard_map/ppermute | solution.py:299
  402.6 179.8 %collective-permute-start.13 = (f32[128,1152]{1,0:T(8,128)}, f32[128,1152]{1,0:T(8,128)}, u32[]{:S(2)}, u32[]{:S(2)}) collective-permute-start(f32[128,1152]{1,0:T(8,128)} %constant_dynamic-slice_fusion.26), channel_id=1, source_target_pairs={{0,2},{2,0},{1,3},{3,1},{4,6},{6,4},{5,7},{7,5},{8,10},{10,8},{9,1... | collective-permute-start | bytes 1769480 | tf_op jit(solution)/shard_map/ppermute | solution.py:295
  503.9 80.0 %collective-permute-start.14 = (f32[128,1152]{1,0:T(8,128)}, f32[128,1152]{1,0:T(8,128)}, u32[]{:S(2)}, u32[]{:S(2)}) collective-permute-start(f32[128,1152]{1,0:T(8,128)} %constant_dynamic-slice_fusion.26), channel_id=1, source_target_pairs={{0,4},{4,0},{1,5},{5,1},{2,6},{6,2},{3,7},{7,3},{8,12},{12,8},{9,1... | collective-permute-start | bytes 1769480 | tf_op jit(solution)/shard_map/ppermute | solution.py:295
  582.4 77.4 %collective-permute-start.55 = (f32[128,1152]{1,0:T(8,128)}, f32[128,1152]{1,0:T(8,128)}, u32[]{:S(2)}, u32[]{:S(2)}) collective-permute-start(f32[128,1152]{1,0:T(8,128)} %collective-permute-done.54.refs_0_), channel_id=1, source_target_pairs={{0,1},{1,0},{2,3},{3,2},{4,5},{5,4},{6,7},{7,6},{8,9},{9,8},{10,11... | collective-permute-start | bytes 1769480 | tf_op jit(solution)/shard_map/ppermute | solution.py:295
  583.5 64.2 %collective-permute-start.7 = (f32[256,1152]{1,0:T(8,128)}, f32[256,1152]{1,0:T(8,128)}, u32[]{:S(2)}, u32[]{:S(2)}) collective-permute-start(f32[256,1152]{1,0:T(8,128)} %convolution_add_fusion), channel_id=1, source_target_pairs={{0,1},{1,0},{2,3},{3,2},{4,5},{5,4},{6,7},{7,6},{8,9},{9,8},{10,11... | collective-permute-start | bytes 3538952 | tf_op jit(solution)/shard_map/ppermute | solution.py:295
  612.5 49.2 %collective-permute-start.57 = (f32[128,1152]{1,0:T(8,128)}, f32[128,1152]{1,0:T(8,128)}, u32[]{:S(2)}, u32[]{:S(2)}) collective-permute-start(f32[128,1152]{1,0:T(8,128)} %collective-permute-done.56.refs_2_), channel_id=1, source_target_pairs={{0,1},{1,0},{2,3},{3,2},{4,5},{5,4},{6,7},{7,6},{8,9},{9,8},{10,11... | collective-permute-start | bytes 1769480 | tf_op jit(solution)/shard_map/ppermute | solution.py:295
  615.2 46.5 %collective-permute-start.59 = (f32[128,1152]{1,0:T(8,128)}, f32[128,1152]{1,0:T(8,128)}, u32[]{:S(2)}, u32[]{:S(2)}) collective-permute-start(f32[128,1152]{1,0:T(8,128)} %collective-permute-done.58.refs_4_), channel_id=1, source_target_pairs={{0,1},{1,0},{2,3},{3,2},{4,5},{5,4},{6,7},{7,6},{8,9},{9,8},{10,11... | collective-permute-start | bytes 1769480 | tf_op jit(solution)/shard_map/ppermute | solution.py:295
  644.0 31.3 %collective-permute-start.35 = (f32[3,288,144]{1,2,0:T(8,128)}, f32[3,288,144]{1,2,0:T(8,128)}, u32[]{:S(2)}, u32[]{:S(2)}) collective-permute-start(f32[3,288,144]{1,2,0:T(8,128)} %bitcast_add_fusion.6), channel_id=1, source_target_pairs={{0,8},{8,16},{16,24},{24,0},{1,9},{9,17},{17,25},{25,1},{2,10},{10... | collective-permute-start | bytes 1493000 | tf_op jit(solution)/shard_map/ppermute | solution.py:299
  652.9 47.4 %collective-permute-start.8 = (f32[128,1152]{1,0:T(8,128)}, f32[128,1152]{1,0:T(8,128)}, u32[]{:S(2)}, u32[]{:S(2)}) collective-permute-start(f32[128,1152]{1,0:T(8,128)} %constant_dynamic-slice_fusion.27), channel_id=1, source_target_pairs={{0,2},{2,0},{1,3},{3,1},{4,6},{6,4},{5,7},{7,5},{8,10},{10,8},{9,1... | collective-permute-start | bytes 1769480 | tf_op jit(solution)/shard_map/ppermute | solution.py:295
  659.8 46.4 %collective-permute-start.9 = (f32[128,1152]{1,0:T(8,128)}, f32[128,1152]{1,0:T(8,128)}, u32[]{:S(2)}, u32[]{:S(2)}) collective-permute-start(f32[128,1152]{1,0:T(8,128)} %constant_dynamic-slice_fusion.27), channel_id=1, source_target_pairs={{0,4},{4,0},{1,5},{5,1},{2,6},{6,2},{3,7},{7,3},{8,12},{12,8},{9,1... | collective-permute-start | bytes 1769480 | tf_op jit(solution)/shard_map/ppermute | solution.py:295
  683.7 66.3 %collective-permute-start.60 = (f32[4,2,72,576]{3,2,1,0:T(8,128)}, f32[4,2,72,576]{3,2,1,0:T(8,128)}, u32[]{:S(2)}, u32[]{:S(2)}) collective-permute-start(f32[4,2,72,576]{3,2,1,0:T(8,128)} %dynamic-slice_bitcast_fusion.1), channel_id=1, source_target_pairs={{0,2},{2,0},{1,3},{3,1},{4,6},{6,4},{5,7},{7,5},{8,10},{10,8},{9,1... | collective-permute-start | bytes 3981320 | tf_op jit(solution)/shard_map/ppermute | solution.py:295
  706.2 298.2 %collective-permute-start.47 = (f32[36,1152]{1,0:T(8,128)}, f32[36,1152]{1,0:T(8,128)}, u32[]{:S(2)}, u32[]{:S(2)}) collective-permute-start(f32[36,1152]{1,0:T(8,128)} %bitcast_add_fusion.16), channel_id=1, source_target_pairs={{0,0},{2,8},{4,16},{6,24},{8,2},{10,10},{12,18},{14,26},{16,4},{18... | collective-permute-start | bytes 497672 | tf_op jit(solution)/shard_map/ppermute | solution.py:489
  710.0 46.4 %collective-permute-start.82 = (f32[2,144,1152]{2,1,0:T(8,128)}, f32[2,144,1152]{2,1,0:T(8,128)}, u32[]{:S(2)}, u32[]{:S(2)}) collective-permute-start(f32[2,144,1152]{2,1,0:T(8,128)} %dynamic-slice_bitcast_fusion.3), channel_id=1, source_target_pairs={{0,4},{4,0},{1,5},{5,1},{2,6},{6,2},{3,7},{7,3},{8,12},{12,8},{9,1... | collective-permute-start | bytes 3981320 | tf_op jit(solution)/shard_map/ppermute | solution.py:295
  749.5 45.9 %collective-permute-start.12 = (f32[3,128,1152]{2,1,0:T(8,128)}, f32[3,128,1152]{2,1,0:T(8,128)}, u32[]{:S(2)}, u32[]{:S(2)}) collective-permute-start(f32[3,128,1152]{2,1,0:T(8,128)} %pad_maximum_fusion.remote_ref), channel_id=1, source_target_pairs={{0,1},{1,0},{2,3},{3,2},{4,5},{5,4},{6,7},{7,6},{8,9},{9,8},{10,11... | collective-permute-start | bytes 5308424 | tf_op jit(solution)/shard_map/ppermute | solution.py:295
  839.1 118.9 %collective-permute-start.28 = (f32[3,288,144]{1,2,0:T(8,128)}, f32[3,288,144]{1,2,0:T(8,128)}, u32[]{:S(2)}, u32[]{:S(2)}) collective-permute-start(f32[3,288,144]{1,2,0:T(8,128)} %bitcast.745), channel_id=1, source_target_pairs={{0,8},{8,16},{16,24},{24,0},{1,9},{9,17},{17,25},{25,1},{2,10},{10... | collective-permute-start | bytes 1493000 | tf_op jit(solution)/shard_map/ppermute | solution.py:299
  843.0 114.2 %collective-permute-start.40 = (f32[36,1152]{1,0:T(8,128)S(1)}, f32[36,1152]{1,0:T(8,128)S(1)}, u32[]{:S(2)}, u32[]{:S(2)}) collective-permute-start(f32[36,1152]{1,0:T(8,128)S(1)} %dynamic-slice_bitcast_fusion.37), channel_id=1, source_target_pairs={{0,8},{8,16},{16,24},{24,0},{1,9},{9,17},{17,25},{25,1},{2,10},{10... | collective-permute-start | bytes 497672 | tf_op jit(solution)/shard_map/ppermute | solution.py:299
  (236 other events, 2355.5 us)
Sparse Core Ops, SparseCore 0:
  840.8 108.8 all-reduce.39

commit v2 on v0

v2 whole, which is shorter than its diff:
```python
import functools
import math

import jax
import jax.numpy as jnp
from jax import lax
from jax.experimental import pallas as pl
from jax.experimental.pallas import tpu as pltpu
from jax.sharding import Mesh
from jax.sharding import PartitionSpec as P

SIDE = 16
HALF = 8
SPAN = SIDE * SIDE
IMAGES = 4
BLOCK = SPAN // IMAGES
GROUP = 4
EPSILON = 1e-06
MASKED = -1e30
ROOT_HALF = 0.7071067811865476
SLOPE_NORM = 0.3989422804014327
LINES = ("line", "col", "row")
LOW = jnp.bfloat16
FULL = jnp.float32
KIND, AT_LINE, AT_COL, AT_ROW, AT_CORE = range(5)


def matmul(left, right, dims=((1,), (0,))):
    return lax.dot_general(left, right, (dims, ((), ())), preferred_element_type=FULL)


NT = ((1,), (1,))
TN = ((0,), (0,))


def normal_of(stream):
    center = stream - jnp.mean(stream, axis=-1, keepdims=True)
    inverse = lax.rsqrt(jnp.mean(center * center, axis=-1, keepdims=True) + EPSILON)
    return center * inverse, inverse


def norm_backward(stream, gain, upstream):
    normal, inverse = normal_of(stream)
    gain_part = jnp.sum(upstream * normal, axis=0, keepdims=True)
    shift_part = jnp.sum(upstream, axis=0, keepdims=True)
    scaled = upstream * gain
    inner = (
        scaled
        - jnp.mean(scaled, axis=-1, keepdims=True)
        - normal * jnp.mean(scaled * normal, axis=-1, keepdims=True)
    )
    return inner * inverse, gain_part, shift_part


def sinusoid(steps, feature, width):
    half = width // 2
    rates = jnp.exp(-math.log(10000.0) * (feature % half).astype(FULL) / half)
    angles = steps.astype(FULL)[:, None] * rates[None, :]
    wave = jnp.where(feature[None, :] < half, jnp.cos(angles), jnp.sin(angles))
    return wave.astype(LOW)


def whole(shape):
    return pl.BlockSpec(shape, lambda *_: (0,) * len(shape))


def whole_once(shape):
    return pl.BlockSpec(shape, lambda *_: (0,) * len(shape), pipeline_mode=pl.Buffered(1))


def call(kernel, name, grid, in_specs, out_specs, out_shape, scratch, flops, size, scalars=1, after=()):
    first = scalars + len(in_specs)

    def body(*refs):
        kernel(*refs[:first], *refs[first + len(after) :])

    made = pl.pallas_call(
        body,
        grid_spec=pltpu.PrefetchScalarGridSpec(
            num_scalar_prefetch=scalars,
            grid=grid,
            in_specs=[*in_specs, *[pl.BlockSpec(memory_space=pl.ANY)] * len(after)],
            out_specs=out_specs,
            scratch_shapes=scratch,
        ),
        out_shape=[pltpu.HBM(out.shape, out.dtype) for out in out_shape],
        compiler_params=pltpu.CompilerParams(vmem_limit_bytes=40 << 20),
        cost_estimate=pl.CostEstimate(
            flops=int(flops), bytes_accessed=int(size), transcendentals=0
        ),
        name=name,
    )
    return lambda *operands: made(*operands, *map(in_hbm, after))


def shape_of(shape, kind=FULL):
    return jax.ShapeDtypeStruct(shape, kind)


def regroup(value, pieces):
    lane = lax.broadcasted_iota(jnp.int32, (value.shape[0], 128), 1)
    total = jnp.zeros((value.shape[0], 128), FULL)
    for tile, source, place, lanes in pieces:
        part = value[:, tile * 128 : tile * 128 + 128]
        turn = (place - source) % 128
        part = part if turn == 0 else pltpu.roll(part, turn, 1)
        total = jnp.where((lane >= place) & (lane < place + lanes), part, total)
    return total


def expand_kernel(table_ref, wide_ref, small_ref):
    size = table_ref.shape[1]
    table = table_ref[...]
    for c in range(SIDE):
        turned = pltpu.roll(table, size - SIDE + c, 1)
        wide = jnp.concatenate(
            [
                regroup(
                    turned,
                    [(2 * o + p // 4, 32 * (p % 4), 16 * p, 16) for p in range(8)],
                )
                for o in range(4)
            ],
            axis=1,
        )
        wide_ref[:, c, :] = wide
        if c < HALF:
            small_ref[:, c, :] = regroup(
                wide, [(1 + k // 8, 16 * (k % 8), 8 * k, 8) for k in range(16)]
            )


def expand_table(table):
    rows, size = table.shape
    return pl.pallas_call(
        expand_kernel,
        out_shape=[shape_of((rows, SIDE, size // 2)), shape_of((rows, HALF, size // 8))],
        name="expand_table",
    )(table)


def fold_table(wide, small):
    inner = jnp.concatenate([small, jnp.zeros_like(small)], axis=0)
    tiles = [wide[:, 128 * t : 128 * t + 128] for t in range(4)]
    for t in range(2):
        tiles[1 + t] = tiles[1 + t] + regroup(
            inner, [(0, 8 * (8 * t + q), 16 * q, 8) for q in range(8)]
        )
    wide = jnp.concatenate(tiles, axis=1)
    spread = jnp.concatenate(
        [
            regroup(
                wide,
                [(o // 2, 64 * (o % 2) + 16 * q, 32 * q, 16) for q in range(4)],
            )
            for o in range(8)
        ],
        axis=1,
    )
    return functools.reduce(
        jnp.add, [pltpu.roll(spread[c : c + 1], SIDE - c, 1) for c in range(SIDE)]
    )


def fill_bias(heads, kind, wide_ref, small_ref, bias):
    @pl.when(kind == 0)
    def _():
        for head in range(heads):
            wide = wide_ref[head]
            for r in range(SIDE):
                turned = pltpu.roll(wide, 2 * SPAN - SIDE * (SIDE - r), 1)
                bias[head, r * SIDE : (r + 1) * SIDE, :] = turned[:, :SPAN]

    @pl.when(kind != 0)
    def _():
        image = lax.broadcasted_iota(jnp.int32, (HALF, SPAN), 1) // BLOCK
        lane = lax.broadcasted_iota(jnp.int32, (HALF, 2 * BLOCK), 1)
        for head in range(heads):
            small = small_ref[head]
            for r in range(HALF):
                turned = pltpu.roll(small, 2 * BLOCK - HALF * (HALF - r), 1)
                turned = jnp.where(lane < BLOCK, turned, 0.0)
                pair = turned + pltpu.roll(turned, BLOCK, 1)
                line = jnp.concatenate([pair, pair], axis=1)
                for i in range(IMAGES):
                    start = i * BLOCK + r * HALF
                    bias[head, start : start + HALF, :] = jnp.where(image == i, line, MASKED)


def collect_table(heads, kind, back, wide_sum, small_sum):
    @pl.when(kind == 0)
    def _():
        for head in range(heads):
            total = wide_sum[head]
            for r in range(SIDE):
                part = back[head, r * SIDE : (r + 1) * SIDE, :]
                part = jnp.concatenate([part, jnp.zeros_like(part)], axis=1)
                total = total + pltpu.roll(part, SIDE * (SIDE - r), 1)
            wide_sum[head] = total

    @pl.when(kind != 0)
    def _():
        for head in range(heads):
            total = small_sum[head]
            lane = lax.broadcasted_iota(jnp.int32, total.shape, 1)
            for r in range(HALF):
                part = functools.reduce(
                    jnp.add,
                    [
                        back[head, i * BLOCK + r * HALF : i * BLOCK + (r + 1) * HALF, :]
                        for i in range(IMAGES)
                    ],
                )
                part = part[:, : SPAN // 2] + part[:, SPAN // 2 :]
                part = jnp.where(lane < BLOCK, part + pltpu.roll(part, BLOCK, 1), 0.0)
                total = total + pltpu.roll(part, HALF * (HALF - r), 1)
            small_sum[head] = total


def window_of(head, head_dim, width):
    if width <= 256:
        return 0, width
    return head * head_dim // 128 * 128, min(-(-(head + 1) * head_dim // 128) * 128, width)


def mine_of(head, head_dim, first, last, rows):
    lane = lax.broadcasted_iota(jnp.int32, (rows, last - first), 1) + first
    return (lane >= head * head_dim) & (lane < (head + 1) * head_dim)


def softmax_of(queries, keys, bias, scale):
    scores = matmul(keys, queries, NT) * scale + bias
    expo = jnp.exp(scores - jnp.max(scores, axis=0, keepdims=True))
    return expo * (1.0 / jnp.sum(expo, axis=0, keepdims=True))


def attention_forward(heads, row, bias, total):
    count, width = total.shape
    head_dim = width // heads
    scale = 1.0 / math.sqrt(head_dim)
    zero = jnp.zeros((), LOW)
    total[...] = jnp.zeros_like(total)
    for head in range(heads):
        first, last = window_of(head, head_dim, width)
        mine = mine_of(head, head_dim, first, last, count)
        queries = jnp.where(mine, row(0, first, last), zero)
        values = jnp.where(mine, row(2, first, last), zero)
        weights = softmax_of(queries, row(1, first, last), bias[head], scale)
        total[:, first:last] += matmul(weights.astype(LOW), values, TN)


def attention_backward(heads, row, bias, steps, attended, scores_out):
    count, width = steps.shape[1:]
    head_dim = width // heads
    scale = 1.0 / math.sqrt(head_dim)
    zero = jnp.zeros((), LOW)
    steps[...] = jnp.zeros_like(steps)
    if attended is not None:
        attended[...] = jnp.zeros_like(attended)
    for head in range(heads):
        first, last = window_of(head, head_dim, width)
        mine = mine_of(head, head_dim, first, last, count)
        queries, keys, values, upstream = (
            jnp.where(mine, row(member, first, last), zero) for member in range(4)
        )
        weights = softmax_of(queries, keys, bias[head], scale)
        low = weights.astype(LOW)
        back_weights = matmul(values, upstream, NT)
        inner = jnp.sum(weights * back_weights, axis=0, keepdims=True)
        back_scores = (weights * (back_weights - inner)).astype(LOW)
        steps[0, :, first:last] += matmul(back_scores, keys, TN) * scale
        steps[1, :, first:last] += matmul(back_scores, queries) * scale
        steps[2, :, first:last] += matmul(low, upstream)
        if attended is not None:
            attended[:, first:last] += matmul(low, values, TN)
        if scores_out is not None:
            scores_out[head] = back_scores.astype(FULL)


def in_hbm(value):
    return pltpu.with_memory_space_constraint(value, pltpu.HBM)


HBM = pl.BlockSpec(memory_space=pltpu.HBM)
NEAR = pl.BlockSpec(memory_space=pltpu.VMEM)


def plain(kernel, name, scalars, near, far, outs, scratch, flops, size, limit, after=()):
    first = len(scalars) + len(near) + len(far)

    def body(*refs):
        kernel(*refs[:first], *refs[first + len(after) :])

    return pl.pallas_call(
        body,
        in_specs=[
            *[pl.BlockSpec(memory_space=pltpu.SMEM)] * len(scalars),
            *[NEAR] * len(near),
            *[HBM] * (len(far) + len(after)),
        ],
        out_specs=[HBM] * len(outs),
        out_shape=[pltpu.HBM(out.shape, out.dtype) for out in outs],
        scratch_shapes=[*scratch, pltpu.SemaphoreType.DMA((24,))],
        compiler_params=pltpu.CompilerParams(vmem_limit_bytes=limit << 20),
        cost_estimate=pl.CostEstimate(
            flops=int(flops), bytes_accessed=int(size), transcendentals=0
        ),
        name=name,
    )(*scalars, *near, *map(in_hbm, (*far, *after)))


def gate(values):
    def body(*refs):
        del refs

    return pl.pallas_call(
        body,
        in_specs=[HBM] * len(values),
        out_specs=[HBM] * len(values),
        out_shape=[pltpu.HBM(value.shape, value.dtype) for value in values],
        input_output_aliases={i: i for i in range(len(values))},
        name="gate",
    )(*map(in_hbm, values))


class Moves:
    def __init__(self):
        self.running, self.found = [], {}

    def start(self, name, steps):
        self.running.append((name, steps, next(steps)))

    def kernel(self, output, due=()):
        arrived = [array for _, _, arrays in self.running for array in arrays]
        held = gate([output, *due, *arrived])
        self.step(iter(held[1 + len(due) :]))
        return held[: 1 + len(due)]

    def step(self, arrived=None):
        before, self.running = self.running, []
        for name, steps, arrays in before:
            if arrived is not None:
                arrays = [next(arrived) for _ in arrays]
            try:
                self.running.append((name, steps, steps.send(arrays)))
            except StopIteration as stop:
                self.found[name] = stop.value

    def finish(self):
        while self.running:
            self.step()


class Copies:
    def __init__(self, sems):
        self.sems, self.count, self.leaving = sems, 0, []

    def start(self, source, target):
        copy = pltpu.make_async_copy(source, target, self.sems.at[self.count])
        self.count += 1
        copy.start()
        return copy

    def leave(self, source, target):
        self.leaving.append(self.start(source, target))

    def finish(self):
        for copy in self.leaving:
            copy.wait()


def core_half(ref, ids):
    half = ref.shape[0] // 2
    return ref.at[pl.ds(pl.multiple_of(ids[AT_CORE] * half, half), half)]


def attend_kernel(layer, heads, ids, gain_ref, shift_ref, biases_ref, *refs):
    parts = 1 if layer == 0 else 3
    stream_hbm, refs = refs[:parts], refs[parts:]
    token_hbm, out_hbm, image_hbm, wide_hbm, small_hbm = refs[:5]
    stream_out, normed_out, half_out, row_out, partial_out, bias_out = refs[5:11]
    stream_in, token, outer, image, wide, small, normed, low, rows, bias, total, partial, sems = refs[11:]
    copies = Copies(sems)
    per = pl.ds(layer * heads, heads)
    near = [copies.start(source, stream_in.at[i]) for i, source in enumerate(stream_hbm)]
    tables = [copies.start(wide_hbm.at[per], wide), copies.start(small_hbm.at[per], small)]
    tokens = [copies.start(token_hbm.at[layer, 0], token.at[0])]
    images = copies.start(image_hbm.at[layer], image)
    tokens += [copies.start(token_hbm.at[layer, m], token.at[m]) for m in (1, 2)]
    outers = copies.start(out_hbm.at[layer], outer)
    kind = ids[KIND]
    count = low.shape[0]
    for copy in near:
        copy.wait()
    if layer == 0:
        stream = stream_in[0].astype(FULL)
    else:
        stream = stream_in[0] + (stream_in[1] + stream_in[2]) + biases_ref[layer - 1, 1:2, :]
    normed[...] = normal_of(stream)[0] * gain_ref[layer, 0:1, :] + shift_ref[layer, 0:1, :]
    if layer == 0:
        partial[...] = stream
        copies.leave(partial, stream_out)
    else:
        stream_in[0] = stream
        copies.leave(stream_in.at[0], stream_out)
    copies.leave(normed, normed_out)
    copies.leave(core_half(normed, ids), half_out)
    low[...] = normed[...].astype(LOW)
    for copy in tables:
        copy.wait()
    fill_bias(heads, kind, wide, small, bias)
    copies.leave(bias, bias_out)
    for member in range(3):
        tokens[member].wait()
        projected = matmul(low[...], token[member], NT)
        if member == 0:
            images.wait()
        if member == 1:
            rows[member] = projected.astype(LOW)
            continue
        for i in range(IMAGES):
            mine = image[member // 2, i : i + 1, :]
            mine = jnp.where(kind != 0, mine, image[member // 2, 0:1, :])
            here = slice(i * (count // IMAGES), (i + 1) * (count // IMAGES))
            rows[member, here, :] = (projected[here] + mine).astype(LOW)
    copies.leave(rows, row_out)

    def row(index, first, last):
        return rows[index, :, first:last]

    attention_forward(heads, row, bias, total)
    outers.wait()
    if layer == 0:
        copies.leaving.pop(0).wait()
    partial[...] = matmul(total[...].astype(LOW), outer[...])
    copies.leave(partial, partial_out)
    copies.finish()


def attend(layer, ids, stream, gains, shifts, biases, token_rows, per_image, out_proj, wide, small, after=()):
    count, width = stream[0].shape
    depth, _, local, _ = token_rows.shape
    heads = wide.shape[0] // depth
    full = shape_of((count, width))
    outs = [
        full,
        full,
        shape_of((count // 2, width)),
        shape_of((3, count, local), LOW),
        full,
        shape_of((heads, count, count)),
    ]
    return plain(
        functools.partial(attend_kernel, layer, heads),
        f"attend_{layer}",
        (ids,),
        (gains, shifts, biases),
        (*stream, token_rows, out_proj, per_image, wide, small),
        outs,
        [
            pltpu.VMEM((len(stream), count, width), stream[0].dtype),
            pltpu.VMEM((3, local, width), LOW),
            pltpu.VMEM((local, width), LOW),
            pltpu.VMEM(per_image.shape[1:], FULL),
            pltpu.VMEM((heads, *wide.shape[1:]), FULL),
            pltpu.VMEM((heads, *small.shape[1:]), FULL),
            pltpu.VMEM((count, width), FULL),
            pltpu.VMEM((count, width), LOW),
            pltpu.VMEM((3, count, local), LOW),
            pltpu.VMEM((heads, count, count), FULL),
            pltpu.VMEM((count, local), FULL),
            pltpu.VMEM((count, width), FULL),
        ],
        2 * count * width * local * 4 + heads * count * count * 2048,
        8 * width * local + 16 * count * width,
        40,
        after,
    )


CHUNK = 768


def feed_kernel(layer, ids, gain_ref, shift_ref, biases_ref, stream_hbm, part_hbm, other_hbm, in_hbm_ref, out_hbm_ref, middle_out, half_out, slope_out, partial_out, stream_in, inner, outer, normed, low, slope, partial, sems):
    units = inner.shape[1]
    chunks = [slice(at, at + CHUNK) for at in range(0, units, CHUNK)]
    copies = Copies(sems)
    near = [
        copies.start(source, stream_in.at[i])
        for i, source in enumerate((stream_hbm, part_hbm, other_hbm))
    ]
    weights = [
        (
            copies.start(in_hbm_ref.at[layer, :, chunk], inner.at[:, chunk]),
            copies.start(out_hbm_ref.at[layer, chunk, :], outer.at[chunk, :]),
        )
        for chunk in chunks
    ]
    for copy in near:
        copy.wait()
    middle = stream_in[0] + (stream_in[1] + stream_in[2]) + biases_ref[layer, 0:1, :]
    stream_in[0] = middle
    copies.leave(stream_in.at[0], middle_out)
    normed[...] = normal_of(middle)[0] * gain_ref[layer, 1:2, :] + shift_ref[layer, 1:2, :]
    copies.leave(core_half(normed, ids), half_out)
    low[...] = normed[...].astype(LOW)
    for at, chunk in enumerate(chunks):
        weights[at][0].wait()
        hidden = matmul(low[...], inner[:, chunk])
        rise = 0.5 * (1.0 + lax.erf(hidden * ROOT_HALF))
        slope[:, chunk] = rise + hidden * jnp.exp(-0.5 * hidden * hidden) * SLOPE_NORM
        copies.leave(slope.at[:, chunk], slope_out.at[:, chunk])
        weights[at][1].wait()
        product = matmul((hidden * rise).astype(LOW), outer[chunk, :])
        partial[...] = product if at == 0 else partial[...] + product
    copies.leave(partial, partial_out)
    copies.finish()


def feed(layer, ids, stream, partial, other, biases, gains, shifts, hidden_in, hidden_out, after=()):
    count, width = stream.shape
    units = hidden_in.shape[2]
    full = shape_of((count, width))
    return plain(
        functools.partial(feed_kernel, layer),
        f"feed_{layer}",
        (ids,),
        (gains, shifts, biases),
        (stream, partial, other, hidden_in, hidden_out),
        [full, shape_of((count // 2, width)), shape_of((count, units)), full],
        [
            pltpu.VMEM((3, count, width), FULL),
            pltpu.VMEM((width, units), LOW),
            pltpu.VMEM((units, width), LOW),
            pltpu.VMEM((count, width), FULL),
            pltpu.VMEM((count, width), LOW),
            pltpu.VMEM((count, units), FULL),
            pltpu.VMEM((count, width), FULL),
        ],
        4 * count * width * units,
        4 * width * units + 4 * count * (units + 6 * width),
        48,
        after,
    )


def feed_back_kernel(layer, last, ids, gain_ref, *refs):
    parts = 1 if last else 4
    up_hbm, refs = refs[:parts], refs[parts:]
    slope_hbm, in_hbm_ref, out_hbm_ref, upstream_out, half_out, sums_out, partial_out = refs[:7]
    up_in, inner, outer, upstream, low, slope, sums, partial, sems = refs[7:]
    units = inner.shape[1]
    chunks = [slice(at, at + CHUNK) for at in range(0, units, CHUNK)]
    copies = Copies(sems)
    near = [copies.start(source, up_in.at[i]) for i, source in enumerate(up_hbm)]
    weights = [
        (
            copies.start(out_hbm_ref.at[layer, chunk, :], outer.at[chunk, :]),
            copies.start(slope_hbm.at[:, chunk], slope.at[:, chunk]),
            copies.start(in_hbm_ref.at[layer, :, chunk], inner.at[:, chunk]),
        )
        for chunk in chunks
    ]
    for copy in near:
        copy.wait()
    sums[...] = jnp.zeros_like(sums)
    if last:
        upstream[...] = up_in[0].astype(FULL)
    else:
        step, gain_part, shift_part = norm_backward(
            up_in[3], gain_ref[layer + 1, 0:1, :], up_in[1] + up_in[2]
        )
        upstream[...] = up_in[0] + step
        sums[1:2, :] = gain_part
        sums[2:3, :] = shift_part
    copies.leave(upstream, upstream_out)
    copies.leave(core_half(upstream, ids), half_out)
    low[...] = upstream[...].astype(LOW)
    sums[0:1, :] = jnp.sum(low[...].astype(FULL), axis=0, keepdims=True)
    copies.leave(sums, sums_out)
    for at, chunk in enumerate(chunks):
        weights[at][0].wait()
        back = matmul(low[...], outer[chunk, :], NT)
        weights[at][1].wait()
        weights[at][2].wait()
        product = matmul((back * slope[:, chunk]).astype(LOW), inner[:, chunk], NT)
        partial[...] = product if at == 0 else partial[...] + product
    copies.leave(partial, partial_out)
    copies.finish()


def feed_back(layer, ids, upstream, slope, hidden_in, hidden_out, gains, after=()):
    count, width = upstream[0].shape
    units = hidden_in.shape[2]
    full = shape_of((count, width))
    return plain(
        functools.partial(feed_back_kernel, layer, len(upstream) == 1),
        f"feed_back_{layer}",
        (ids,),
        (gains,),
        (*upstream, slope, hidden_in, hidden_out),
        [full, shape_of((count // 2, width)), shape_of((8, width)), full],
        [
            pltpu.VMEM((len(upstream), count, width), upstream[0].dtype),
            pltpu.VMEM((width, units), LOW),
            pltpu.VMEM((units, width), LOW),
            pltpu.VMEM((count, width), FULL),
            pltpu.VMEM((count, width), LOW),
            pltpu.VMEM((count, units), FULL),
            pltpu.VMEM((8, width), FULL),
            pltpu.VMEM((count, width), FULL),
        ],
        4 * count * width * units,
        4 * width * units + 4 * count * (units + 6 * width),
        48,
        after,
    )


def attend_back_kernel(layer, heads, ids, gain_ref, up_hbm, part_hbm, other_hbm, middle_hbm, row_hbm, bias_hbm, out_hbm, token_hbm, back_out, half_out, sums_out, partial_out, up_in, rows, bias, token, outer, back, sums, upstream, steps, partial, sems):
    copies = Copies(sems)
    near = [
        copies.start(source, up_in.at[i])
        for i, source in enumerate((up_hbm, part_hbm, other_hbm, middle_hbm))
    ]
    outers = copies.start(out_hbm.at[layer], outer)
    saved = [copies.start(row_hbm, rows), copies.start(bias_hbm, bias)]
    tokens = [copies.start(token_hbm.at[layer, member], token.at[member]) for member in range(3)]
    for copy in near:
        copy.wait()
    step, gain_part, shift_part = norm_backward(
        up_in[3], gain_ref[layer, 1:2, :], up_in[1] + up_in[2]
    )
    back[...] = up_in[0] + step
    copies.leave(back, back_out)
    copies.leave(core_half(back, ids), half_out)
    rounded = back[...].astype(LOW)
    sums[...] = jnp.zeros_like(sums)
    sums[0:1, :] = jnp.sum(rounded.astype(FULL), axis=0, keepdims=True)
    sums[1:2, :] = gain_part
    sums[2:3, :] = shift_part
    copies.leave(sums, sums_out)
    outers.wait()
    upstream[...] = matmul(rounded, outer[...], NT).astype(LOW)

    def row(index, first, last):
        return upstream[:, first:last] if index == 3 else rows[index, :, first:last]

    for copy in saved:
        copy.wait()
    attention_backward(heads, row, bias, steps, None, None)
    for member in range(3):
        tokens[member].wait()
        product = matmul(steps[member].astype(LOW), token[member])
        partial[...] = product if member == 0 else partial[...] + product
    copies.leave(partial, partial_out)
    copies.finish()


def attend_back(layer, ids, upstream, partial, other, middle, gains, rows, bias, out_proj, token_rows, after=()):
    count, width = upstream.shape
    local = token_rows.shape[2]
    heads = bias.shape[0]
    full = shape_of((count, width))
    return plain(
        functools.partial(attend_back_kernel, layer, heads),
        f"attend_back_{layer}",
        (ids,),
        (gains,),
        (upstream, partial, other, middle, rows, bias, out_proj, token_rows),
        [full, shape_of((count // 2, width)), shape_of((8, width)), full],
        [
            pltpu.VMEM((4, count, width), FULL),
            pltpu.VMEM((3, count, local), LOW),
            pltpu.VMEM((heads, count, count), FULL),
            pltpu.VMEM((3, local, width), LOW),
            pltpu.VMEM((local, width), LOW),
            pltpu.VMEM((count, width), FULL),
            pltpu.VMEM((8, width), FULL),
            pltpu.VMEM((count, local), LOW),
            pltpu.VMEM((3, count, local), FULL),
            pltpu.VMEM((count, width), FULL),
        ],
        2 * count * width * local * 4 + heads * count * count * 4096,
        8 * width * local + 24 * count * width,
        40,
        after,
    )


def finish_kernel(gain_ref, up_hbm, part_hbm, other_hbm, stream_hbm, gradient_out, sums_out, up_in, gradient, sums, sems):
    copies = Copies(sems)
    near = [
        copies.start(source, up_in.at[i])
        for i, source in enumerate((up_hbm, part_hbm, other_hbm, stream_hbm))
    ]
    for copy in near:
        copy.wait()
    step, gain_part, shift_part = norm_backward(up_in[3], gain_ref[0, 0:1, :], up_in[1] + up_in[2])
    gradient[...] = (up_in[0] + step).astype(LOW)
    copies.leave(gradient, gradient_out)
    sums[...] = jnp.zeros_like(sums)
    sums[1:2, :] = gain_part
    sums[2:3, :] = shift_part
    copies.leave(sums, sums_out)
    copies.finish()


def finish(upstream, partial, other, stream, gains):
    count, width = stream.shape
    return plain(
        finish_kernel,
        "finish",
        (),
        (gains,),
        (upstream, partial, other, stream),
        [shape_of((count, width), LOW), shape_of((8, width))],
        [
            pltpu.VMEM((4, count, width), FULL),
            pltpu.VMEM((count, width), LOW),
            pltpu.VMEM((8, width), FULL),
        ],
        0,
        20 * count * width,
        24,
    )


def line_window(units, line):
    own = units // line
    offsets = [z * own % 128 for z in range(line)]
    size = -(-(max(offsets) + own) // 128) * 128
    starts = [min(z * own // 128 * 128, units - size) for z in range(line)]
    return starts, [z * own - starts[z] for z in range(line)], size


def feed_gradients_kernel(layer, line, ids, x_hbm, y_hbm, in_hbm, out_hbm, outer_keep, outer_send, inner_keep, inner_send, stage, part_in, part_out, low_x, low_y, active, back, outer, inner, sems):
    units = in_hbm.shape[2]
    width = low_x.shape[1]
    rows = stage.shape[2]
    own = units // line
    starts, offsets, size = line_window(units, line)
    at = ids[AT_LINE]
    start, offset = jnp.int32(starts[0]), jnp.int32(offsets[0])
    for z in range(1, line):
        start = jnp.where(at == z, starts[z], start)
        offset = jnp.where(at == z, offsets[z], offset)
    start = pl.multiple_of(start, 128)
    copies = [
        pltpu.make_async_copy(in_hbm.at[layer, :, pl.ds(start, size)], part_in, sems.at[0, 2]),
        pltpu.make_async_copy(out_hbm.at[layer, pl.ds(start, size), :], part_out, sems.at[1, 2]),
    ]

    def fetch(tile):
        slot = tile % 2
        return [
            pltpu.make_async_copy(
                source.at[pl.ds(tile * rows, rows)], stage.at[side, slot], sems.at[side, slot]
            )
            for side, source in enumerate((x_hbm, y_hbm))
        ]

    flying = {0: fetch(0)}
    for copy in (*flying[0], *copies):
        copy.start()
    for tile in range(line):
        if tile + 1 < line:
            flying[tile + 1] = fetch(tile + 1)
            for copy in flying[tile + 1]:
                copy.start()
        for copy in flying[tile]:
            copy.wait()
        if tile == 0:
            for copy in copies:
                copy.wait()
        here = slice(tile * rows, (tile + 1) * rows)
        low_x[here, :] = stage[0, tile % 2].astype(LOW)
        low_y[here, :] = stage[1, tile % 2].astype(LOW)
        hidden = matmul(low_x[here, :], part_in[...])
        rise = 0.5 * (1.0 + lax.erf(hidden * ROOT_HALF))
        active[here, :] = (hidden * rise).astype(LOW)
        slope = rise + hidden * jnp.exp(-0.5 * hidden * hidden) * SLOPE_NORM
        back[here, :] = (matmul(low_y[here, :], part_out[...], NT) * slope).astype(LOW)

    @pl.loop(0, size // 128)
    def _(tile):
        lanes = pl.ds(pl.multiple_of(tile * 128, 128), 128)
        outer[lanes, :] = matmul(active[:, lanes], low_y[...], TN)

    @pl.loop(0, width // 128)
    def _(tile):
        lanes = pl.ds(pl.multiple_of(tile * 128, 128), 128)
        inner[lanes, :] = matmul(low_x[:, lanes], back[...], TN)

    pair = own // 2
    step = width // (GROUP * line)
    for z in range(len(set(offsets))):
        shifted = sorted(set(offsets))[z]
        for col in range(2):

            @pl.when((offset == shifted) & (ids[AT_COL] == col))
            def _(shifted=shifted, col=col):
                for target, part in ((outer_keep, col), (outer_send, 1 - col)):
                    first = shifted + part * pair
                    for r in range(2):
                        begin = first + r * (pair // 2)
                        target[r] = outer[begin : begin + pair // 2, :]

    for row in range(2):

        @pl.when(ids[AT_ROW] == row)
        def _(row=row):
            for z in range(line):
                for c in range(2):
                    for target, part in ((inner_keep, row), (inner_send, 1 - row)):
                        begin = (GROUP * z + 2 * c + part) * step
                        target[c, z] = inner[begin : begin + step, :]


def feed_gradients(layer, line, ids, xs, ys, hidden_in, hidden_out, after=()):
    count, width = xs.shape
    rows = count // line
    units = hidden_in.shape[2]
    own = units // line
    size = line_window(units, line)[2]
    anywhere = pl.BlockSpec(memory_space=pl.ANY)
    outs = [shape_of((2, own // 4, width))] * 2 + [shape_of((2, line, width // (GROUP * line), size))] * 2
    return call(
        functools.partial(feed_gradients_kernel, layer, line),
        f"feed_gradients_{layer}",
        (1,),
        [anywhere] * 2 + [pl.BlockSpec(memory_space=pltpu.HBM)] * 2,
        [whole_once(out.shape) for out in outs],
        outs,
        [
            pltpu.VMEM((2, 2, rows, width), FULL),
            pltpu.VMEM((width, size), LOW),
            pltpu.VMEM((size, width), LOW),
            pltpu.VMEM((line * rows, width), LOW),
            pltpu.VMEM((line * rows, width), LOW),
            pltpu.VMEM((line * rows, size), LOW),
            pltpu.VMEM((line * rows, size), LOW),
            pltpu.VMEM((size, width), FULL),
            pltpu.VMEM((width, size), FULL),
            pltpu.SemaphoreType.DMA((2, 3)),
        ],
        8 * line * rows * width * size,
        8 * line * rows * width + 16 * width * size,
        after=after,
    )(ids, *map(in_hbm, (xs, ys, hidden_in, hidden_out)))


def feed_scatter(pieces, line):
    outer_keep, outer_send, inner_keep, inner_send = pieces
    row, col = lax.axis_index("row"), lax.axis_index("col")
    outer_half, inner_half = yield [swap(outer_send, "col"), swap(inner_send, "row")]
    outer_other, inner_other = yield [
        swap(pick(outer_keep, 1 - row) + pick(outer_half, 1 - row), "row"),
        swap(pick(inner_keep, 1 - col) + pick(inner_half, 1 - col), "col"),
    ]
    outer = pick(outer_keep, row) + pick(outer_half, row) + outer_other
    inner = pick(inner_keep, col) + pick(inner_half, col) + inner_other
    place = lax.axis_index("line")
    far = yield [shift(pick(inner, (place + by) % line), line, by) for by in range(1, line)]
    slots = [pick(inner, place), *far]
    turned = jnp.stack([slots[-i % line] for i in range(line)] * 2)
    return lax.dynamic_slice_in_dim(turned, (line - place) % line, line, 0), outer


def piece_rows(own, line):
    padded = -(-own // line // 8) * 8
    return 3 * padded, padded


def attention_gradients_kernel(layer, heads, line, ids, kinds, *refs):
    parts = 2 * GROUP - 1
    sources = refs[:parts], refs[parts : 2 * parts]
    token_hbm, out_hbm, image_hbm, wide_ref, small_ref = refs[2 * parts : 2 * parts + 5]
    refs = refs[2 * parts + 5 :]
    token_out, table_out, images_out = refs[:3]
    (images, low_x, low_y, joined, attended_low, rows, bias, steps, attended) = refs[3:12]
    wide_sum, small_sum, stage, token, outer, scores, image_all, sems, weight_sems = refs[12:]
    slot = pl.program_id(0)
    kind = kinds[slot]
    count = low_x.shape[1]
    half = count // 2
    own = images.shape[2]
    at = 2 * ids[AT_COL] + ids[AT_ROW]

    def fetch(near):
        if near == 0:
            return [
                pltpu.make_async_copy(sources[side][0], stage.at[side, 0], sems.at[side, 0])
                for side in range(2)
            ]
        return [
            pltpu.make_async_copy(
                sources[side][(far + 1) * (GROUP - 1) + near - GROUP + 1],
                stage.at[side, near, pl.ds(pl.multiple_of(place * half, half), half)],
                sems.at[side, 2 * near + far - 1],
            )
            for side in range(2)
            for far, place in enumerate((ids[AT_CORE], 1 - ids[AT_CORE]))
        ]

    mine = pl.ds(pl.multiple_of(at * own, 16), own)
    weights = [
        pltpu.make_async_copy(token_hbm.at[layer, :, mine, :], token, weight_sems.at[0]),
        pltpu.make_async_copy(out_hbm.at[layer, mine, :], outer, weight_sems.at[1]),
        pltpu.make_async_copy(image_hbm.at[layer], image_all, weight_sems.at[2]),
    ]

    @pl.when(slot == 0)
    def _():
        for copy in (*fetch(0), *weights):
            copy.start()
        for near in range(1, GROUP):
            for copy in fetch(near):
                copy.start()
        wide_sum[...] = jnp.zeros_like(wide_sum)
        small_sum[...] = jnp.zeros_like(small_sum)
    for near in range(GROUP):

        @pl.when(slot == near)
        def _(near=near):
            for copy in fetch(near):
                copy.wait()

    @pl.when(slot == 0)
    def _():
        for copy in weights:
            copy.wait()
        for j in range(GROUP):

            @pl.when(at == j)
            def _(j=j):
                for member in range(2):
                    images[member] = image_all[member, :, j * own : (j + 1) * own]

    fill_bias(heads, kind, wide_ref, small_ref, bias)
    low_x[slot] = stage[0, slot].astype(LOW)
    low_y[slot] = stage[1, slot].astype(LOW)
    for member in range(3):
        projected = matmul(low_x[slot], token[member], NT)
        for i in range(IMAGES):
            here = slice(i * (count // IMAGES), (i + 1) * (count // IMAGES))
            if member == 1:
                rows[member, here, :] = projected[here].astype(LOW)
            else:
                near = images[member // 2]
                first = near[0:1, :]
                mine = near[i : i + 1, :]
                for other in range(1, GROUP):
                    begin = other * IMAGES
                    first = jnp.where(slot == other, near[begin : begin + 1, :], first)
                    mine = jnp.where(slot == other, near[begin + i : begin + i + 1, :], mine)
                mine = jnp.where(kind != 0, mine, first)
                rows[member, here, :] = (projected[here] + mine).astype(LOW)
    rows[3] = matmul(low_y[slot], outer[...], NT).astype(LOW)

    def row(index, first, last):
        return rows[index, :, first:last]

    attention_backward(heads, row, bias, steps, attended, scores)
    collect_table(heads, kind, scores, wide_sum, small_sum)
    attended_low[slot] = attended[...].astype(LOW)
    for member in range(3):
        rounded = steps[member].astype(LOW)
        joined[slot, :, member * own : (member + 1) * own] = rounded
        if member != 1:
            sums = [
                jnp.sum(
                    rounded[i * (count // IMAGES) : (i + 1) * (count // IMAGES)].astype(FULL),
                    axis=0,
                    keepdims=True,
                )
                for i in range(IMAGES)
            ]
            everything = sums[0] + sums[1] + sums[2] + sums[3]
            for i in range(IMAGES):
                alone = everything if i == 0 else jnp.zeros_like(everything)
                images_out[0, member // 2, i : i + 1, :] = jnp.where(kind != 0, sums[i], alone)

    @pl.when(slot == GROUP - 1)
    def _():
        flat = GROUP * count
        width = low_x.shape[2]

        chunk, piece = width // line, own // line
        rest, padded = piece_rows(own, line)
        product = matmul(low_x[...].reshape(flat, width), joined[...].reshape(flat, -1), TN)
        projection = matmul(
            attended_low[...].reshape(flat, -1), low_y[...].reshape(flat, -1), TN
        )
        size = width // 3
        for z in range(line):
            begin = z * (chunk + rest)
            token_out[begin : begin + chunk, :] = product[z * chunk : (z + 1) * chunk]
            for third in range(3):
                at_row = begin + chunk + third * padded
                token_out[at_row : at_row + padded, :] = jnp.zeros((padded, 3 * own), FULL)
                token_out[at_row : at_row + piece, :size] = projection[
                    z * piece : (z + 1) * piece, third * size : (third + 1) * size
                ]
        for head in range(heads):
            table_out[head : head + 1, :] = fold_table(wide_sum[head], small_sum[head])


def attention_gradients(layer, line, ids, kinds, near_x, near_y, token_rows, per_image, out_proj, wide, small, after=()):
    count, width = near_x[0].shape
    depth, _, local, _ = token_rows.shape
    own, heads = local // GROUP, wide.shape[0] // depth // GROUP
    near = [pl.BlockSpec(memory_space=pl.ANY)] * (len(near_x) + len(near_y))

    def own_heads(slot, ids, kinds):
        return (layer * GROUP + 2 * ids[AT_COL] + ids[AT_ROW], 0, 0)

    outs = [
        shape_of((width + line * piece_rows(own, line)[0], 3 * own)),
        shape_of((heads, 4 * SPAN)),
        shape_of((GROUP, 2, IMAGES, own)),
    ]
    return call(
        functools.partial(attention_gradients_kernel, layer, heads, line),
        f"attention_gradients_{layer}",
        (GROUP,),
        [
            *near,
            pl.BlockSpec(memory_space=pltpu.HBM),
            pl.BlockSpec(memory_space=pltpu.HBM),
            pl.BlockSpec(memory_space=pltpu.HBM),
            pl.BlockSpec((heads, *wide.shape[1:]), own_heads),
            pl.BlockSpec((heads, *small.shape[1:]), own_heads),
        ],
        [
            *[whole_once(out.shape) for out in outs[:2]],
            pl.BlockSpec((1, 2, IMAGES, own), lambda s, ids, kinds: (s, 0, 0, 0)),
        ],
        outs,
        [
            pltpu.VMEM((2, GROUP * IMAGES, own), FULL),
            pltpu.VMEM((GROUP, count, width), LOW),
            pltpu.VMEM((GROUP, count, width), LOW),
            pltpu.VMEM((GROUP, count, 3 * own), LOW),
            pltpu.VMEM((GROUP, count, own), LOW),
            pltpu.VMEM((4, count, own), LOW),
            pltpu.VMEM((heads, count, count), FULL),
            pltpu.VMEM((3, count, own), FULL),
            pltpu.VMEM((count, own), FULL),
            pltpu.VMEM((heads, *wide.shape[1:]), FULL),
            pltpu.VMEM((heads, *small.shape[1:]), FULL),
            pltpu.VMEM((2, GROUP, count, width), FULL),
            pltpu.VMEM((3, own, width), LOW),
            pltpu.VMEM((own, width), LOW),
            pltpu.VMEM((heads, count, count), FULL),
            pltpu.VMEM(per_image.shape[1:], FULL),
            pltpu.SemaphoreType.DMA((2, 2 * GROUP)),
            pltpu.SemaphoreType.DMA((3,)),
        ],
        2 * GROUP * count * width * own * 8 + GROUP * heads * count * count * 4096,
        8 * GROUP * count * width + 8 * width * local,
        2,
        after,
    )(
        ids, kinds, *map(in_hbm, (*near_x, *near_y, token_rows, out_proj, per_image)), wide, small
    )


def swap(value, axis):
    return lax.ppermute(value, axis, [(0, 1), (1, 0)])


def shift(value, line, by=1):
    return lax.ppermute(value, "line", [(i, (i + by) % line) for i in range(line)])


def pick(value, index, axis=0):
    return lax.dynamic_index_in_dim(value, index, axis, keepdims=False)


def gather_line(half):
    return lax.all_gather(half, ("line", "tensor"), tiled=True)


def plane_steps(value, half):
    across, along = yield [swap(half, "row"), swap(half, "col")]
    (corner,) = yield [swap_corner(half)]
    others = yield [swap(part, "tensor") for part in (across, along, corner)]
    return [value, across, along, corner, *others]


def swap_corner(value):
    return lax.ppermute(value, ("col", "row"), [(0, 3), (3, 0), (1, 2), (2, 1)])


def scatter_line(value, line):
    place = lax.axis_index("line")
    far = yield [shift(pick(value, (place + by) % line), line, by) for by in range(1, line)]
    return functools.reduce(jnp.add, far, pick(value, place))


def scatter_vectors(value, line):
    row, col = lax.axis_index("row"), lax.axis_index("col")
    (other,) = yield [swap(pick(value, 1 - row, 2), "row")]
    value = pick(value, row, 2) + other
    (other,) = yield [swap(pick(value, 1 - col, 1), "col")]
    return (yield from scatter_line(pick(value, col, 1) + other, line))


def scatter_table(value, line):
    return exchange_plane((yield from scatter_line(value, line)))


def line_steps(value, line):
    far = yield [shift(value, line, by) for by in range(1, line)]
    return jnp.concatenate([value, *far])


def exchange_plane(value):
    col, row = lax.axis_index("col"), lax.axis_index("row")
    place = 2 * col + row
    across = swap(pick(value, place ^ 1), "row")
    along = swap(pick(value, place ^ 2), "col")
    corner = swap_corner(pick(value, place ^ 3))
    slots = [pick(value, place), across, along, corner]
    slots = [jnp.where(row == 0, slots[i], slots[i ^ 1]) for i in range(4)]
    return jnp.stack([jnp.where(col == 0, slots[i], slots[i ^ 2]) for i in range(4)])


def local(
    tokens,
    segment_ids,
    timesteps,
    norm_gain,
    norm_bias,
    token_proj,
    time_proj,
    bias_table,
    out_proj,
    hidden_in,
    hidden_out,
    branch_bias,
    cotangent,
    *,
    line,
):
    count, width = tokens.shape
    depth, _, _, local_width = token_proj.shape
    heads = bias_table.shape[1]
    units = hidden_in.shape[2]
    own = local_width // GROUP
    n_dp = GROUP * line
    features = width // n_dp
    line_at = lax.axis_index("line")
    place = 2 * lax.axis_index("col") + lax.axis_index("row")
    ids = jnp.stack(
        [segment_ids[-1], line_at, lax.axis_index("col"), lax.axis_index("row"), lax.axis_index("tensor")]
    ).astype(jnp.int32)
    embedded = sinusoid(timesteps[0], jnp.arange(width, dtype=jnp.int32), width)
    per_image = lax.dot_general(
        time_proj, embedded, (((2,), (1,)), ((), ())), preferred_element_type=FULL
    )
    per_image = jnp.swapaxes(per_image, 2, 3)
    info = jnp.concatenate([timesteps[0], segment_ids[-1:]]).astype(FULL)
    packed = jnp.concatenate(
        [
            per_image.reshape(2 * depth * IMAGES, local_width),
            jnp.pad(info[None], ((0, 7), (0, local_width - IMAGES - 1))),
        ]
    )
    packed = jnp.stack([packed, swap(packed, "row"), swap(packed, "col"), swap_corner(packed)])
    near_image = packed[:, : 2 * depth * IMAGES].reshape(GROUP, depth, 2, IMAGES, local_width)
    near_image = jnp.moveaxis(near_image, 0, 2).reshape(depth, 2, GROUP * IMAGES, local_width)
    near = packed[:, 2 * depth * IMAGES, : IMAGES + 1]
    kinds = near[:, IMAGES].astype(jnp.int32)
    near = jnp.pad(near, ((0, 4), (0, 123 - IMAGES + 4)))
    every = jnp.concatenate([near] + [shift(near, line, by) for by in range(1, line)])
    every = every.reshape(line, 8, -1)[:, :GROUP, :IMAGES]
    own_feature = line_at * (GROUP * features) + jnp.arange(GROUP * features, dtype=jnp.int32)
    embedded_every = sinusoid(every.reshape(-1), own_feature, width).astype(FULL)
    token_rows = jnp.swapaxes(token_proj, 2, 3)
    wide, small = expand_table(bias_table.reshape(depth * heads, -1))

    stream = (tokens,)
    saved = []
    moves = Moves()
    half = lax.dynamic_slice_in_dim(cotangent, lax.axis_index("tensor") * (count // 2), count // 2, 0)
    gathered_up = gather_line(half.astype(FULL))
    for layer in range(depth):
        held, normed, half, rows, partial, bias = attend(
            layer, ids, stream, norm_gain, norm_bias, branch_bias, token_rows, per_image, out_proj, wide, small
        )
        if layer == depth - 1:
            partial, gathered_up = moves.kernel(partial, [gathered_up])
        else:
            (partial,) = moves.kernel(partial)
        moves.start(("first", layer), plane_steps(normed, half))
        middle, half_second, slope, partial = feed(
            layer,
            ids,
            held,
            partial,
            swap(partial, "tensor"),
            branch_bias,
            norm_gain,
            norm_bias,
            hidden_in,
            hidden_out,
        )
        (partial,) = moves.kernel(partial)
        line_second = gather_line(half_second)
        saved.append((held, rows, middle, slope, line_second, bias))
        stream = (middle, partial, swap(partial, "tensor"))
    output = (stream[0] + (stream[1] + stream[2]) + branch_bias[depth - 1, 1]).astype(LOW)

    upstream = (cotangent,)
    collected = [None] * depth
    vectors = [None] * depth
    gathered = [None] * depth
    gathered_line = [None] * depth
    for layer in reversed(range(depth)):
        held, rows, middle, slope, _, bias = saved[layer]
        current, half_up, feed_sums, partial = feed_back(
            layer, ids, upstream, slope, hidden_in, hidden_out, norm_gain
        )
        (partial,) = moves.kernel(partial)
        if layer < depth - 1:
            gathered_up = gather_line(half_up)
        back_middle, half, middle_sums, back_partial = attend_back(
            layer,
            ids,
            current,
            partial,
            swap(partial, "tensor"),
            middle,
            norm_gain,
            rows,
            bias,
            out_proj,
            token_rows,
        )
        other = depth - 1 - layer
        back_partial, gathered_line[other] = moves.kernel(back_partial, [saved[other][4]])
        moves.start(("branch", layer), plane_steps(back_middle, half))
        upstream = (back_middle, back_partial, swap(back_partial, "tensor"), held)
        vectors[layer] = (feed_sums, middle_sums)
        gathered[layer] = gathered_up
    gradient_tokens, last_sums = finish(*upstream, norm_gain)
    (last_sums,) = moves.kernel(last_sums)
    firsts = [last_sums] + [vectors[layer][0] for layer in range(depth - 1)]
    rows = jnp.stack(
        [
            jnp.stack([jnp.stack([firsts[l][1], vectors[l][1][1]]) for l in range(depth)]),
            jnp.stack([jnp.stack([firsts[l][2], vectors[l][1][2]]) for l in range(depth)]),
            jnp.stack([jnp.stack([vectors[l][1][0], vectors[l][0][0]]) for l in range(depth)]),
        ]
    )
    rows = jnp.moveaxis(rows.reshape(6 * depth, line, 2, 2, features), 0, 3)
    moves.start("rows", scatter_vectors(rows, line))

    turn = last_sums
    tokens_of = {}

    def run_feed(layer, turn):
        pieces = feed_gradients(
            layer, line, ids, gathered_line[layer], gathered[layer], hidden_in, hidden_out, after=(turn,)
        )
        (turn,) = moves.kernel(pieces[0])
        moves.start(("feed", layer), feed_scatter((turn, *pieces[1:]), line))
        return turn

    def run_attention(layer, turn):
        token, table, images = attention_gradients(
            layer,
            line,
            ids,
            kinds,
            moves.found["first", layer],
            moves.found["branch", layer],
            token_rows,
            near_image,
            out_proj,
            wide,
            small,
            after=(turn,),
        )
        turn, gathered[0] = moves.kernel(table, [gathered[0]])
        tokens_of[layer] = lax.psum_scatter(token, "line", scatter_dimension=0, tiled=True)
        table = turn.reshape(-1, line, GROUP, 4 * SPAN // n_dp)
        moves.start(("table", layer), scatter_table(jnp.moveaxis(table, 0, 2), line))
        moves.start(("images", layer), line_steps(images, line))
        return turn

    for layer in reversed(range(1, depth)):
        turn = run_feed(layer, run_attention(layer, turn))
    run_feed(0, run_attention(0, turn))
    moves.finish()

    for layer in reversed(range(depth)):
        inner, outer = moves.found["feed", layer]
        offsets = line_window(units, line)[1]
        inner = jnp.concatenate(
            [inner[z, :, offsets[z] : offsets[z] + units // line] for z in range(line)], axis=1
        )
        token, images = tokens_of[layer], moves.found["images", layer]
        chunk, padded = GROUP * features, piece_rows(own, line)[1]
        thirds = [
            token[chunk + third * padded : chunk + third * padded + own // line, : width // 3]
            for third in range(3)
        ]
        projection = jnp.concatenate(thirds, axis=1)
        token = token[:chunk]
        projection = lax.ppermute(
            projection,
            LINES,
            [(GROUP * z + j, line * j + z) for z in range(line) for j in range(GROUP)],
        )
        time = jnp.einsum(
            "rif,rmic->fmc",
            embedded_every.reshape(n_dp, IMAGES, GROUP * features),
            images,
            precision=lax.Precision.HIGHEST,
        )
        joined = jnp.concatenate([token, time.reshape(GROUP * features, 2 * own)], axis=1)
        joined = exchange_plane(joined.reshape(GROUP, features, 5 * own))
        joined = joined.reshape(GROUP, features, 5, own).transpose(2, 1, 0, 3)
        joined = joined.reshape(5, features, local_width)
        collected[layer] = (joined[:3], joined[3:], projection, inner, outer)
    rows = moves.found["rows"].reshape(3, depth, 2, features)
    table = jnp.stack([moves.found["table", layer].reshape(heads, -1) for layer in range(depth)])
    stacked = [jnp.stack([terms[member] for terms in collected]) for member in range(5)]
    token, time, projection, inner, outer = stacked
    return (
        output,
        gradient_tokens,
        rows[0],
        rows[1],
        token,
        time,
        table,
        projection,
        inner,
        outer,
        rows[2],
    )


def solution(mesh):
    line = mesh.shape["dp"] // GROUP
    fine = Mesh(mesh.devices.reshape(line, 2, 2, mesh.shape["tensor"]), (*LINES, "tensor"))
    return jax.shard_map(
        functools.partial(local, line=line),
        mesh=fine,
        in_specs=(
            P(LINES, None),
            P(LINES),
            P(LINES, None),
            P(),
            P(),
            P(None, None, None, "tensor"),
            P(None, None, None, "tensor"),
            P(None, "tensor", None),
            P(None, "tensor", None),
            P(None, None, "tensor"),
            P(None, "tensor", None),
            P(),
            P(LINES, None),
        ),
        out_specs=(
            P(LINES, None),
            P(LINES, None),
            P(None, None, LINES),
            P(None, None, LINES),
            P(None, None, LINES, "tensor"),
            P(None, None, LINES, "tensor"),
            P(None, "tensor", LINES),
            P(None, ("tensor", *LINES), None),
            P(None, LINES, "tensor"),
            P(None, ("tensor", *LINES), None),
            P(None, None, LINES),
        ),
        check_vma=False,
    )
```

time: 2230 us -> 518 us (0.23)
  waiting for transfers between devices: 1550 us -> 148 us
  matrix products: 371 us -> 8.81 us
  Pallas kernels: 0 us -> 160 us
  local copies, waits for them, and re-layouts: 147 us -> 47.6 us
  starting transfers between devices: 1.29 us -> 97.9 us
  blocking collectives: 73.4 us -> 0 us
  other arithmetic: 62.8 us -> 33.5 us
    unnamed x15 -> x6, waiting for transfers between devices: 857 us -> 0.1 us
    reduce_scatter x2, waiting for transfers between devices: 634 us -> 0.01 us  [run_attention(): lax.psum_scatter(token, 'line', scatter_dimension=0, tiled=True)]
    dot_general x56 -> x3, matrix products: 371 us -> 8.81 us  [the longest x1 4.78 us: local(): lax.dot_general(time_proj, embedded, (((2,), (1,)), ((), ())), preferred_...]
    pallas_call x0 -> x27, Pallas kernels: none -> 160 us  [the longest x9 83.9 us: plain(): pl.pallas_call(body, in_specs=[*[pl.BlockSpec(memory_space=pltpu.SMEM)] *...]
    ppermute x0 -> x83, waiting for transfers between devices: none -> 148 us  [the longest x48 104 us: swap(): return lax.ppermute(value, axis, [(0, 1), (1, 0)])]
    another operation x23 -> x14, local copies, waits for them, and re-layouts: 116 us -> 4.31 us  [the longest x4 2.52 us: local(): jnp.stack([terms[member] for terms in collected])]
    ppermute x0 -> x83, starting transfers between devices: none -> 97.4 us  [the longest x24 37.8 us: shift(): lax.ppermute(value, 'line', [(i, (i + by) % line) for i in range(line)])]
    unnamed x1 -> x0, blocking collectives: 73.4 us -> none
  transfers between devices with their start and end apart: 12 -> 89, of which waited for: 7 -> 36; matrix products, arithmetic and copies ran while one was open for 13% -> 12% of each run, Pallas kernels for 0% -> 31%
where the time goes in v2:
time: 518 us; the launch traced here: 512 us
  Pallas kernels  160 us (31%)
  waiting for transfers between devices  148 us (29%)
  starting transfers between devices  97.9 us (19%)
  local copies, waits for them, and re-layouts  47.6 us (9%)
  other arithmetic  33.5 us (6%)
  between operations  15.9 us (3%)
  matrix products  8.81 us (2%)
    ppermute x48, waiting for transfers between devices, swap(): return lax.ppermute(value, axis, [(0, 1), (1, 0)])  104 us
    pallas_call x9, Pallas kernels, plain(): pl.pallas_call(body, in_specs=[*[pl.BlockSpec(memory_space=pltpu.SMEM)] *...  83.9 us
    pallas_call x4, Pallas kernels, call(): return lambda *operands: made(*operands, *map(in_hbm, after))  71.8 us
    ppermute x24, starting transfers between devices, shift(): lax.ppermute(value, 'line', [(i, (i + by) % line) for i in range(line)])  37.8 us
    ppermute x48, starting transfers between devices, swap(): return lax.ppermute(value, axis, [(0, 1), (1, 0)])  35.1 us
    ppermute x24, waiting for transfers between devices, shift(): lax.ppermute(value, 'line', [(i, (i + by) % line) for i in range(line)])  25.8 us
    unnamed x172, local copies, waits for them, and re-layouts  20.9 us
    ppermute x9, waiting for transfers between devices, swap_corner(): return lax.ppermute(value, ('col', 'row'), [(0, 3), (3, 0), (1, 2), (2, 1)])  18.3 us
  transfers between devices with their start and end apart: 89, of which 36 were waited for; matrix products, arithmetic and copies ran while one was open for 12% of the time, Pallas kernels for 31%

profile of v2, /device:TPU:2, one launch (start us, length us, event | category | flops | bytes accessed | tf_op | source)
XLA Modules:
  0.0 512.0 jit_solution(2467282375824985752)
XLA Ops:
  9.7 4.3 expand_table.1
  14.9 4.8 convolution_bitcast_fusion.2.refs_7_.refs_9_
  19.7 8.3 %attend_0.1 = (f32[256,1152]{1,0:T(8,128)}, f32[256,1152]{1,0:T(8,128)}, f32[128,1152]{1,0:T(8,128)}, bf16[3,256,576]{2,1,0:T(8,128)(2,1)}, f32[256,1152]{1,0:T(8,128)}, /*index=5*/f32[8,256,256]{2,1,0:T(8,128)}) custom-call(s32[5]{0:T(128)S(1)} %stack.233.refs_0_, f32[2,2,1152]{2,1,0:T(2,128)S(1)} %copy-done.1, f32[2,2,1152]{2,1,0:T(2,128)S(1)} %copy-done.4, ...), custom_call_target="tpu_custom_call" | custom-call | flops 2432696320 | bytes 10027008 | tf_op jit(solution)/shard_map/attend_0/pallas_call | solution.py:294
  32.3 9.6 %feed_0.1 = (f32[256,1152]{1,0:T(8,128)}, f32[128,1152]{1,0:T(8,128)}, f32[256,2304]{1,0:T(8,128)}, f32[256,1152]{1,0:T(8,128)}) custom-call(s32[5]{0:T(128)S(1)} %stack.233.refs_0_, f32[2,2,1152]{2,1,0:T(2,128)S(1)} %copy-done.1, f32[2,2,1152]{2,1,0:T(2,128)S(1)} %copy-done.4, f32[2,2,1152]{2,1,0:T(2,128)S(1)} %copy-done.3, ...), custom_call_target="tpu_custom_call" | custom-call | flops 2717908992 | bytes 20054016 | tf_op jit(solution)/shard_map/feed_0/pallas_call | solution.py:294
  43.9 13.6 %collective-permute-done.1.refs_1_ = f32[128,1152]{1,0:T(8,128)} collective-permute-done((f32[128,1152]{1,0:T(8,128)S(1)}, f32[128,1152]{1,0:T(8,128)}, u32[]{:S(2)}, u32[]{:S(2)}) %collective-permute-start.1) | collective-permute-done | bytes 589856 | tf_op jit(solution)/shard_map/ppermute | solution.py:1070
  62.3 9.6 %attend_1.1 = (f32[256,1152]{1,0:T(8,128)}, f32[256,1152]{1,0:T(8,128)}, f32[128,1152]{1,0:T(8,128)}, bf16[3,256,576]{2,1,0:T(8,128)(2,1)}, f32[256,1152]{1,0:T(8,128)}, /*index=5*/f32[8,256,256]{2,1,0:T(8,128)}) custom-call(s32[5]{0:T(128)S(1)} %stack.233.refs_0_, f32[2,2,1152]{2,1,0:T(2,128)S(1)} %copy-done.1, f32[2,2,1152]{2,1,0:T(2,128)S(1)} %copy-done.4, ...), custom_call_target="tpu_custom_call" | custom-call | flops 2432696320 | bytes 10027008 | tf_op jit(solution)/shard_map/attend_1/pallas_call | solution.py:294
  79.8 9.6 %feed_1.1 = (f32[256,1152]{1,0:T(8,128)}, f32[128,1152]{1,0:T(8,128)}, f32[256,2304]{1,0:T(8,128)}, f32[256,1152]{1,0:T(8,128)}) custom-call(s32[5]{0:T(128)S(1)} %stack.233.refs_0_, f32[2,2,1152]{2,1,0:T(2,128)S(1)} %copy-done.1, f32[2,2,1152]{2,1,0:T(2,128)S(1)} %copy-done.4, f32[2,2,1152]{2,1,0:T(2,128)S(1)} %copy-done.3, ...), custom_call_target="tpu_custom_call" | custom-call | flops 2717908992 | bytes 20054016 | tf_op jit(solution)/shard_map/feed_1/pallas_call | solution.py:294
  92.3 9.0 %feed_back_1.1 = (f32[256,1152]{1,0:T(8,128)}, f32[128,1152]{1,0:T(8,128)}, f32[8,1152]{1,0:T(8,128)}, f32[256,1152]{1,0:T(8,128)}) custom-call(s32[5]{0:T(128)S(1)} %stack.233.refs_0_, f32[2,2,1152]{2,1,0:T(2,128)S(1)} %copy-done.1, bf16[256,1152]{1,0:T(8,128)(2,1)} %refs_2_.9, f32[256,2304]{1,0:T(8,128)} %get-tuple-element.144.refs_3_, ...), custom_call_target="tpu_custom_call" | custom-call | flops 2717908992 | bytes 20054016 | tf_op jit(solution)/shard_map/feed_back_1/pallas_call | solution.py:294
  101.2 4.7 collective-permute-done.12.refs_1_
  110.6 12.0 %collective-permute-done.9.refs_4_ = f32[128,1152]{1,0:T(8,128)S(1)} collective-permute-done((f32[128,1152]{1,0:T(8,128)S(1)}, f32[128,1152]{1,0:T(8,128)S(1)}, u32[]{:S(2)}, u32[]{:S(2)}) %collective-permute-start.9) | collective-permute-done | bytes 589856 | tf_op jit(solution)/shard_map/ppermute | solution.py:1070
  126.7 11.4 %attend_back_1.1 = (f32[256,1152]{1,0:T(8,128)}, f32[128,1152]{1,0:T(8,128)}, f32[8,1152]{1,0:T(8,128)}, f32[256,1152]{1,0:T(8,128)}) custom-call(s32[5]{0:T(128)S(1)} %stack.233.refs_0_, f32[2,2,1152]{2,1,0:T(2,128)S(1)} %copy-done.1, f32[256,1152]{1,0:T(8,128)} %get-tuple-element.145.refs_2_, f32[256,1152]{1,0:T(8,128)} %get-tuple-element.147.refs_3_, ...), custom_call_target="tpu_custom_call" | custom-call | flops 3506438144 | bytes 12386304 | tf_op jit(solution)/shard_map/attend_back_1/pallas_call | solution.py:294
  143.7 10.3 %feed_back_0.1 = (f32[256,1152]{1,0:T(8,128)}, f32[128,1152]{1,0:T(8,128)}, f32[8,1152]{1,0:T(8,128)}, f32[256,1152]{1,0:T(8,128)}) custom-call(s32[5]{0:T(128)S(1)} %stack.233.refs_0_, f32[2,2,1152]{2,1,0:T(2,128)S(1)} %copy-done.1, f32[256,1152]{1,0:T(8,128)} %get-tuple-element.150.refs_2_.refs_9_, f32[256,1152]{1,0:T(8,128)} %get-tuple-element.156.refs_3_, ...), custom_call_target="tpu_custom_call" | custom-call | flops 2717908992 | bytes 20054016 | tf_op jit(solution)/shard_map/feed_back_0/pallas_call | solution.py:294
  156.2 13.8 %collective-permute-done.18.refs_1_ = f32[128,1152]{1,0:T(8,128)} collective-permute-done((f32[128,1152]{1,0:T(8,128)S(1)}, f32[128,1152]{1,0:T(8,128)}, u32[]{:S(2)}, u32[]{:S(2)}) %collective-permute-start.18) | collective-permute-done | bytes 589856 | tf_op jit(solution)/shard_map/ppermute | solution.py:1070
  174.2 11.7 %attend_back_0.1 = (f32[256,1152]{1,0:T(8,128)}, f32[128,1152]{1,0:T(8,128)}, f32[8,1152]{1,0:T(8,128)}, f32[256,1152]{1,0:T(8,128)}) custom-call(s32[5]{0:T(128)S(1)} %stack.233.refs_0_, f32[2,2,1152]{2,1,0:T(2,128)S(1)} %copy-done.1, f32[256,1152]{1,0:T(8,128)} %get-tuple-element.158.refs_2_, f32[256,1152]{1,0:T(8,128)} %get-tuple-element.161.refs_3_, ...), custom_call_target="tpu_custom_call" | custom-call | flops 3506438144 | bytes 12386304 | tf_op jit(solution)/shard_map/attend_back_0/pallas_call | solution.py:294
  197.4 3.6 collective-permute-start.50
  211.3 4.3 finish.1
  220.7 18.1 %attention_gradients_1.1 = (f32[1632,432]{1,0:T(8,128)}, f32[2,1024]{1,0:T(2,128)}, f32[4,2,4,144]{3,2,1,0:T(4,128)}) custom-call(s32[5]{0:T(128)S(1)} %stack.233.refs_0_, s32[4]{0:T(128)S(1)} %convert_reduce_fusion.refs_1_, f32[256,1152]{1,0:T(8,128)} %get-tuple-element.179.refs_2_, f32[128,1152]{1,0:T(8,128)} %get-tuple-element.153.refs_3_, ...), custom_call_target="tpu_custom_call" | custom-call | flops 4865392640 | bytes 14745600 | tf_op jit(solution)/shard_map/attention_gradients_1/pallas_call | solution.py:93
  249.7 5.8 %collective-permute-done.31.refs_2_ = f32[128,1152]{1,0:T(8,128)} collective-permute-done((f32[128,1152]{1,0:T(8,128)}, f32[128,1152]{1,0:T(8,128)}, u32[]{:S(2)}, u32[]{:S(2)}) %collective-permute-start.31) | collective-permute-done | bytes 589856 | tf_op jit(solution)/shard_map/ppermute | solution.py:1093
  257.3 3.6 collective-permute-start.42
  270.7 17.8 %feed_gradients_1.1 = (f32[2,144,1152]{2,1,0:T(8,128)}, f32[2,144,1152]{2,1,0:T(8,128)}, f32[2,4,72,640]{3,2,1,0:T(8,128)}, f32[2,4,72,640]{3,2,1,0:T(8,128)}) custom-call(s32[5]{0:T(128)S(1)} %stack.233.refs_0_, f32[1024,1152]{1,0:T(8,128)} %get-tuple-element.189.refs_1_, f32[1024,1152]{1,0:T(8,128)} %get-tuple-element.190.refs_2_, ...), custom_call_target="tpu_custom_call" | custom-call | flops 6039797760 | bytes 21233664 | tf_op jit(solution)/shard_map/feed_gradients_1/pallas_call | solution.py:93
  297.4 18.2 %attention_gradients_0.1 = (f32[1632,432]{1,0:T(8,128)}, f32[2,1024]{1,0:T(2,128)}, f32[4,2,4,144]{3,2,1,0:T(4,128)}) custom-call(s32[5]{0:T(128)S(1)} %stack.233.refs_0_, s32[4]{0:T(128)S(1)} %convert_reduce_fusion.refs_1_, f32[256,1152]{1,0:T(8,128)} %get-tuple-element.198.refs_2_, f32[128,1152]{1,0:T(8,128)} %get-tuple-element.139.refs_3_, ...), custom_call_target="tpu_custom_call" | custom-call | flops 4865392640 | bytes 14745600 | tf_op jit(solution)/shard_map/attention_gradients_0/pallas_call | solution.py:93
  340.2 17.8 %feed_gradients_0.1 = (f32[2,144,1152]{2,1,0:T(8,128)}, f32[2,144,1152]{2,1,0:T(8,128)}, f32[2,4,72,640]{3,2,1,0:T(8,128)}, f32[2,4,72,640]{3,2,1,0:T(8,128)}) custom-call(s32[5]{0:T(128)S(1)} %stack.233.refs_0_, f32[1024,1152]{1,0:T(8,128)} %get-tuple-element.215.refs_1_, f32[1024,1152]{1,0:T(8,128)} %get-tuple-element.216.refs_2_, ...), custom_call_target="tpu_custom_call" | custom-call | flops 6039797760 | bytes 21233664 | tf_op jit(solution)/shard_map/feed_gradients_0/pallas_call | solution.py:93
  381.3 11.1 %collective-permute-done.66 = f32[2,64]{1,0:T(2,128)S(1)} collective-permute-done((f32[2,64]{1,0:T(2,128)S(1)}, f32[2,64]{1,0:T(2,128)S(1)}, u32[]{:S(2)}, u32[]{:S(2)}) %collective-permute-start.66) | collective-permute-done | bytes 544 | tf_op jit(solution)/shard_map/ppermute | solution.py:1070
  399.7 6.5 %collective-permute-done.79 = f32[72,640]{1,0:T(8,128)S(1)} collective-permute-done((f32[72,640]{1,0:T(8,128)S(1)}, f32[72,640]{1,0:T(8,128)S(1)}, u32[]{:S(2)}, u32[]{:S(2)}) %collective-permute-start.79) | collective-permute-done | bytes 184352 | tf_op jit(solution)/shard_map/ppermute | solution.py:1074
  414.3 9.1 %collective-permute-done.82 = f32[144,1152]{1,0:T(8,128)} collective-permute-done((f32[144,1152]{1,0:T(8,128)}, f32[144,1152]{1,0:T(8,128)}, u32[]{:S(2)}, u32[]{:S(2)}) %collective-permute-start.82) | collective-permute-done | bytes 663584 | tf_op jit(solution)/shard_map/ppermute | solution.py:1070
  435.2 7.9 %collective-permute-done.76 = f32[72,640]{1,0:T(8,128)S(1)} collective-permute-done((f32[72,640]{1,0:T(8,128)S(1)}, f32[72,640]{1,0:T(8,128)S(1)}, u32[]{:S(2)}, u32[]{:S(2)}) %collective-permute-start.76) | collective-permute-done | bytes 184352 | tf_op jit(solution)/shard_map/ppermute | solution.py:1074
  453.9 4.5 collective-permute-done.63
  458.4 9.4 %collective-permute-done.62 = f32[72,720]{0,1:T(8,128)S(1)} collective-permute-done((f32[72,720]{0,1:T(8,128)}, f32[72,720]{0,1:T(8,128)S(1)}, u32[]{:S(2)}, u32[]{:S(2)}) %collective-permute-start.62) | collective-permute-done | bytes 207392 | tf_op jit(solution)/shard_map/ppermute | solution.py:1070
  471.6 8.9 %collective-permute-start.71 = (f32[36,1152]{1,0:T(8,128)S(1)}, f32[36,1152]{1,0:T(8,128)}, u32[]{:S(2)}, u32[]{:S(2)}) collective-permute-start(f32[36,1152]{1,0:T(8,128)S(1)} %pad_maximum_fusion.7), channel_id=1, source_target_pairs={{0,0},{2,8},{4,16},{6,24},{8,2},{10,10},{12,18},{14,26},{16,4},{18... | collective-permute-start | bytes 497672 | tf_op jit(solution)/shard_map/ppermute | solution.py:1313
  482.2 3.5 collective-permute-start.59
  487.8 6.7 %collective-permute-done.60 = f32[72,720]{0,1:T(8,128)S(1)} collective-permute-done((f32[72,720]{0,1:T(8,128)S(1)}, f32[72,720]{0,1:T(8,128)S(1)}, u32[]{:S(2)}, u32[]{:S(2)}) %collective-permute-start.60) | collective-permute-done | bytes 207392 | tf_op jit(solution)/shard_map/ppermute | solution.py:1070
  494.5 5.2 %collective-permute-done.59 = f32[72,720]{0,1:T(8,128)} collective-permute-done((f32[72,720]{0,1:T(8,128)}, f32[72,720]{0,1:T(8,128)}, u32[]{:S(2)}, u32[]{:S(2)}) %collective-permute-start.59) | collective-permute-done | bytes 207392 | tf_op jit(solution)/shard_map/ppermute | solution.py:1070
  (476 shorter events, 201.6 us)
Async XLA Ops:
  7.2 67.7 %all-gather.5.cloned.1.call-start = ((), (), s32[]{:S(2)}) async-start(), calls=%async_computation.2 | async-start | bytes 5308416 | tf_op jit(solution)/shard_map/all_gather | solution.py:1082
  9.1 129.0 %all-gather.7.cloned.1.call-start = ((), (), s32[]{:S(2)}) async-start(), calls=%async_computation.3 | async-start | bytes 5308416 | tf_op jit(solution)/shard_map/all_gather | solution.py:1082
  41.9 144.9 %all-gather.9.cloned.1.call-start = ((), (), s32[]{:S(2)}) async-start(), calls=%async_computation.4 | async-start | bytes 5308416 | tf_op jit(solution)/shard_map/all_gather | solution.py:1082
  89.4 171.5 %all-gather.11.cloned.1.call-start = ((), (), s32[]{:S(2)}) async-start(), calls=%async_computation.5 | async-start | bytes 5308416 | tf_op jit(solution)/shard_map/all_gather | solution.py:1082
  92.3 18.2 %collective-permute-start.6 = (f32[128,1152]{1,0:T(8,128)}, f32[128,1152]{1,0:T(8,128)S(1)}, u32[]{:S(2)}, u32[]{:S(2)}) collective-permute-start(f32[128,1152]{1,0:T(8,128)} %get-tuple-element.139.refs_3_), channel_id=1, source_target_pairs={{0,1},{1,0},{2,3},{3,2},{4,5},{5,4},{6,7},{7,6},{8,9},{9,8},{10,11... | collective-permute-start | bytes 1769480 | tf_op jit(solution)/shard_map/ppermute | solution.py:1070
  106.8 20.0 %collective-permute-start.13 = (f32[256,1152]{1,0:T(8,128)}, f32[256,1152]{1,0:T(8,128)}, u32[]{:S(2)}, u32[]{:S(2)}) collective-permute-start(f32[256,1152]{1,0:T(8,128)} %get-tuple-element.147.refs_3_), channel_id=1, source_target_pairs={{0,1},{1,0},{2,3},{3,2},{4,5},{5,4},{6,7},{7,6},{8,9},{9,8},{10,11... | collective-permute-start | bytes 3538952 | tf_op jit(solution)/shard_map/ppermute | solution.py:1070
  154.1 290.8 %reduce-scatter.5.cloned.1.call-start = ((), (), s32[]{:S(2)}) async-start(), calls=%async_computation.7 | async-start | bytes 4177920 | tf_op jit(solution)/shard_map/reduce_scatter | solution.py:1288
  187.6 19.9 %collective-permute-start.22 = (f32[256,1152]{1,0:T(8,128)}, f32[256,1152]{1,0:T(8,128)S(1)}, u32[]{:S(2)}, u32[]{:S(2)}) collective-permute-start(f32[256,1152]{1,0:T(8,128)} %get-tuple-element.167.refs_2_), channel_id=1, source_target_pairs={{0,1},{1,0},{2,3},{3,2},{4,5},{5,4},{6,7},{7,6},{8,9},{9,8},{10,11... | collective-permute-start | bytes 3538952 | tf_op jit(solution)/shard_map/ppermute | solution.py:1070
  215.7 30.2 %collective-permute-start.11 = (f32[256,1152]{1,0:T(8,128)S(1)}, f32[256,1152]{1,0:T(8,128)}, u32[]{:S(2)}, u32[]{:S(2)}) collective-permute-start(f32[256,1152]{1,0:T(8,128)S(1)} %copy-done.12), channel_id=1, source_target_pairs={{0,1},{1,0},{2,3},{3,2},{4,5},{5,4},{6,7},{7,6},{8,9},{9,8},{10,11... | collective-permute-start | bytes 3538952 | tf_op jit(solution)/shard_map/ppermute | solution.py:1070
  238.8 231.8 %reduce-scatter.3.cloned.1.call-start = ((), (), s32[]{:S(2)}) async-start(), calls=%async_computation.6 | async-start | bytes 4177920 | tf_op jit(solution)/shard_map/reduce_scatter | solution.py:1288
  245.3 22.8 %collective-permute-start.33 = (f32[128,1152]{1,0:T(8,128)}, f32[128,1152]{1,0:T(8,128)}, u32[]{:S(2)}, u32[]{:S(2)}) collective-permute-start(f32[128,1152]{1,0:T(8,128)} %get-tuple-element.193.refs_10_), channel_id=1, source_target_pairs={{0,1},{1,0},{2,3},{3,2},{4,5},{5,4},{6,7},{7,6},{8,9},{9,8},{10,11... | collective-permute-start | bytes 1769480 | tf_op jit(solution)/shard_map/ppermute | solution.py:1070
  245.3 22.8 %collective-permute-start.34 = (f32[128,1152]{1,0:T(8,128)}, f32[128,1152]{1,0:T(8,128)}, u32[]{:S(2)}, u32[]{:S(2)}) collective-permute-start(f32[128,1152]{1,0:T(8,128)} %get-tuple-element.194.refs_11_), channel_id=1, source_target_pairs={{0,1},{1,0},{2,3},{3,2},{4,5},{5,4},{6,7},{7,6},{8,9},{9,8},{10,11... | collective-permute-start | bytes 1769480 | tf_op jit(solution)/shard_map/ppermute | solution.py:1070
  263.8 27.0 %collective-permute-start.35 = (f32[128,1152]{1,0:T(8,128)}, f32[128,1152]{1,0:T(8,128)}, u32[]{:S(2)}, u32[]{:S(2)}) collective-permute-start(f32[128,1152]{1,0:T(8,128)} %get-tuple-element.195.refs_12_), channel_id=1, source_target_pairs={{0,1},{1,0},{2,3},{3,2},{4,5},{5,4},{6,7},{7,6},{8,9},{9,8},{10,11... | collective-permute-start | bytes 1769480 | tf_op jit(solution)/shard_map/ppermute | solution.py:1070
  264.0 26.9 %collective-permute-start.36 = (f32[4,12,72]{2,1,0:T(8,128)}, f32[4,12,72]{2,1,0:T(8,128)S(1)}, u32[]{:S(2)}, u32[]{:S(2)}) collective-permute-start(f32[4,12,72]{2,1,0:T(8,128)} %dynamic-slice_bitcast_fusion.14), channel_id=1, source_target_pairs={{0,4},{4,0},{1,5},{5,1},{2,6},{6,2},{3,7},{7,3},{8,12},{12,8},{9,1... | collective-permute-start | bytes 41480 | tf_op jit(solution)/shard_map/ppermute | solution.py:1070
  265.0 23.5 %collective-permute-start.37 = (f32[4,2,64]{2,1,0:T(2,128)S(1)}, f32[4,2,64]{2,1,0:T(2,128)S(1)}, u32[]{:S(2)}, u32[]{:S(2)}) collective-permute-start(f32[4,2,64]{2,1,0:T(2,128)S(1)} %bitcast.352), channel_id=1, source_target_pairs={{0,8},{8,16},{16,24},{24,0},{1,9},{9,17},{17,25},{25,1},{2,10},{10... | collective-permute-start | bytes 6152 | tf_op jit(solution)/shard_map/ppermute | solution.py:1074
  268.1 20.9 %collective-permute-start.38 = (f32[4,2,64]{2,1,0:T(2,128)S(1)}, f32[4,2,64]{2,1,0:T(2,128)S(1)}, u32[]{:S(2)}, u32[]{:S(2)}) collective-permute-start(f32[4,2,64]{2,1,0:T(2,128)S(1)} %bitcast.351), channel_id=1, source_target_pairs={{0,16},{8,24},{16,0},{24,8},{1,17},{9,25},{17,1},{25,9},{2,18},{10... | collective-permute-start | bytes 6152 | tf_op jit(solution)/shard_map/ppermute | solution.py:1074
  268.1 22.7 %collective-permute-start.39 = (f32[4,2,64]{2,1,0:T(2,128)S(1)}, f32[4,2,64]{2,1,0:T(2,128)S(1)}, u32[]{:S(2)}, u32[]{:S(2)}) collective-permute-start(f32[4,2,64]{2,1,0:T(2,128)S(1)} %bitcast.350), channel_id=1, source_target_pairs={{0,24},{8,0},{16,8},{24,16},{1,25},{9,1},{17,9},{25,17},{2,26},{10... | collective-permute-start | bytes 6152 | tf_op jit(solution)/shard_map/ppermute | solution.py:1074
  288.5 42.3 %collective-permute-start.46 = (f32[2,144,1152]{2,1,0:T(8,128)}, f32[2,144,1152]{2,1,0:T(8,128)S(1)}, u32[]{:S(2)}, u32[]{:S(2)}) collective-permute-start(f32[2,144,1152]{2,1,0:T(8,128)} %get-tuple-element.208), channel_id=1, source_target_pairs={{0,4},{4,0},{1,5},{5,1},{2,6},{6,2},{3,7},{7,3},{8,12},{12,8},{9,1... | collective-permute-start | bytes 3981320 | tf_op jit(solution)/shard_map/ppermute | solution.py:1070
  289.0 41.8 %collective-permute-start.47 = (f32[2,4,72,640]{3,2,1,0:T(8,128)}, f32[2,4,72,640]{3,2,1,0:T(8,128)S(1)}, u32[]{:S(2)}, u32[]{:S(2)}) collective-permute-start(f32[2,4,72,640]{3,2,1,0:T(8,128)} %get-tuple-element.209), channel_id=1, source_target_pairs={{0,2},{2,0},{1,3},{3,1},{4,6},{6,4},{5,7},{7,5},{8,10},{10,8},{9,1... | collective-permute-start | bytes 4423688 | tf_op jit(solution)/shard_map/ppermute | solution.py:1070
  293.9 24.2 %collective-permute-start.69 = (f32[2,64]{1,0:T(2,128)S(1)}, f32[2,64]{1,0:T(2,128)S(1)}, u32[]{:S(2)}, u32[]{:S(2)}) collective-permute-start(f32[2,64]{1,0:T(2,128)S(1)} %get-tuple-element.354), channel_id=1, source_target_pairs={{0,4},{4,0},{1,5},{5,1},{2,6},{6,2},{3,7},{7,3},{8,12},{12,8},{9,1... | collective-permute-start | bytes 1544 | tf_op jit(solution)/shard_map/ppermute | solution.py:1070
  294.5 27.8 %collective-permute-start.70 = (f32[2,64]{1,0:T(2,128)S(1)}, f32[2,64]{1,0:T(2,128)S(1)}, u32[]{:S(2)}, u32[]{:S(2)}) collective-permute-start(f32[2,64]{1,0:T(2,128)S(1)} %get-tuple-element.353), channel_id=1, source_target_pairs={{0,6},{6,0},{2,4},{4,2},{1,7},{7,1},{3,5},{5,3},{8,14},{14,8},{10,... | collective-permute-start | bytes 1544 | tf_op jit(solution)/shard_map/ppermute | solution.py:1093
  295.5 28.4 %collective-permute-start.68 = (f32[2,64]{1,0:T(2,128)S(1)}, f32[2,64]{1,0:T(2,128)S(1)}, u32[]{:S(2)}, u32[]{:S(2)}) collective-permute-start(f32[2,64]{1,0:T(2,128)S(1)} %get-tuple-element.352), channel_id=1, source_target_pairs={{0,2},{2,0},{1,3},{3,1},{4,6},{6,4},{5,7},{7,5},{8,10},{10,8},{9,1... | collective-permute-start | bytes 1544 | tf_op jit(solution)/shard_map/ppermute | solution.py:1070
  325.8 34.4 %collective-permute-start.56 = (f32[4,2,4,144]{3,2,1,0:T(4,128)}, f32[4,2,4,144]{3,2,1,0:T(4,128)}, u32[]{:S(2)}, u32[]{:S(2)}) collective-permute-start(f32[4,2,4,144]{3,2,1,0:T(4,128)} %get-tuple-element.214), channel_id=1, source_target_pairs={{0,8},{8,16},{16,24},{24,0},{1,9},{9,17},{17,25},{25,1},{2,10},{10... | collective-permute-start | bytes 55304 | tf_op jit(solution)/shard_map/ppermute | solution.py:1074
  327.3 32.9 %collective-permute-start.57 = (f32[4,2,4,144]{3,2,1,0:T(4,128)}, f32[4,2,4,144]{3,2,1,0:T(4,128)}, u32[]{:S(2)}, u32[]{:S(2)}) collective-permute-start(f32[4,2,4,144]{3,2,1,0:T(4,128)} %get-tuple-element.214), channel_id=1, source_target_pairs={{0,16},{8,24},{16,0},{24,8},{1,17},{9,25},{17,1},{25,9},{2,18},{10... | collective-permute-start | bytes 55304 | tf_op jit(solution)/shard_map/ppermute | solution.py:1074
  328.7 33.5 %collective-permute-start.58 = (f32[4,2,4,144]{3,2,1,0:T(4,128)}, f32[4,2,4,144]{3,2,1,0:T(4,128)}, u32[]{:S(2)}, u32[]{:S(2)}) collective-permute-start(f32[4,2,4,144]{3,2,1,0:T(4,128)} %get-tuple-element.214), channel_id=1, source_target_pairs={{0,24},{8,0},{16,8},{24,16},{1,25},{9,1},{17,9},{25,17},{2,26},{10... | collective-permute-start | bytes 55304 | tf_op jit(solution)/shard_map/ppermute | solution.py:1074
  335.7 31.8 %collective-permute-start.51 = (f32[144,1152]{1,0:T(8,128)}, f32[144,1152]{1,0:T(8,128)}, u32[]{:S(2)}, u32[]{:S(2)}) collective-permute-start(f32[144,1152]{1,0:T(8,128)} %add_bitcast_fusion.3), channel_id=1, source_target_pairs={{0,2},{2,0},{1,3},{3,1},{4,6},{6,4},{5,7},{7,5},{8,10},{10,8},{9,1... | collective-permute-start | bytes 1990664 | tf_op jit(solution)/shard_map/ppermute | solution.py:1070
  339.2 28.4 %collective-permute-start.52 = (f32[4,72,640]{2,1,0:T(8,128)}, f32[4,72,640]{2,1,0:T(8,128)S(1)}, u32[]{:S(2)}, u32[]{:S(2)}) collective-permute-start(f32[4,72,640]{2,1,0:T(8,128)} %add_bitcast_fusion.1), channel_id=1, source_target_pairs={{0,4},{4,0},{1,5},{5,1},{2,6},{6,2},{3,7},{7,3},{8,12},{12,8},{9,1... | collective-permute-start | bytes 2211848 | tf_op jit(solution)/shard_map/ppermute | solution.py:1070
  365.9 42.7 %collective-permute-start.73 = (f32[2,4,72,640]{3,2,1,0:T(8,128)}, f32[2,4,72,640]{3,2,1,0:T(8,128)}, u32[]{:S(2)}, u32[]{:S(2)}) collective-permute-start(f32[2,4,72,640]{3,2,1,0:T(8,128)} %get-tuple-element.236), channel_id=1, source_target_pairs={{0,2},{2,0},{1,3},{3,1},{4,6},{6,4},{5,7},{7,5},{8,10},{10,8},{9,1... | collective-permute-start | bytes 4423688 | tf_op jit(solution)/shard_map/ppermute | solution.py:1070
  366.6 39.8 %collective-permute-start.81 = (f32[2,144,1152]{2,1,0:T(8,128)}, f32[2,144,1152]{2,1,0:T(8,128)}, u32[]{:S(2)}, u32[]{:S(2)}) collective-permute-start(f32[2,144,1152]{2,1,0:T(8,128)} %get-tuple-element.239), channel_id=1, source_target_pairs={{0,4},{4,0},{1,5},{5,1},{2,6},{6,2},{3,7},{7,3},{8,12},{12,8},{9,1... | collective-permute-start | bytes 3981320 | tf_op jit(solution)/shard_map/ppermute | solution.py:1070
  376.1 19.3 %collective-permute-start.67 = (f32[2,64]{1,0:T(2,128)S(1)}, f32[2,64]{1,0:T(2,128)S(1)}, u32[]{:S(2)}, u32[]{:S(2)}) collective-permute-start(f32[2,64]{1,0:T(2,128)S(1)} %get-tuple-element.350), channel_id=1, source_target_pairs={{0,6},{6,0},{2,4},{4,2},{1,7},{7,1},{3,5},{5,3},{8,14},{14,8},{10,... | collective-permute-start | bytes 1544 | tf_op jit(solution)/shard_map/ppermute | solution.py:1093
  377.8 17.5 %collective-permute-start.65 = (f32[2,64]{1,0:T(2,128)S(1)}, f32[2,64]{1,0:T(2,128)S(1)}, u32[]{:S(2)}, u32[]{:S(2)}) collective-permute-start(f32[2,64]{1,0:T(2,128)S(1)} %get-tuple-element.349), channel_id=1, source_target_pairs={{0,2},{2,0},{1,3},{3,1},{4,6},{6,4},{5,7},{7,5},{8,10},{10,8},{9,1... | collective-permute-start | bytes 1544 | tf_op jit(solution)/shard_map/ppermute | solution.py:1070
  451.9 33.9 %collective-permute-start.72 = (f32[36,1152]{1,0:T(8,128)}, f32[36,1152]{1,0:T(8,128)}, u32[]{:S(2)}, u32[]{:S(2)}) collective-permute-start(f32[36,1152]{1,0:T(8,128)} %pad_maximum_fusion.8), channel_id=1, source_target_pairs={{0,0},{2,8},{4,16},{6,24},{8,2},{10,10},{12,18},{14,26},{16,4},{18... | collective-permute-start | bytes 497672 | tf_op jit(solution)/shard_map/ppermute | solution.py:1313
  (135 other events, 997.7 us)
Sparse Core Ops, SparseCore 0:
  9.7 52.9 all-gather.4
  64.9 51.5 all-gather.6
  118.1 50.5 all-gather.8
  170.2 50.7 all-gather.10
  238.9 65.6 reduce-scatter.4
  315.8 64.4 reduce-scatter.2

commit v3 on v2

--- a/solution.py
+++ b/solution.py
@@ -15,6 +15,7 @@
 IMAGES = 4
 BLOCK = SPAN // IMAGES
 GROUP = 4
+WEIGHT, GRADIENT_WEIGHT, WHOLE_COST = 10, 6, 40_000_000_000
 EPSILON = 1e-06
 MASKED = -1e30
 ROOT_HALF = 0.7071067811865476
@@ -86,7 +87,7 @@
         out_shape=[pltpu.HBM(out.shape, out.dtype) for out in out_shape],
         compiler_params=pltpu.CompilerParams(vmem_limit_bytes=40 << 20),
         cost_estimate=pl.CostEstimate(
-            flops=int(flops), bytes_accessed=int(size), transcendentals=0
+            flops=int(flops * GRADIENT_WEIGHT), bytes_accessed=int(size * GRADIENT_WEIGHT), transcendentals=0
         ),
         name=name,
     )
@@ -303,7 +304,7 @@
         scratch_shapes=[*scratch, pltpu.SemaphoreType.DMA((24,))],
         compiler_params=pltpu.CompilerParams(vmem_limit_bytes=limit << 20),
         cost_estimate=pl.CostEstimate(
-            flops=int(flops), bytes_accessed=int(size), transcendentals=0
+            flops=int(flops * WEIGHT), bytes_accessed=int(size * WEIGHT), transcendentals=0
         ),
         name=name,
     )(*scalars, *near, *map(in_hbm, (*far, *after)))
@@ -335,6 +336,22 @@
         held = gate([output, *due, *arrived])
         self.step(iter(held[1 + len(due) :]))
         return held[: 1 + len(due)]
+
+    def chain(self, partial, due=()):
+        arrived = [array for _, _, arrays in self.running for array in arrays]
+        partial, *rest = gate([partial, *due, *arrived])
+        partial, other, *rest = gate([partial, swap(partial, "tensor"), *rest])
+        self.step(iter(rest[len(due) :]))
+        return partial, other, *rest[: len(due)]
+
+    def hurry(self, name):
+        if name in self.found:
+            return self.found[name]
+        others = [entry for entry in self.running if entry[0] != name]
+        self.running = [entry for entry in self.running if entry[0] == name]
+        self.finish()
+        self.running = others
+        return self.found[name]
 
     def step(self, arrived=None):
         before, self.running = self.running, []
@@ -471,7 +488,7 @@
             pltpu.VMEM((count, local), FULL),
             pltpu.VMEM((count, width), FULL),
         ],
-        2 * count * width * local * 4 + heads * count * count * 2048,
+        2 * count * width * local * 4,
         8 * width * local + 16 * count * width,
         40,
         after,
@@ -850,36 +867,248 @@
     )(ids, *map(in_hbm, (xs, ys, hidden_in, hidden_out)))
 
 
-def feed_scatter(pieces, line):
+def whole_call(kernel, name, scalars, near, outs, scratch=(), limit=40):
+    return pl.pallas_call(
+        kernel,
+        in_specs=[
+            *[pl.BlockSpec(memory_space=pltpu.SMEM)] * len(scalars),
+            *[NEAR] * len(near),
+        ],
+        out_specs=[NEAR] * len(outs),
+        out_shape=[pltpu.HBM(out.shape, out.dtype) for out in outs],
+        scratch_shapes=list(scratch),
+        compiler_params=pltpu.CompilerParams(vmem_limit_bytes=limit << 20),
+        cost_estimate=pl.CostEstimate(
+            flops=WHOLE_COST, bytes_accessed=WHOLE_COST // 300, transcendentals=0
+        ),
+        name=name,
+    )(*scalars, *map(in_hbm, near))
+
+
+def feed_halve_kernel(ids, outer_keep, outer_half, inner_keep, inner_half, outer_own, outer_send, inner_own, inner_send):
+    row, col = ids[AT_ROW], ids[AT_COL]
+    outer_own[...] = outer_keep[row] + outer_half[row]
+    outer_send[...] = outer_keep[1 - row] + outer_half[1 - row]
+    inner_own[...] = inner_keep[col] + inner_half[col]
+    inner_send[...] = inner_keep[1 - col] + inner_half[1 - col]
+
+
+def feed_deal_kernel(line, ids, inner_own, inner_other, *outs):
+    place = ids[AT_LINE]
+    for by in range(line):
+        to = lax.rem(place + by, line)
+        outs[by][...] = inner_own[to] + inner_other[to]
+
+
+def feed_scatter(layer, ids, pieces, line):
     outer_keep, outer_send, inner_keep, inner_send = pieces
-    row, col = lax.axis_index("row"), lax.axis_index("col")
     outer_half, inner_half = yield [swap(outer_send, "col"), swap(inner_send, "row")]
-    outer_other, inner_other = yield [
-        swap(pick(outer_keep, 1 - row) + pick(outer_half, 1 - row), "row"),
-        swap(pick(inner_keep, 1 - col) + pick(inner_half, 1 - col), "col"),
+    outer_part, inner_part = shape_of(outer_keep.shape[1:]), shape_of(inner_keep.shape[1:])
+    outer_own, outer_send, inner_own, inner_send = whole_call(
+        feed_halve_kernel,
+        f"feed_halve_{layer}",
+        (ids,),
+        (outer_keep, outer_half, inner_keep, inner_half),
+        [outer_part, outer_part, inner_part, inner_part],
+    )
+    outer_other, inner_other = yield [swap(outer_send, "row"), swap(inner_send, "col")]
+    own, *rest = whole_call(
+        functools.partial(feed_deal_kernel, line),
+        f"feed_deal_{layer}",
+        (ids,),
+        (inner_own, inner_other),
+        [shape_of(inner_own.shape[1:])] * line,
+    )
+    far = yield [shift(rest[by - 1], line, by) for by in range(1, line)]
+    return [own, *far], [outer_own, outer_other]
+
+
+def attention_deal_kernel(layer, line, heads, at_rows, ids, summed, embedded, *refs):
+    images, projection, outs = refs[:line], refs[line], refs[line + 1 :]
+    own = images[0].shape[1]
+    chunk, lanes, left = at_rows.chunk, at_rows.LANES, at_rows.left
+    features = chunk // GROUP
+    for third in range(3):
+        row = at_rows.projection + third * at_rows.piece
+        projection[:, third * lanes : (third + 1) * lanes] = summed[row : row + at_rows.piece, :]
+    time = []
+    for member in range(2):
+        every = jnp.concatenate(
+            [ref[member * GROUP * IMAGES : (member + 1) * GROUP * IMAGES, :] for ref in images],
+            axis=0,
+        )
+        high = every.astype(LOW)
+        middle = (every - high.astype(FULL)).astype(LOW)
+        low = (every - high.astype(FULL) - middle.astype(FULL)).astype(LOW)
+        time.append(
+            matmul(embedded[...], high, TN)
+            + (matmul(embedded[...], middle, TN) + matmul(embedded[...], low, TN))
+        )
+    at = 2 * ids[AT_COL] + ids[AT_ROW]
+    entries = 4 * SPAN // line // GROUP
+    fold = chunk // at_rows.folds
+    for j in range(GROUP):
+
+        @pl.when(at == j)
+        def _(j=j):
+            for by in range(GROUP):
+                to, out = j ^ by, outs[by]
+                here = slice(to * features, (to + 1) * features)
+                out[:features, :lanes] = summed[here, :]
+                for i in range(at_rows.folds):
+                    first, last = max(i * fold, here.start), min((i + 1) * fold, here.stop)
+                    if first < last:
+                        row = at_rows.folded - i * fold
+                        out[first - here.start : last - here.start, lanes : 3 * own] = summed[
+                            row + first : row + last, i * left : (i + 1) * left
+                        ]
+                for member in range(2):
+                    out[:features, (3 + member) * own : (4 + member) * own] = time[member][here]
+                out[features:, :] = jnp.zeros((out.shape[0] - features, 5 * own), FULL)
+                out[features : features + heads, :entries] = summed[
+                    at_rows.table : at_rows.table + heads, to * entries : (to + 1) * entries
+                ]
+                if layer == 0:
+                    first = features + TABLE_ROWS
+                    out[first : first + VECTORS, :features] = summed[
+                        at_rows.vectors : at_rows.vectors + VECTORS, here
+                    ]
+
+
+def attention_deal(layer, line, ids, summed, embedded, images, heads, width, own):
+    at_rows = Rows(own, width, heads, VECTORS if layer == 0 else 0, line)
+    rows = width // line // GROUP + TABLE_ROWS + (VECTOR_ROWS if layer == 0 else 0)
+    projection, *blocks = whole_call(
+        functools.partial(attention_deal_kernel, layer, line, heads, at_rows),
+        f"attention_deal_{layer}",
+        (ids,),
+        (summed, embedded, *images),
+        [shape_of((own // line, width))] + [shape_of((rows, 5 * own))] * GROUP,
+    )
+    moved = lax.ppermute(
+        projection,
+        LINES,
+        [(GROUP * z + j, line * j + z) for z in range(line) for j in range(GROUP)],
+    )
+    projection, across, along, corner = yield [
+        moved,
+        swap(blocks[1], "row"),
+        swap(blocks[2], "col"),
+        swap_corner(blocks[3]),
     ]
-    outer = pick(outer_keep, row) + pick(outer_half, row) + outer_other
-    inner = pick(inner_keep, col) + pick(inner_half, col) + inner_other
-    place = lax.axis_index("line")
-    far = yield [shift(pick(inner, (place + by) % line), line, by) for by in range(1, line)]
-    slots = [pick(inner, place), *far]
-    turned = jnp.stack([slots[-i % line] for i in range(line)] * 2)
-    return lax.dynamic_slice_in_dim(turned, (line - place) % line, line, 0), outer
-
-
-def piece_rows(own, line):
-    padded = -(-own // line // 8) * 8
-    return 3 * padded, padded
-
-
-def attention_gradients_kernel(layer, heads, line, ids, kinds, *refs):
+    return projection, [blocks[0], across, along, corner]
+
+
+def assemble_kernel(depth, line, heads, ids, *refs):
+    blocks, refs = refs[: depth * GROUP], refs[depth * GROUP :]
+    projections, refs = refs[:depth], refs[depth:]
+    inners, refs = refs[: depth * line], refs[depth * line :]
+    outers, refs = refs[: 2 * depth], refs[2 * depth :]
+    token, time, table, projection, inner, outer, gain, shift_out, bias, sorted_inner = refs
+    features, local = token.shape[2:]
+    own = local // GROUP
+    units = inner.shape[2]
+    part = units // line
+    offsets = line_window(units, line)[1]
+    entries = table.shape[2]
+    at = 2 * ids[AT_COL] + ids[AT_ROW]
+    place = ids[AT_LINE]
+    for layer in range(depth):
+        projection[layer] = projections[layer][...]
+        outer[layer] = outers[2 * layer][...] + outers[2 * layer + 1][...]
+        for by in range(line):
+            sorted_inner[lax.rem(place + line - by, line)] = inners[layer * line + by][...]
+        for z in range(line):
+            inner[layer, :, z * part : (z + 1) * part] = sorted_inner[
+                z, :, offsets[z] : offsets[z] + part
+            ]
+        for j in range(GROUP):
+
+            @pl.when(at == j)
+            def _(j=j, layer=layer):
+                for by in range(GROUP):
+                    ref, source = blocks[layer * GROUP + by], j ^ by
+                    lanes = slice(source * own, (source + 1) * own)
+                    for member in range(3):
+                        token[layer, member, :, lanes] = ref[
+                            :features, member * own : (member + 1) * own
+                        ]
+                    for member in range(2):
+                        time[layer, member, :, lanes] = ref[
+                            :features, (3 + member) * own : (4 + member) * own
+                        ]
+                    table[layer, source * heads : (source + 1) * heads, :] = ref[
+                        features : features + heads, :entries
+                    ]
+
+    first = features + TABLE_ROWS
+    total = functools.reduce(
+        jnp.add, [blocks[by][first : first + 6 * depth, :features] for by in range(GROUP)]
+    )
+    for kind, out in enumerate((gain, shift_out, bias)):
+        for layer in range(depth):
+            begin = (kind * depth + layer) * 2
+            out[layer] = total[begin : begin + 2]
+
+
+def assemble(depth, line, ids, attention, feeds, heads, local, units, width):
+    features = width // (GROUP * line)
+    vector = shape_of((depth, 2, features))
+    size = line_window(units, line)[2]
+    return whole_call(
+        functools.partial(assemble_kernel, depth, line, heads // GROUP),
+        "assemble",
+        (ids,),
+        (
+            *[block for layer in range(depth) for block in attention[layer][1]],
+            *[attention[layer][0] for layer in range(depth)],
+            *[block for layer in range(depth) for block in feeds[layer][0]],
+            *[part for layer in range(depth) for part in feeds[layer][1]],
+        ),
+        [
+            shape_of((depth, 3, features, local)),
+            shape_of((depth, 2, features, local)),
+            shape_of((depth, heads, 4 * SPAN // (GROUP * line))),
+            shape_of((depth, local // (GROUP * line), width)),
+            shape_of((depth, features, units)),
+            shape_of((depth, units // (GROUP * line), width)),
+            vector,
+            vector,
+            vector,
+        ],
+        [pltpu.VMEM((line, features, size), FULL)],
+    )
+
+
+class Rows:
+    LANES = 384
+
+    def __init__(self, own, width, heads, vectors, line):
+        self.chunk, self.piece = width // line, own // line
+        self.left = 3 * own - self.LANES
+        self.folds = self.LANES // self.left
+        self.folded = self.chunk
+        self.projection = self.folded + self.chunk // self.folds
+        self.table = self.projection + 3 * self.piece
+        self.vectors = self.table + heads
+        self.total = -(-(self.vectors + vectors) // 8) * 8
+
+
+VECTORS = 12
+TABLE_ROWS, VECTOR_ROWS = 8, 16
+
+
+def attention_gradients_kernel(layer, heads, line, vector_count, ids, kinds, *refs):
     parts = 2 * GROUP - 1
     sources = refs[:parts], refs[parts : 2 * parts]
-    token_hbm, out_hbm, image_hbm, wide_ref, small_ref = refs[2 * parts : 2 * parts + 5]
-    refs = refs[2 * parts + 5 :]
-    token_out, table_out, images_out = refs[:3]
-    (images, low_x, low_y, joined, attended_low, rows, bias, steps, attended) = refs[3:12]
-    wide_sum, small_sum, stage, token, outer, scores, image_all, sems, weight_sems = refs[12:]
+    token_hbm, out_hbm = refs[2 * parts : 2 * parts + 2]
+    image_hbm = refs[2 * parts + 2 : 2 * parts + 2 + GROUP]
+    refs = refs[2 * parts + 2 + GROUP :]
+    wide_ref, small_ref = refs[:2]
+    vectors, refs = refs[2 : 2 + vector_count], refs[2 + vector_count :]
+    token_out, images_out = refs[:2]
+    (images, low_x, low_y, joined, attended_low, rows, bias, steps, attended) = refs[2:11]
+    wide_sum, small_sum, stage, token, outer, scores, image_all, sems, weight_sems = refs[11:]
     slot = pl.program_id(0)
     kind = kinds[slot]
     count = low_x.shape[1]
@@ -907,7 +1136,10 @@
     weights = [
         pltpu.make_async_copy(token_hbm.at[layer, :, mine, :], token, weight_sems.at[0]),
         pltpu.make_async_copy(out_hbm.at[layer, mine, :], outer, weight_sems.at[1]),
-        pltpu.make_async_copy(image_hbm.at[layer], image_all, weight_sems.at[2]),
+        *[
+            pltpu.make_async_copy(image_hbm[near], image_all.at[near], weight_sems.at[2 + near])
+            for near in range(GROUP)
+        ],
     ]
 
     @pl.when(slot == 0)
@@ -935,7 +1167,11 @@
             @pl.when(at == j)
             def _(j=j):
                 for member in range(2):
-                    images[member] = image_all[member, :, j * own : (j + 1) * own]
+                    first = (2 * layer + member) * IMAGES
+                    for near in range(GROUP):
+                        images[member, near * IMAGES : (near + 1) * IMAGES, :] = image_all[
+                            near, first : first + IMAGES, j * own : (j + 1) * own
+                        ]
 
     fill_bias(heads, kind, wide_ref, small_ref, bias)
     low_x[slot] = stage[0, slot].astype(LOW)
@@ -986,54 +1222,84 @@
         flat = GROUP * count
         width = low_x.shape[2]
 
-        chunk, piece = width // line, own // line
-        rest, padded = piece_rows(own, line)
         product = matmul(low_x[...].reshape(flat, width), joined[...].reshape(flat, -1), TN)
         projection = matmul(
             attended_low[...].reshape(flat, -1), low_y[...].reshape(flat, -1), TN
         )
-        size = width // 3
+        tables = [fold_table(wide_sum[head], small_sum[head]) for head in range(heads)]
+        size, cells = width // 3, 4 * SPAN // line
+        at_rows = Rows(own, width, heads, VECTORS if vectors else 0, line)
+        chunk, lanes, left = at_rows.chunk, at_rows.LANES, at_rows.left
+        fold = chunk // at_rows.folds
         for z in range(line):
-            begin = z * (chunk + rest)
-            token_out[begin : begin + chunk, :] = product[z * chunk : (z + 1) * chunk]
+            begin = z * at_rows.total
+            token_out[begin : begin + chunk, :] = product[z * chunk : (z + 1) * chunk, :lanes]
+            row = begin + at_rows.folded
+            for i in range(at_rows.folds):
+                first = z * chunk + i * fold
+                token_out[row : row + fold, i * left : (i + 1) * left] = product[
+                    first : first + fold, lanes:
+                ]
             for third in range(3):
-                at_row = begin + chunk + third * padded
-                token_out[at_row : at_row + padded, :] = jnp.zeros((padded, 3 * own), FULL)
-                token_out[at_row : at_row + piece, :size] = projection[
-                    z * piece : (z + 1) * piece, third * size : (third + 1) * size
+                row = begin + at_rows.projection + third * at_rows.piece
+                token_out[row : row + at_rows.piece, :] = projection[
+                    z * at_rows.piece : (z + 1) * at_rows.piece, third * size : (third + 1) * size
                 ]
-        for head in range(heads):
-            table_out[head : head + 1, :] = fold_table(wide_sum[head], small_sum[head])
-
-
-def attention_gradients(layer, line, ids, kinds, near_x, near_y, token_rows, per_image, out_proj, wide, small, after=()):
+            row = begin + at_rows.table
+            token_out[row : begin + at_rows.total, :] = jnp.zeros(
+                (at_rows.total - at_rows.table, lanes), FULL
+            )
+            for head in range(heads):
+                token_out[row + head : row + head + 1, :cells] = tables[head][
+                    :, z * cells : (z + 1) * cells
+                ]
+            row = begin + at_rows.vectors
+            for i, (ref, r) in enumerate(vector_places(vectors)):
+                token_out[row + i : row + i + 1, :chunk] = ref[
+                    r : r + 1, z * chunk : (z + 1) * chunk
+                ]
+
+
+def vector_places(vectors):
+    if not vectors:
+        return []
+    depth = (len(vectors) - 1) // 2
+    feeds, middles = vectors[1 : 1 + depth], vectors[1 + depth :]
+    firsts = [vectors[0], *feeds]
+    return (
+        [place for l in range(depth) for place in ((firsts[l], 1), (middles[l], 1))]
+        + [place for l in range(depth) for place in ((firsts[l], 2), (middles[l], 2))]
+        + [place for l in range(depth) for place in ((middles[l], 0), (feeds[l], 0))]
+    )
+
+
+def attention_gradients(layer, line, ids, kinds, near_x, near_y, token_rows, images, out_proj, wide, small, vectors, after=()):
     count, width = near_x[0].shape
     depth, _, local, _ = token_rows.shape
     own, heads = local // GROUP, wide.shape[0] // depth // GROUP
-    near = [pl.BlockSpec(memory_space=pl.ANY)] * (len(near_x) + len(near_y))
+    near = [HBM] * (len(near_x) + len(near_y))
+    at_rows = Rows(own, width, heads, VECTORS if vectors else 0, line)
 
     def own_heads(slot, ids, kinds):
         return (layer * GROUP + 2 * ids[AT_COL] + ids[AT_ROW], 0, 0)
 
     outs = [
-        shape_of((width + line * piece_rows(own, line)[0], 3 * own)),
-        shape_of((heads, 4 * SPAN)),
+        shape_of((line * at_rows.total, at_rows.LANES)),
         shape_of((GROUP, 2, IMAGES, own)),
     ]
     return call(
-        functools.partial(attention_gradients_kernel, layer, heads, line),
+        functools.partial(attention_gradients_kernel, layer, heads, line, len(vectors)),
         f"attention_gradients_{layer}",
         (GROUP,),
         [
             *near,
-            pl.BlockSpec(memory_space=pltpu.HBM),
-            pl.BlockSpec(memory_space=pltpu.HBM),
-            pl.BlockSpec(memory_space=pltpu.HBM),
+            *[HBM] * (2 + GROUP),
             pl.BlockSpec((heads, *wide.shape[1:]), own_heads),
             pl.BlockSpec((heads, *small.shape[1:]), own_heads),
+            *[whole(vector.shape) for vector in vectors],
         ],
         [
-            *[whole_once(out.shape) for out in outs[:2]],
+            whole_once(outs[0].shape),
             pl.BlockSpec((1, 2, IMAGES, own), lambda s, ids, kinds: (s, 0, 0, 0)),
         ],
         outs,
@@ -1053,16 +1319,16 @@
             pltpu.VMEM((3, own, width), LOW),
             pltpu.VMEM((own, width), LOW),
             pltpu.VMEM((heads, count, count), FULL),
-            pltpu.VMEM(per_image.shape[1:], FULL),
+            pltpu.VMEM((GROUP, *images[0].shape), FULL),
             pltpu.SemaphoreType.DMA((2, 2 * GROUP)),
-            pltpu.SemaphoreType.DMA((3,)),
+            pltpu.SemaphoreType.DMA((2 + GROUP,)),
         ],
         2 * GROUP * count * width * own * 8 + GROUP * heads * count * count * 4096,
         8 * GROUP * count * width + 8 * width * local,
         2,
         after,
     )(
-        ids, kinds, *map(in_hbm, (*near_x, *near_y, token_rows, out_proj, per_image)), wide, small
+        ids, kinds, *map(in_hbm, (*near_x, *near_y, token_rows, out_proj, *images)), wide, small, *vectors
     )
 
 
@@ -1074,18 +1340,14 @@
     return lax.ppermute(value, "line", [(i, (i + by) % line) for i in range(line)])
 
 
-def pick(value, index, axis=0):
-    return lax.dynamic_index_in_dim(value, index, axis, keepdims=False)
-
-
 def gather_line(half):
     return lax.all_gather(half, ("line", "tensor"), tiled=True)
 
 
 def plane_steps(value, half):
     across, along = yield [swap(half, "row"), swap(half, "col")]
-    (corner,) = yield [swap_corner(half)]
-    others = yield [swap(part, "tensor") for part in (across, along, corner)]
+    corner, *others = yield [swap_corner(half), swap(across, "tensor"), swap(along, "tensor")]
+    others += yield [swap(corner, "tensor")]
     return [value, across, along, corner, *others]
 
 
@@ -1093,38 +1355,14 @@
     return lax.ppermute(value, ("col", "row"), [(0, 3), (3, 0), (1, 2), (2, 1)])
 
 
-def scatter_line(value, line):
-    place = lax.axis_index("line")
-    far = yield [shift(pick(value, (place + by) % line), line, by) for by in range(1, line)]
-    return functools.reduce(jnp.add, far, pick(value, place))
-
-
-def scatter_vectors(value, line):
-    row, col = lax.axis_index("row"), lax.axis_index("col")
-    (other,) = yield [swap(pick(value, 1 - row, 2), "row")]
-    value = pick(value, row, 2) + other
-    (other,) = yield [swap(pick(value, 1 - col, 1), "col")]
-    return (yield from scatter_line(pick(value, col, 1) + other, line))
-
-
-def scatter_table(value, line):
-    return exchange_plane((yield from scatter_line(value, line)))
-
-
-def line_steps(value, line):
+def plane_all(value):
+    across, along, corner = yield [swap(value, "row"), swap(value, "col"), swap_corner(value)]
+    return [value, across, along, corner]
+
+
+def line_all(value, line):
     far = yield [shift(value, line, by) for by in range(1, line)]
-    return jnp.concatenate([value, *far])
-
-
-def exchange_plane(value):
-    col, row = lax.axis_index("col"), lax.axis_index("row")
-    place = 2 * col + row
-    across = swap(pick(value, place ^ 1), "row")
-    along = swap(pick(value, place ^ 2), "col")
-    corner = swap_corner(pick(value, place ^ 3))
-    slots = [pick(value, place), across, along, corner]
-    slots = [jnp.where(row == 0, slots[i], slots[i ^ 1]) for i in range(4)]
-    return jnp.stack([jnp.where(col == 0, slots[i], slots[i ^ 2]) for i in range(4)])
+    return [value, *far]
 
 
 def local(
@@ -1152,7 +1390,6 @@
     n_dp = GROUP * line
     features = width // n_dp
     line_at = lax.axis_index("line")
-    place = 2 * lax.axis_index("col") + lax.axis_index("row")
     ids = jnp.stack(
         [segment_ids[-1], line_at, lax.axis_index("col"), lax.axis_index("row"), lax.axis_index("tensor")]
     ).astype(jnp.int32)
@@ -1168,22 +1405,14 @@
             jnp.pad(info[None], ((0, 7), (0, local_width - IMAGES - 1))),
         ]
     )
-    packed = jnp.stack([packed, swap(packed, "row"), swap(packed, "col"), swap_corner(packed)])
-    near_image = packed[:, : 2 * depth * IMAGES].reshape(GROUP, depth, 2, IMAGES, local_width)
-    near_image = jnp.moveaxis(near_image, 0, 2).reshape(depth, 2, GROUP * IMAGES, local_width)
-    near = packed[:, 2 * depth * IMAGES, : IMAGES + 1]
-    kinds = near[:, IMAGES].astype(jnp.int32)
-    near = jnp.pad(near, ((0, 4), (0, 123 - IMAGES + 4)))
-    every = jnp.concatenate([near] + [shift(near, line, by) for by in range(1, line)])
-    every = every.reshape(line, 8, -1)[:, :GROUP, :IMAGES]
     own_feature = line_at * (GROUP * features) + jnp.arange(GROUP * features, dtype=jnp.int32)
-    embedded_every = sinusoid(every.reshape(-1), own_feature, width).astype(FULL)
     token_rows = jnp.swapaxes(token_proj, 2, 3)
     wide, small = expand_table(bias_table.reshape(depth * heads, -1))
 
     stream = (tokens,)
     saved = []
     moves = Moves()
+    moves.start("packed", plane_all(packed))
     half = lax.dynamic_slice_in_dim(cotangent, lax.axis_index("tensor") * (count // 2), count // 2, 0)
     gathered_up = gather_line(half.astype(FULL))
     for layer in range(depth):
@@ -1191,26 +1420,33 @@
             layer, ids, stream, norm_gain, norm_bias, branch_bias, token_rows, per_image, out_proj, wide, small
         )
         if layer == depth - 1:
-            partial, gathered_up = moves.kernel(partial, [gathered_up])
+            partial, other, gathered_up = moves.chain(partial, [gathered_up])
         else:
-            (partial,) = moves.kernel(partial)
+            partial, other = moves.chain(partial)
         moves.start(("first", layer), plane_steps(normed, half))
+        if layer == depth - 1:
+            near = jnp.stack(
+                [part[2 * depth * IMAGES, : IMAGES + 1] for part in moves.found["packed"]]
+            )
+            kinds = near[:, IMAGES].astype(jnp.int32)
+            info = jnp.pad(near, ((0, 8 - GROUP), (0, 128 - IMAGES - 1)))
+            moves.start("info", line_all(info, line))
         middle, half_second, slope, partial = feed(
             layer,
             ids,
             held,
             partial,
-            swap(partial, "tensor"),
+            other,
             branch_bias,
             norm_gain,
             norm_bias,
             hidden_in,
             hidden_out,
         )
-        (partial,) = moves.kernel(partial)
+        partial, other = moves.chain(partial)
         line_second = gather_line(half_second)
         saved.append((held, rows, middle, slope, line_second, bias))
-        stream = (middle, partial, swap(partial, "tensor"))
+        stream = (middle, partial, other)
     output = (stream[0] + (stream[1] + stream[2]) + branch_bias[depth - 1, 1]).astype(LOW)
 
     upstream = (cotangent,)
@@ -1223,7 +1459,7 @@
         current, half_up, feed_sums, partial = feed_back(
             layer, ids, upstream, slope, hidden_in, hidden_out, norm_gain
         )
-        (partial,) = moves.kernel(partial)
+        partial, other = moves.chain(partial)
         if layer < depth - 1:
             gathered_up = gather_line(half_up)
         back_middle, half, middle_sums, back_partial = attend_back(
@@ -1231,7 +1467,7 @@
             ids,
             current,
             partial,
-            swap(partial, "tensor"),
+            other,
             middle,
             norm_gain,
             rows,
@@ -1239,109 +1475,106 @@
             out_proj,
             token_rows,
         )
-        other = depth - 1 - layer
-        back_partial, gathered_line[other] = moves.kernel(back_partial, [saved[other][4]])
+        if layer > 0:
+            back_partial, other, gathered_line[0] = moves.chain(back_partial, [saved[0][4]])
+        else:
+            back_partial, other = moves.chain(back_partial)
         moves.start(("branch", layer), plane_steps(back_middle, half))
-        upstream = (back_middle, back_partial, swap(back_partial, "tensor"), held)
+        upstream = (back_middle, back_partial, other, held)
         vectors[layer] = (feed_sums, middle_sums)
         gathered[layer] = gathered_up
     gradient_tokens, last_sums = finish(*upstream, norm_gain)
-    (last_sums,) = moves.kernel(last_sums)
-    firsts = [last_sums] + [vectors[layer][0] for layer in range(depth - 1)]
-    rows = jnp.stack(
-        [
-            jnp.stack([jnp.stack([firsts[l][1], vectors[l][1][1]]) for l in range(depth)]),
-            jnp.stack([jnp.stack([firsts[l][2], vectors[l][1][2]]) for l in range(depth)]),
-            jnp.stack([jnp.stack([vectors[l][1][0], vectors[l][0][0]]) for l in range(depth)]),
-        ]
-    )
-    rows = jnp.moveaxis(rows.reshape(6 * depth, line, 2, 2, features), 0, 3)
-    moves.start("rows", scatter_vectors(rows, line))
-
-    turn = last_sums
+    sums = [last_sums, *[pair[0] for pair in vectors], *[pair[1] for pair in vectors]]
+    packed = moves.found["packed"]
     tokens_of = {}
 
-    def run_feed(layer, turn):
+
+    def run_feed(layer, turn, due=()):
         pieces = feed_gradients(
-            layer, line, ids, gathered_line[layer], gathered[layer], hidden_in, hidden_out, after=(turn,)
+            layer, line, ids, gathered_line[layer], gathered[layer], hidden_in, hidden_out, after=turn
         )
-        (turn,) = moves.kernel(pieces[0])
-        moves.start(("feed", layer), feed_scatter((turn, *pieces[1:]), line))
-        return turn
-
-    def run_attention(layer, turn):
-        token, table, images = attention_gradients(
+        turn, *due = moves.kernel(pieces[0], due)
+        moves.start(("feed", layer), feed_scatter(layer, ids, (turn, *pieces[1:]), line))
+        return turn, due
+
+    def run_attention(layer, turn, due=()):
+        token, found = attention_gradients(
             layer,
             line,
             ids,
             kinds,
             moves.found["first", layer],
-            moves.found["branch", layer],
+            moves.hurry(("branch", layer)),
             token_rows,
-            near_image,
+            packed,
             out_proj,
             wide,
             small,
-            after=(turn,),
+            sums if layer == 0 else (),
+            after=turn,
         )
-        turn, gathered[0] = moves.kernel(table, [gathered[0]])
+        turn, *due = moves.kernel(found, due)
         tokens_of[layer] = lax.psum_scatter(token, "line", scatter_dimension=0, tiled=True)
-        table = turn.reshape(-1, line, GROUP, 4 * SPAN // n_dp)
-        moves.start(("table", layer), scatter_table(jnp.moveaxis(table, 0, 2), line))
-        moves.start(("images", layer), line_steps(images, line))
-        return turn
-
-    for layer in reversed(range(1, depth)):
-        turn = run_feed(layer, run_attention(layer, turn))
-    run_feed(0, run_attention(0, turn))
+        moved = jnp.swapaxes(turn, 0, 1).reshape(2 * GROUP * IMAGES, own)
+        moves.start(("images", layer), line_all(moved, line))
+        return turn, due
+
+    top = depth - 1
+    turn, (gathered_line[top],) = run_attention(top, (), [saved[top][4]])
+    turn, (gathered[0],) = run_feed(top, (turn,), [gathered[0]])
+    turn, _ = run_feed(0, (turn,))
+    _, (tokens_of[top],) = run_attention(0, (turn,), [tokens_of[top]])
+    every = jnp.concatenate([part[:GROUP, :IMAGES].reshape(-1) for part in moves.found["info"]])
+    embedded_every = sinusoid(every, own_feature, width)
+    def deal(layer):
+        moves.start(
+            ("attention", layer),
+            attention_deal(
+                layer,
+                line,
+                ids,
+                tokens_of[layer],
+                embedded_every,
+                moves.hurry(("images", layer)),
+                heads // GROUP,
+                width,
+                own,
+            ),
+        )
+
+    for layer in range(1, depth):
+        deal(layer)
+    moves.hurry(("images", 0))
     moves.finish()
-
-    for layer in reversed(range(depth)):
-        inner, outer = moves.found["feed", layer]
-        offsets = line_window(units, line)[1]
-        inner = jnp.concatenate(
-            [inner[z, :, offsets[z] : offsets[z] + units // line] for z in range(line)], axis=1
-        )
-        token, images = tokens_of[layer], moves.found["images", layer]
-        chunk, padded = GROUP * features, piece_rows(own, line)[1]
-        thirds = [
-            token[chunk + third * padded : chunk + third * padded + own // line, : width // 3]
-            for third in range(3)
-        ]
-        projection = jnp.concatenate(thirds, axis=1)
-        token = token[:chunk]
-        projection = lax.ppermute(
-            projection,
-            LINES,
-            [(GROUP * z + j, line * j + z) for z in range(line) for j in range(GROUP)],
-        )
-        time = jnp.einsum(
-            "rif,rmic->fmc",
-            embedded_every.reshape(n_dp, IMAGES, GROUP * features),
-            images,
-            precision=lax.Precision.HIGHEST,
-        )
-        joined = jnp.concatenate([token, time.reshape(GROUP * features, 2 * own)], axis=1)
-        joined = exchange_plane(joined.reshape(GROUP, features, 5 * own))
-        joined = joined.reshape(GROUP, features, 5, own).transpose(2, 1, 0, 3)
-        joined = joined.reshape(5, features, local_width)
-        collected[layer] = (joined[:3], joined[3:], projection, inner, outer)
-    rows = moves.found["rows"].reshape(3, depth, 2, features)
-    table = jnp.stack([moves.found["table", layer].reshape(heads, -1) for layer in range(depth)])
-    stacked = [jnp.stack([terms[member] for terms in collected]) for member in range(5)]
-    token, time, projection, inner, outer = stacked
+    others = [moves.found["feed", 0], moves.found["attention", depth - 1]]
+    held, others = jax.tree.flatten(others)
+    tokens_of[0], *held = gate([tokens_of[0], *held])
+    moves.found["feed", 0], moves.found["attention", depth - 1] = jax.tree.unflatten(others, held)
+    deal(0)
+    moves.finish()
+    token, time, table, projection, inner, outer, gain, shifts, bias = assemble(
+        depth,
+        line,
+        ids,
+        [moves.found["attention", layer] for layer in range(depth)],
+        [moves.found["feed", layer] for layer in range(depth)],
+        heads,
+        local_width,
+        units,
+        width,
+    )
     return (
         output,
         gradient_tokens,
-        rows[0],
-        rows[1],
+        gain,
+        shifts,
         token,
         time,
         table,
         projection,
         inner,
         outer,
-        rows[2],
+        bias,
     )
 
 

time: 518 us -> 421 us (0.81)
  waiting for transfers between devices: 148 us -> 108 us
  starting transfers between devices: 97.9 us -> 68.5 us
  other arithmetic: 33.5 us -> 4.93 us
  Pallas kernels: 160 us -> 184 us
  local copies, waits for them, and re-layouts: 47.6 us -> 29 us
    ppermute x48 -> x42, waiting for transfers between devices: 104 us -> 63.7 us  [swap(): return lax.ppermute(value, axis, [(0, 1), (1, 0)])]
    pallas_call x0 -> x7, Pallas kernels: none -> 25.9 us  [whole_call(): pl.pallas_call(kernel, in_specs=[*[pl.BlockSpec(memory_space=pltpu.SMEM)]...]
    ppermute x2, waiting for transfers between devices: 0.01 us -> 23.5 us  [attention_deal(): lax.ppermute(projection, LINES, [(GROUP * z + j, line * j + z) for z in r...]
    ppermute x24 -> x15, starting transfers between devices: 37.8 us -> 21.7 us  [shift(): lax.ppermute(value, 'line', [(i, (i + by) % line) for i in range(line)])]
    ppermute x24 -> x15, waiting for transfers between devices: 25.8 us -> 9.82 us  [shift(): lax.ppermute(value, 'line', [(i, (i + by) % line) for i in range(line)])]
    add x11 -> x0, other arithmetic: 13.3 us -> none  [the longest x2 4.15 us: feed_scatter(): pick(outer_keep, 1 - row) + pick(outer_half, 1 - row)]
    ppermute x9 -> x7, waiting for transfers between devices: 18.3 us -> 6.78 us  [swap_corner(): return lax.ppermute(value, ('col', 'row'), [(0, 3), (3, 0), (1, 2), (2, 1)])]
    another operation x21 -> x1, other arithmetic: 9.61 us -> 0.01 us  [local(): jnp.stack([part[2 * depth * IMAGES, :IMAGES + 1] for part in moves.found[...]
  transfers between devices with their start and end apart: 89 -> 72, of which waited for: 36 -> 26; matrix products, arithmetic and copies ran while one was open for 12% -> 3% of each run, Pallas kernels for 31% -> 43%
where the time goes in v3:
time: 421 us; the launch traced here: 414 us
  Pallas kernels  184 us (44%)
  waiting for transfers between devices  108 us (26%)
  starting transfers between devices  68.5 us (16%)
  local copies, waits for them, and re-layouts  29 us (7%)
  between operations  15.3 us (4%)
  other arithmetic  4.93 us (1%)
    pallas_call x9, Pallas kernels, plain(): pl.pallas_call(body, in_specs=[*[pl.BlockSpec(memory_space=pltpu.SMEM)] *...  82.4 us
    pallas_call x4, Pallas kernels, call(): return lambda *operands: made(*operands, *map(in_hbm, after))  71.5 us
    ppermute x42, waiting for transfers between devices, swap(): return lax.ppermute(value, axis, [(0, 1), (1, 0)])  63.7 us
    ppermute x42, starting transfers between devices, swap(): return lax.ppermute(value, axis, [(0, 1), (1, 0)])  30 us
    pallas_call x7, Pallas kernels, whole_call(): pl.pallas_call(kernel, in_specs=[*[pl.BlockSpec(memory_space=pltpu.SMEM)]...  25.9 us
    unnamed x181, local copies, waits for them, and re-layouts  24.5 us
    ppermute x2, waiting for transfers between devices, attention_deal(): lax.ppermute(projection, LINES, [(GROUP * z + j, line * j + z) for z in r...  23.5 us
    ppermute x15, starting transfers between devices, shift(): lax.ppermute(value, 'line', [(i, (i + by) % line) for i in range(line)])  21.7 us
  transfers between devices with their start and end apart: 72, of which 26 were waited for; matrix products, arithmetic and copies ran while one was open for 3% of the time, Pallas kernels for 43%

profile of v3, /device:TPU:2, one launch (start us, length us, event | category | flops | bytes accessed | tf_op | source)
XLA Modules:
  0.0 414.2 jit_solution(4409866394990099716)
XLA Ops:
  9.8 4.2 %convolution_bitcast_fusion.refs_7_.refs_9_ = f32[2,2,4,576]{3,2,1,0:T(4,128)S(1)} fusion(bf16[2,2,1152,576]{2,3,1,0:T(8,128)(2,1)} %param.19, f32[1152]{0:T(1024)S(1)} %fusion.11, f32[4]{0:T(128)S(1)} %convert_bitcast_fusion, pred[1152]{0:T(1024)(128)(4,1)S(1)} %iota_compare_fusion.1), kind=kOutput, calls=%fused_computation.1 | convolution fusion | flops 21247488 | bytes 5351056 | tf_op jit(solution)/shard_map/dot_general | solution.py:1397
  18.3 4.3 %expand_table.1 = (f32[16,16,512]{2,1,0:T(8,128)}, f32[16,8,128]{2,1,0:T(8,128)}) custom-call(f32[16,1024]{1,0:T(8,128)} %bitcast.23), custom_call_target="tpu_custom_call" | custom-call | tf_op jit(solution)/shard_map/expand_table/pallas_call | solution.py:136
  23.4 8.0 %attend_0.1 = (f32[256,1152]{1,0:T(8,128)}, f32[256,1152]{1,0:T(8,128)}, f32[128,1152]{1,0:T(8,128)}, bf16[3,256,576]{2,1,0:T(8,128)(2,1)}, f32[256,1152]{1,0:T(8,128)}, /*index=5*/f32[8,256,256]{2,1,0:T(8,128)}) custom-call(s32[5]{0:T(128)S(1)} %stack.22.refs_0_.ids, f32[2,2,1152]{2,1,0:T(2,128)S(1)} %copy-done, f32[2,2,1152]{2,1,0:T(2,128)S(1)} %copy-done.5, ...), custom_call_target="tpu_custom_call" | custom-call | flops 13589544960 | bytes 100270080 | tf_op jit(solution)/shard_map/attend_0/pallas_call | solution.py:295
  36.3 9.6 %feed_0.1 = (f32[256,1152]{1,0:T(8,128)}, f32[128,1152]{1,0:T(8,128)}, f32[256,2304]{1,0:T(8,128)}, f32[256,1152]{1,0:T(8,128)}) custom-call(s32[5]{0:T(128)S(1)} %stack.22.refs_0_.ids, f32[2,2,1152]{2,1,0:T(2,128)S(1)} %copy-done, f32[2,2,1152]{2,1,0:T(2,128)S(1)} %copy-done.5, f32[2,2,1152]{2,1,0:T(2,128)S(1)} %copy-done.1, ...), custom_call_target="tpu_custom_call" | custom-call | flops 27179089920 | bytes 200540160 | tf_op jit(solution)/shard_map/feed_0/pallas_call | solution.py:295
  53.4 9.1 %attend_1.1 = (f32[256,1152]{1,0:T(8,128)}, f32[256,1152]{1,0:T(8,128)}, f32[128,1152]{1,0:T(8,128)}, bf16[3,256,576]{2,1,0:T(8,128)(2,1)}, f32[256,1152]{1,0:T(8,128)}, /*index=5*/f32[8,256,256]{2,1,0:T(8,128)}) custom-call(s32[5]{0:T(128)S(1)} %stack.22.refs_0_.ids, f32[2,2,1152]{2,1,0:T(2,128)S(1)} %copy-done, f32[2,2,1152]{2,1,0:T(2,128)S(1)} %copy-done.5, ...), custom_call_target="tpu_custom_call" | custom-call | flops 13589544960 | bytes 100270080 | tf_op jit(solution)/shard_map/attend_1/pallas_call | solution.py:295
  77.7 9.5 %feed_1.1 = (f32[256,1152]{1,0:T(8,128)}, f32[128,1152]{1,0:T(8,128)}, f32[256,2304]{1,0:T(8,128)}, f32[256,1152]{1,0:T(8,128)}) custom-call(s32[5]{0:T(128)S(1)} %stack.22.refs_0_.ids, f32[2,2,1152]{2,1,0:T(2,128)S(1)} %copy-done, f32[2,2,1152]{2,1,0:T(2,128)S(1)} %copy-done.5, f32[2,2,1152]{2,1,0:T(2,128)S(1)} %copy-done.1, ...), custom_call_target="tpu_custom_call" | custom-call | flops 27179089920 | bytes 200540160 | tf_op jit(solution)/shard_map/feed_1/pallas_call | solution.py:295
  96.5 9.0 %feed_back_1.1 = (f32[256,1152]{1,0:T(8,128)}, f32[128,1152]{1,0:T(8,128)}, f32[8,1152]{1,0:T(8,128)}, f32[256,1152]{1,0:T(8,128)}) custom-call(s32[5]{0:T(128)S(1)} %stack.22.refs_0_.ids, f32[2,2,1152]{2,1,0:T(2,128)S(1)} %copy-done, bf16[256,1152]{1,0:T(8,128)(2,1)} %refs_2_.9, f32[256,2304]{1,0:T(8,128)} %get-tuple-element.250.refs_3_, ...), custom_call_target="tpu_custom_call" | custom-call | flops 27179089920 | bytes 200540160 | tf_op jit(solution)/shard_map/feed_back_1/pallas_call | solution.py:295
  114.1 11.4 %attend_back_1.1 = (f32[256,1152]{1,0:T(8,128)}, f32[128,1152]{1,0:T(8,128)}, f32[8,1152]{1,0:T(8,128)}, f32[256,1152]{1,0:T(8,128)}) custom-call(s32[5]{0:T(128)S(1)} %stack.22.refs_0_.ids, f32[2,2,1152]{2,1,0:T(2,128)S(1)} %copy-done, f32[256,1152]{1,0:T(8,128)} %get-tuple-element.251.refs_2_, f32[256,1152]{1,0:T(8,128)} %get-tuple-element.259.refs_3_, ...), custom_call_target="tpu_custom_call" | custom-call | flops 35064381440 | bytes 123863040 | tf_op jit(solution)/shard_map/attend_back_1/pallas_call | solution.py:295
  130.5 10.1 %feed_back_0.1 = (f32[256,1152]{1,0:T(8,128)}, f32[128,1152]{1,0:T(8,128)}, f32[8,1152]{1,0:T(8,128)}, f32[256,1152]{1,0:T(8,128)}) custom-call(s32[5]{0:T(128)S(1)} %stack.22.refs_0_.ids, f32[2,2,1152]{2,1,0:T(2,128)S(1)} %copy-done, f32[256,1152]{1,0:T(8,128)} %get-tuple-element.263.refs_2_.refs_9_, f32[256,1152]{1,0:T(8,128)} %get-tuple-element.270.refs_3_, ...), custom_call_target="tpu_custom_call" | custom-call | flops 27179089920 | bytes 200540160 | tf_op jit(solution)/shard_map/feed_back_0/pallas_call | solution.py:295
  148.8 11.4 %attend_back_0.1 = (f32[256,1152]{1,0:T(8,128)}, f32[128,1152]{1,0:T(8,128)}, f32[8,1152]{1,0:T(8,128)}, f32[256,1152]{1,0:T(8,128)}) custom-call(s32[5]{0:T(128)S(1)} %stack.22.refs_0_.ids, f32[2,2,1152]{2,1,0:T(2,128)S(1)} %copy-done, f32[256,1152]{1,0:T(8,128)} %get-tuple-element.273.refs_2_, f32[256,1152]{1,0:T(8,128)} %get-tuple-element.279.refs_3_, ...), custom_call_target="tpu_custom_call" | custom-call | flops 35064381440 | bytes 123863040 | tf_op jit(solution)/shard_map/attend_back_0/pallas_call | solution.py:295
  172.0 4.3 %finish.1 = (bf16[256,1152]{1,0:T(8,128)(2,1)}, f32[8,1152]{1,0:T(8,128)}) custom-call(f32[2,2,1152]{2,1,0:T(2,128)S(1)} %copy-done, f32[256,1152]{1,0:T(8,128)} %get-tuple-element.283.refs_1_.refs_9_, f32[256,1152]{1,0:T(8,128)} %get-tuple-element.291.refs_2_, f32[256,1152]{1,0:T(8,128)} %get-tuple-element.292.refs_3_, f32[256,1152]{1,0:T(8,128)} %get-tuple-element.207.refs_4_), custom_call_target="tpu_custom_call" | custom-call | bytes 58982400 | tf_op jit(solution)/shard_map/finish/pallas_call | solution.py:295
  176.4 17.9 %attention_gradients_1.1 = (f32[1760,384]{1,0:T(8,128)}, f32[4,2,4,144]{3,2,1,0:T(4,128)}) custom-call(s32[5]{0:T(128)S(1)} %stack.22.refs_0_.ids, s32[4]{0:T(128)S(1)} %convert_reduce_fusion.refs_1_, f32[256,1152]{1,0:T(8,128)} %get-tuple-element.298.refs_2_, f32[128,1152]{1,0:T(8,128)} %get-tuple-element.253.refs_3_, ...), custom_call_target="tpu_custom_call" | custom-call | flops 29192355840 | bytes 88473600 | tf_op jit(solution)/shard_map/attention_gradients_1/pallas_call | solution.py:94
  194.3 3.4 collective-permute-done.33.refs_3_
  203.8 17.8 %feed_gradients_1.1 = (f32[2,144,1152]{2,1,0:T(8,128)}, f32[2,144,1152]{2,1,0:T(8,128)}, f32[2,4,72,640]{3,2,1,0:T(8,128)}, f32[2,4,72,640]{3,2,1,0:T(8,128)}) custom-call(s32[5]{0:T(128)S(1)} %stack.22.refs_0_.ids, f32[1024,1152]{1,0:T(8,128)} %get-tuple-element.310.refs_1_, f32[1024,1152]{1,0:T(8,128)} %get-tuple-element.311.refs_2_, ...), custom_call_target="tpu_custom_call" | custom-call | flops 36238786560 | bytes 127401984 | tf_op jit(solution)/shard_map/feed_gradients_1/pallas_call | solution.py:94
  223.6 4.1 all-gather.11.cloned.1.call-done.refs_1_
  228.0 17.8 %feed_gradients_0.1 = (f32[2,144,1152]{2,1,0:T(8,128)}, f32[2,144,1152]{2,1,0:T(8,128)}, f32[2,4,72,640]{3,2,1,0:T(8,128)}, f32[2,4,72,640]{3,2,1,0:T(8,128)}) custom-call(s32[5]{0:T(128)S(1)} %stack.22.refs_0_.ids, f32[1024,1152]{1,0:T(8,128)} %get-tuple-element.318.refs_1_, f32[1024,1152]{1,0:T(8,128)} %get-tuple-element.319.refs_2_, ...), custom_call_target="tpu_custom_call" | custom-call | flops 36238786560 | bytes 127401984 | tf_op jit(solution)/shard_map/feed_gradients_0/pallas_call | solution.py:94
  248.0 6.4 %collective-permute-done.41.refs_2_ = f32[2,144,1152]{2,1,0:T(8,128)} collective-permute-done((f32[2,144,1152]{2,1,0:T(8,128)}, f32[2,144,1152]{2,1,0:T(8,128)}, u32[]{:S(2)}, u32[]{:S(2)}) %collective-permute-start.41) | collective-permute-done | bytes 1327136 | tf_op jit(solution)/shard_map/ppermute | solution.py:1336
  254.4 4.5 %collective-permute-done.42.refs_3_ = f32[2,4,72,640]{3,2,1,0:T(8,128)} collective-permute-done((f32[2,4,72,640]{3,2,1,0:T(8,128)}, f32[2,4,72,640]{3,2,1,0:T(8,128)}, u32[]{:S(2)}, u32[]{:S(2)}) %collective-permute-start.42) | collective-permute-done | bytes 1474592 | tf_op jit(solution)/shard_map/ppermute | solution.py:1336
  258.9 4.5 %feed_halve_1.1 = (f32[144,1152]{1,0:T(8,128)}, f32[144,1152]{1,0:T(8,128)}, f32[4,72,640]{2,1,0:T(8,128)}, f32[4,72,640]{2,1,0:T(8,128)}) custom-call(s32[5]{0:T(128)S(1)} %stack.22.refs_0_.ids, f32[2,144,1152]{2,1,0:T(8,128)} %get-tuple-element.320.refs_5_.outer_keep, f32[2,144,1152]{2,1,0:T(8,128)} %get-tuple-element.334.outer_half, ...), custom_call_target="tpu_custom_call" | custom-call | flops 40000000000 | bytes 133333336 | tf_op jit(solution)/shard_map/feed_halve_1/pallas_call | solution.py:871
  264.2 18.0 %attention_gradients_0.1 = (f32[1792,384]{1,0:T(8,128)}, f32[4,2,4,144]{3,2,1,0:T(4,128)}) custom-call(s32[5]{0:T(128)S(1)} %stack.22.refs_0_.ids, s32[4]{0:T(128)S(1)} %convert_reduce_fusion.refs_1_, f32[256,1152]{1,0:T(8,128)} %get-tuple-element.294.refs_2_, f32[128,1152]{1,0:T(8,128)} %get-tuple-element.225.refs_3_, ...), custom_call_target="tpu_custom_call" | custom-call | flops 29192355840 | bytes 88473600 | tf_op jit(solution)/shard_map/attention_gradients_0/pallas_call | solution.py:94
  282.3 21.2 %collective-permute-done.43.refs_2_ = f32[144,1152]{1,0:T(8,128)} collective-permute-done((f32[144,1152]{1,0:T(8,128)}, f32[144,1152]{1,0:T(8,128)}, u32[]{:S(2)}, u32[]{:S(2)}) %collective-permute-start.43) | collective-permute-done | bytes 663584 | tf_op jit(solution)/shard_map/ppermute | solution.py:1336
  305.2 4.5 %feed_halve_0.1 = (f32[144,1152]{1,0:T(8,128)}, f32[144,1152]{1,0:T(8,128)}, f32[4,72,640]{2,1,0:T(8,128)}, f32[4,72,640]{2,1,0:T(8,128)}) custom-call(s32[5]{0:T(128)S(1)} %stack.22.refs_0_.ids, f32[2,144,1152]{2,1,0:T(8,128)} %get-tuple-element.330.refs_29_.outer_keep, f32[2,144,1152]{2,1,0:T(8,128)} %get-tuple-element.341.outer_half, ...), custom_call_target="tpu_custom_call" | custom-call | flops 40000000000 | bytes 133333336 | tf_op jit(solution)/shard_map/feed_halve_0/pallas_call | solution.py:871
  313.7 3.8 collective-permute-start.52
  317.6 3.4 collective-permute-start.54
  321.0 10.6 %collective-permute-done.47.inner_other = f32[4,72,640]{2,1,0:T(8,128)S(1)} collective-permute-done((f32[4,72,640]{2,1,0:T(8,128)}, f32[4,72,640]{2,1,0:T(8,128)S(1)}, u32[]{:S(2)}, u32[]{:S(2)}) %collective-permute-start.47) | collective-permute-done | bytes 737312 | tf_op jit(solution)/shard_map/ppermute | solution.py:1336
  334.8 13.8 %collective-permute-done.52.refs_7_ = f32[36,1152]{1,0:T(8,128)S(1)} collective-permute-done((f32[36,1152]{1,0:T(8,128)}, f32[36,1152]{1,0:T(8,128)S(1)}, u32[]{:S(2)}, u32[]{:S(2)}) %collective-permute-start.52) | collective-permute-done | bytes 165920 | tf_op jit(solution)/shard_map/ppermute | solution.py:988
  348.8 4.4 %collective-permute-start.57 = (f32[32,144]{1,0:T(8,128)S(1)}, f32[32,144]{1,0:T(8,128)S(1)}, u32[]{:S(2)}, u32[]{:S(2)}) collective-permute-start(f32[32,144]{1,0:T(8,128)S(1)} %reshape.123.refs_0_), channel_id=1, source_target_pairs={{0,16},{8,24},{16,0},{24,8},{1,17},{9,25},{17,1},{25,9},{2,18},{10... | collective-permute-start | bytes 55304 | tf_op jit(solution)/shard_map/ppermute | solution.py:1340
  360.0 6.5 %collective-permute-done.49.refs_3_ = f32[72,640]{1,0:T(8,128)S(1)} collective-permute-done((f32[72,640]{1,0:T(8,128)}, f32[72,640]{1,0:T(8,128)S(1)}, u32[]{:S(2)}, u32[]{:S(2)}) %collective-permute-start.49) | collective-permute-done | bytes 184352 | tf_op jit(solution)/shard_map/ppermute | solution.py:1340
  370.7 3.3 collective-permute-start.65
  377.7 6.2 %collective-permute-start.59 = (f32[96,720]{1,0:T(8,128)}, f32[96,720]{1,0:T(8,128)S(1)}, u32[]{:S(2)}, u32[]{:S(2)}) collective-permute-start(f32[96,720]{1,0:T(8,128)} %get-tuple-element.367), channel_id=1, source_target_pairs={{0,2},{2,0},{1,3},{3,1},{4,6},{6,4},{5,7},{7,5},{8,10},{10,8},{9,1... | collective-permute-start | bytes 829448 | tf_op jit(solution)/shard_map/ppermute | solution.py:1336
  388.4 9.6 %collective-permute-done.62.refs_8_ = f32[36,1152]{1,0:T(8,128)S(1)} collective-permute-done((f32[36,1152]{1,0:T(8,128)}, f32[36,1152]{1,0:T(8,128)S(1)}, u32[]{:S(2)}, u32[]{:S(2)}) %collective-permute-start.62) | collective-permute-done | bytes 165920 | tf_op jit(solution)/shard_map/ppermute | solution.py:988
  399.0 6.2 %assemble.1 = (f32[2,3,72,576]{3,2,1,0:T(8,128)}, f32[2,2,72,576]{3,2,1,0:T(8,128)}, f32[2,8,64]{2,1,0:T(8,128)}, f32[2,36,1152]{2,1,0:T(8,128)}, f32[2,72,2304]...) custom-call(s32[5]{0:T(128)S(1)} %stack.22.refs_0_.ids, ...), custom_call_target="tpu_custom_call" | custom-call | flops 40000000000 | bytes 133333336 | tf_op jit(solution)/shard_map/assemble/pallas_call | solution.py:871
  (374 shorter events, 120.0 us)
Async XLA Ops:
  7.2 58.4 %all-gather.5.cloned.1.call-start = ((), (), s32[]{:S(2)}) async-start(), calls=%async_computation.2 | async-start | bytes 5308416 | tf_op jit(solution)/shard_map/all_gather | solution.py:1344
  9.1 116.4 %all-gather.7.cloned.1.call-start = ((), (), s32[]{:S(2)}) async-start(), calls=%async_computation.3 | async-start | bytes 5308416 | tf_op jit(solution)/shard_map/all_gather | solution.py:1344
  66.9 130.9 %all-gather.9.cloned.1.call-start = ((), (), s32[]{:S(2)}) async-start(), calls=%async_computation.4 | async-start | bytes 5308416 | tf_op jit(solution)/shard_map/all_gather | solution.py:1344
  109.9 117.8 %all-gather.11.cloned.1.call-start = ((), (), s32[]{:S(2)}) async-start(), calls=%async_computation.5 | async-start | bytes 5308416 | tf_op jit(solution)/shard_map/all_gather | solution.py:1344
  146.4 135.9 %reduce-scatter.7.cloned.1.call-start = ((), (), s32[]{:S(2)}) async-start(), calls=%async_computation.7 | async-start | bytes 3379200
  168.5 25.8 %collective-permute-start.32 = (f32[128,1152]{1,0:T(8,128)S(1)}, f32[128,1152]{1,0:T(8,128)S(1)}, u32[]{:S(2)}, u32[]{:S(2)}) collective-permute-start(f32[128,1152]{1,0:T(8,128)S(1)} %copy-done.74), channel_id=1, source_target_pairs={{0,2},{2,0},{1,3},{3,1},{4,6},{6,4},{5,7},{7,5},{8,10},{10,8},{9,1... | collective-permute-start | bytes 1769480 | tf_op jit(solution)/shard_map/ppermute | solution.py:1336
  170.0 27.7 %collective-permute-start.33 = (f32[128,1152]{1,0:T(8,128)S(1)}, f32[128,1152]{1,0:T(8,128)S(1)}, u32[]{:S(2)}, u32[]{:S(2)}) collective-permute-start(f32[128,1152]{1,0:T(8,128)S(1)} %copy-done.74), channel_id=1, source_target_pairs={{0,4},{4,0},{1,5},{5,1},{2,6},{6,2},{3,7},{7,3},{8,12},{12,8},{9,1... | collective-permute-start | bytes 1769480 | tf_op jit(solution)/shard_map/ppermute | solution.py:1336
  171.3 32.0 %collective-permute-start.34 = (f32[128,1152]{1,0:T(8,128)S(1)}, f32[128,1152]{1,0:T(8,128)S(1)}, u32[]{:S(2)}, u32[]{:S(2)}) collective-permute-start(f32[128,1152]{1,0:T(8,128)S(1)} %copy-done.74), channel_id=1, source_target_pairs={{0,6},{6,0},{2,4},{4,2},{1,7},{7,1},{3,5},{5,3},{8,14},{14,8},{10,... | collective-permute-start | bytes 1769480 | tf_op jit(solution)/shard_map/ppermute | solution.py:1355
  199.4 22.7 %collective-permute-start.37 = (f32[32,144]{1,0:T(8,128)S(1)}, f32[32,144]{1,0:T(8,128)S(1)}, u32[]{:S(2)}, u32[]{:S(2)}) collective-permute-start(f32[32,144]{1,0:T(8,128)S(1)} %reshape.118.refs_0_), channel_id=1, source_target_pairs={{0,8},{8,16},{16,24},{24,0},{1,9},{9,17},{17,25},{25,1},{2,10},{10... | collective-permute-start | bytes 55304 | tf_op jit(solution)/shard_map/ppermute | solution.py:1340
  199.8 23.6 %collective-permute-start.38 = (f32[32,144]{1,0:T(8,128)S(1)}, f32[32,144]{1,0:T(8,128)S(1)}, u32[]{:S(2)}, u32[]{:S(2)}) collective-permute-start(f32[32,144]{1,0:T(8,128)S(1)} %reshape.118.refs_0_), channel_id=1, source_target_pairs={{0,16},{8,24},{16,0},{24,8},{1,17},{9,25},{17,1},{25,9},{2,18},{10... | collective-permute-start | bytes 55304 | tf_op jit(solution)/shard_map/ppermute | solution.py:1340
  200.4 23.1 %collective-permute-start.39 = (f32[32,144]{1,0:T(8,128)S(1)}, f32[32,144]{1,0:T(8,128)S(1)}, u32[]{:S(2)}, u32[]{:S(2)}) collective-permute-start(f32[32,144]{1,0:T(8,128)S(1)} %reshape.118.refs_0_), channel_id=1, source_target_pairs={{0,24},{8,0},{16,8},{24,16},{1,25},{9,1},{17,9},{25,17},{2,26},{10... | collective-permute-start | bytes 55304 | tf_op jit(solution)/shard_map/ppermute | solution.py:1340
  203.2 20.3 %collective-permute-start.35 = (f32[128,1152]{1,0:T(8,128)}, f32[128,1152]{1,0:T(8,128)S(1)}, u32[]{:S(2)}, u32[]{:S(2)}) collective-permute-start(f32[128,1152]{1,0:T(8,128)} %get-tuple-element.308.refs_10_), channel_id=1, source_target_pairs={{0,1},{1,0},{2,3},{3,2},{4,5},{5,4},{6,7},{7,6},{8,9},{9,8},{10,11... | collective-permute-start | bytes 1769480 | tf_op jit(solution)/shard_map/ppermute | solution.py:1336
  203.2 20.3 %collective-permute-start.36 = (f32[128,1152]{1,0:T(8,128)}, f32[128,1152]{1,0:T(8,128)S(1)}, u32[]{:S(2)}, u32[]{:S(2)}) collective-permute-start(f32[128,1152]{1,0:T(8,128)} %get-tuple-element.309.refs_11_), channel_id=1, source_target_pairs={{0,1},{1,0},{2,3},{3,2},{4,5},{5,4},{6,7},{7,6},{8,9},{9,8},{10,11... | collective-permute-start | bytes 1769480 | tf_op jit(solution)/shard_map/ppermute | solution.py:1336
  221.6 148.2 %reduce-scatter.5.cloned.1.call-start = ((), (), s32[]{:S(2)}) async-start(), calls=%async_computation.6 | async-start | bytes 3440640 | tf_op jit(solution)/shard_map/reduce_scatter | solution.py:1517
  222.1 32.4 %collective-permute-start.41 = (f32[2,144,1152]{2,1,0:T(8,128)}, f32[2,144,1152]{2,1,0:T(8,128)}, u32[]{:S(2)}, u32[]{:S(2)}) collective-permute-start(f32[2,144,1152]{2,1,0:T(8,128)} %get-tuple-element.322), channel_id=1, source_target_pairs={{0,4},{4,0},{1,5},{5,1},{2,6},{6,2},{3,7},{7,3},{8,12},{12,8},{9,1... | collective-permute-start | bytes 3981320 | tf_op jit(solution)/shard_map/ppermute | solution.py:1336
  223.4 35.5 %collective-permute-start.42 = (f32[2,4,72,640]{3,2,1,0:T(8,128)}, f32[2,4,72,640]{3,2,1,0:T(8,128)}, u32[]{:S(2)}, u32[]{:S(2)}) collective-permute-start(f32[2,4,72,640]{3,2,1,0:T(8,128)} %get-tuple-element.323), channel_id=1, source_target_pairs={{0,2},{2,0},{1,3},{3,1},{4,6},{6,4},{5,7},{7,5},{8,10},{10,8},{9,1... | collective-permute-start | bytes 4423688 | tf_op jit(solution)/shard_map/ppermute | solution.py:1336
  227.7 31.2 %collective-permute-start.40 = (f32[128,1152]{1,0:T(8,128)}, f32[128,1152]{1,0:T(8,128)}, u32[]{:S(2)}, u32[]{:S(2)}) collective-permute-start(f32[128,1152]{1,0:T(8,128)} %get-tuple-element.315.refs_12_), channel_id=1, source_target_pairs={{0,1},{1,0},{2,3},{3,2},{4,5},{5,4},{6,7},{7,6},{8,9},{9,8},{10,11... | collective-permute-start | bytes 1769480 | tf_op jit(solution)/shard_map/ppermute | solution.py:1336
  245.9 57.7 %collective-permute-start.45 = (f32[2,144,1152]{2,1,0:T(8,128)}, f32[2,144,1152]{2,1,0:T(8,128)S(1)}, u32[]{:S(2)}, u32[]{:S(2)}) collective-permute-start(f32[2,144,1152]{2,1,0:T(8,128)} %get-tuple-element.339), channel_id=1, source_target_pairs={{0,4},{4,0},{1,5},{5,1},{2,6},{6,2},{3,7},{7,3},{8,12},{12,8},{9,1... | collective-permute-start | bytes 3981320 | tf_op jit(solution)/shard_map/ppermute | solution.py:1336
  247.4 56.1 %collective-permute-start.46 = (f32[2,4,72,640]{3,2,1,0:T(8,128)}, f32[2,4,72,640]{3,2,1,0:T(8,128)S(1)}, u32[]{:S(2)}, u32[]{:S(2)}) collective-permute-start(f32[2,4,72,640]{3,2,1,0:T(8,128)} %get-tuple-element.340), channel_id=1, source_target_pairs={{0,2},{2,0},{1,3},{3,1},{4,6},{6,4},{5,7},{7,5},{8,10},{10,8},{9,1... | collective-permute-start | bytes 4423688 | tf_op jit(solution)/shard_map/ppermute | solution.py:1336
  263.5 40.1 %collective-permute-start.43 = (f32[144,1152]{1,0:T(8,128)}, f32[144,1152]{1,0:T(8,128)}, u32[]{:S(2)}, u32[]{:S(2)}) collective-permute-start(f32[144,1152]{1,0:T(8,128)} %get-tuple-element.337), channel_id=1, source_target_pairs={{0,2},{2,0},{1,3},{3,1},{4,6},{6,4},{5,7},{7,5},{8,10},{10,8},{9,1... | collective-permute-start | bytes 1990664 | tf_op jit(solution)/shard_map/ppermute | solution.py:1336
  263.6 39.9 %collective-permute-start.44 = (f32[4,72,640]{2,1,0:T(8,128)}, f32[4,72,640]{2,1,0:T(8,128)}, u32[]{:S(2)}, u32[]{:S(2)}) collective-permute-start(f32[4,72,640]{2,1,0:T(8,128)} %get-tuple-element.338), channel_id=1, source_target_pairs={{0,4},{4,0},{1,5},{5,1},{2,6},{6,2},{3,7},{7,3},{8,12},{12,8},{9,1... | collective-permute-start | bytes 2211848 | tf_op jit(solution)/shard_map/ppermute | solution.py:1336
  309.6 22.0 %collective-permute-start.47 = (f32[4,72,640]{2,1,0:T(8,128)}, f32[4,72,640]{2,1,0:T(8,128)S(1)}, u32[]{:S(2)}, u32[]{:S(2)}) collective-permute-start(f32[4,72,640]{2,1,0:T(8,128)} %get-tuple-element.345), channel_id=1, source_target_pairs={{0,4},{4,0},{1,5},{5,1},{2,6},{6,2},{3,7},{7,3},{8,12},{12,8},{9,1... | collective-permute-start | bytes 2211848 | tf_op jit(solution)/shard_map/ppermute | solution.py:1336
  310.4 42.8 %collective-permute-start.51 = (f32[144,1152]{1,0:T(8,128)}, f32[144,1152]{1,0:T(8,128)S(1)}, u32[]{:S(2)}, u32[]{:S(2)}) collective-permute-start(f32[144,1152]{1,0:T(8,128)} %get-tuple-element.351), channel_id=1, source_target_pairs={{0,2},{2,0},{1,3},{3,1},{4,6},{6,4},{5,7},{7,5},{8,10},{10,8},{9,1... | collective-permute-start | bytes 1990664 | tf_op jit(solution)/shard_map/ppermute | solution.py:1336
  313.7 34.9 %collective-permute-start.52 = (f32[36,1152]{1,0:T(8,128)}, f32[36,1152]{1,0:T(8,128)S(1)}, u32[]{:S(2)}, u32[]{:S(2)}) collective-permute-start(f32[36,1152]{1,0:T(8,128)} %get-tuple-element.359), channel_id=1, source_target_pairs={{0,0},{2,8},{4,16},{6,24},{8,2},{10,10},{12,18},{14,26},{16,4},{18... | collective-permute-start | bytes 497672 | tf_op jit(solution)/shard_map/ppermute | solution.py:988
  317.5 31.2 %collective-permute-start.53 = (f32[80,720]{1,0:T(8,128)}, f32[80,720]{1,0:T(8,128)S(1)}, u32[]{:S(2)}, u32[]{:S(2)}) collective-permute-start(f32[80,720]{1,0:T(8,128)} %get-tuple-element.361), channel_id=1, source_target_pairs={{0,2},{2,0},{1,3},{3,1},{4,6},{6,4},{5,7},{7,5},{8,10},{10,8},{9,1... | collective-permute-start | bytes 691208 | tf_op jit(solution)/shard_map/ppermute | solution.py:1336
  317.6 31.2 %collective-permute-start.54 = (f32[80,720]{1,0:T(8,128)}, f32[80,720]{1,0:T(8,128)S(1)}, u32[]{:S(2)}, u32[]{:S(2)}) collective-permute-start(f32[80,720]{1,0:T(8,128)} %get-tuple-element.362), channel_id=1, source_target_pairs={{0,4},{4,0},{1,5},{5,1},{2,6},{6,2},{3,7},{7,3},{8,12},{12,8},{9,1... | collective-permute-start | bytes 691208 | tf_op jit(solution)/shard_map/ppermute | solution.py:1336
  331.6 21.6 %collective-permute-start.55 = (f32[80,720]{1,0:T(8,128)}, f32[80,720]{1,0:T(8,128)S(1)}, u32[]{:S(2)}, u32[]{:S(2)}) collective-permute-start(f32[80,720]{1,0:T(8,128)} %get-tuple-element.363), channel_id=1, source_target_pairs={{0,6},{6,0},{2,4},{4,2},{1,7},{7,1},{3,5},{5,3},{8,14},{14,8},{10,... | collective-permute-start | bytes 691208 | tf_op jit(solution)/shard_map/ppermute | solution.py:1355
  348.7 21.1 %collective-permute-start.56 = (f32[32,144]{1,0:T(8,128)S(1)}, f32[32,144]{1,0:T(8,128)S(1)}, u32[]{:S(2)}, u32[]{:S(2)}) collective-permute-start(f32[32,144]{1,0:T(8,128)S(1)} %reshape.123.refs_0_), channel_id=1, source_target_pairs={{0,8},{8,16},{16,24},{24,0},{1,9},{9,17},{17,25},{25,1},{2,10},{10... | collective-permute-start | bytes 55304 | tf_op jit(solution)/shard_map/ppermute | solution.py:1340
  348.8 25.2 %collective-permute-start.57 = (f32[32,144]{1,0:T(8,128)S(1)}, f32[32,144]{1,0:T(8,128)S(1)}, u32[]{:S(2)}, u32[]{:S(2)}) collective-permute-start(f32[32,144]{1,0:T(8,128)S(1)} %reshape.123.refs_0_), channel_id=1, source_target_pairs={{0,16},{8,24},{16,0},{24,8},{1,17},{9,25},{17,1},{25,9},{2,18},{10... | collective-permute-start | bytes 55304 | tf_op jit(solution)/shard_map/ppermute | solution.py:1340
  353.2 20.9 %collective-permute-start.58 = (f32[32,144]{1,0:T(8,128)S(1)}, f32[32,144]{1,0:T(8,128)S(1)}, u32[]{:S(2)}, u32[]{:S(2)}) collective-permute-start(f32[32,144]{1,0:T(8,128)S(1)} %reshape.123.refs_0_), channel_id=1, source_target_pairs={{0,24},{8,0},{16,8},{24,16},{1,25},{9,1},{17,9},{25,17},{2,26},{10... | collective-permute-start | bytes 55304 | tf_op jit(solution)/shard_map/ppermute | solution.py:1340
  367.0 18.4 %collective-permute-start.64 = (f32[72,640]{1,0:T(8,128)}, f32[72,640]{1,0:T(8,128)S(1)}, u32[]{:S(2)}, u32[]{:S(2)}) collective-permute-start(f32[72,640]{1,0:T(8,128)} %get-tuple-element.384), channel_id=1, source_target_pairs={{0,16},{8,24},{16,0},{24,8},{1,17},{9,25},{17,1},{25,9},{2,18},{10... | collective-permute-start | bytes 552968 | tf_op jit(solution)/shard_map/ppermute | solution.py:1340
  377.7 20.3 %collective-permute-start.59 = (f32[96,720]{1,0:T(8,128)}, f32[96,720]{1,0:T(8,128)S(1)}, u32[]{:S(2)}, u32[]{:S(2)}) collective-permute-start(f32[96,720]{1,0:T(8,128)} %get-tuple-element.367), channel_id=1, source_target_pairs={{0,2},{2,0},{1,3},{3,1},{4,6},{6,4},{5,7},{7,5},{8,10},{10,8},{9,1... | collective-permute-start | bytes 829448 | tf_op jit(solution)/shard_map/ppermute | solution.py:1336
  (130 other events, 869.5 us)
Sparse Core Ops, SparseCore 0:
  9.7 52.9 all-gather.4
  67.0 53.1 all-gather.6
  122.4 50.5 all-gather.8
  174.4 53.2 all-gather.10
  229.9 52.1 reduce-scatter.6
  284.2 57.7 reduce-scatter.4

commit v4 on v3

--- a/solution.py
+++ b/solution.py
@@ -15,7 +15,7 @@
 IMAGES = 4
 BLOCK = SPAN // IMAGES
 GROUP = 4
-WEIGHT, GRADIENT_WEIGHT, WHOLE_COST = 10, 6, 40_000_000_000
+WEIGHT, GRADIENT_WEIGHT, WHOLE_COST = 10, 6, 20_000_000_000
 EPSILON = 1e-06
 MASKED = -1e30
 ROOT_HALF = 0.7071067811865476
@@ -893,11 +893,24 @@
     inner_send[...] = inner_keep[1 - col] + inner_half[1 - col]
 
 
-def feed_deal_kernel(line, ids, inner_own, inner_other, *outs):
+def feed_deal_kernel(depth, line, ids, *refs):
+    parts, outs = refs[: 2 * depth], refs[2 * depth :]
     place = ids[AT_LINE]
     for by in range(line):
         to = lax.rem(place + by, line)
-        outs[by][...] = inner_own[to] + inner_other[to]
+        for layer in range(depth):
+            outs[by][layer] = parts[2 * layer][to] + parts[2 * layer + 1][to]
+
+
+def feed_deal(depth, line, ids, parts):
+    block = parts[0].shape[1:]
+    return whole_call(
+        functools.partial(feed_deal_kernel, depth, line),
+        "feed_deal",
+        (ids,),
+        parts,
+        [shape_of((depth, *block))] * line,
+    )
 
 
 def feed_scatter(layer, ids, pieces, line):
@@ -912,15 +925,7 @@
         [outer_part, outer_part, inner_part, inner_part],
     )
     outer_other, inner_other = yield [swap(outer_send, "row"), swap(inner_send, "col")]
-    own, *rest = whole_call(
-        functools.partial(feed_deal_kernel, line),
-        f"feed_deal_{layer}",
-        (ids,),
-        (inner_own, inner_other),
-        [shape_of(inner_own.shape[1:])] * line,
-    )
-    far = yield [shift(rest[by - 1], line, by) for by in range(1, line)]
-    return [own, *far], [outer_own, outer_other]
+    return [inner_own, inner_other], [outer_own, outer_other]
 
 
 def attention_deal_kernel(layer, line, heads, at_rows, ids, summed, embedded, *refs):
@@ -999,33 +1004,48 @@
     return projection, [blocks[0], across, along, corner]
 
 
-def assemble_kernel(depth, line, heads, ids, *refs):
+def join_feed_kernel(depth, line, ids, *refs):
+    inners, outers, (inner, outer, order) = refs[:line], refs[line : line + 2 * depth], refs[line + 2 * depth :]
+    part = inner.shape[2] // line
+    offsets = line_window(inner.shape[2], line)[1]
+    for by in range(line):
+        order[lax.rem(ids[AT_LINE] + line - by, line)] = inners[by][...]
+    for layer in range(depth):
+        outer[layer] = outers[2 * layer][...] + outers[2 * layer + 1][...]
+        for z in range(line):
+            inner[layer, :, z * part : (z + 1) * part] = order[
+                z, layer, :, offsets[z] : offsets[z] + part
+            ]
+
+
+def join_feed(line, ids, blocks, outers, units):
+    depth, features, size = blocks[0].shape
+    rows, width = outers[0].shape
+    return whole_call(
+        functools.partial(join_feed_kernel, depth, line),
+        "join_feed",
+        (ids,),
+        (*blocks, *outers),
+        [shape_of((depth, features, units)), shape_of((depth, rows, width))],
+        [pltpu.VMEM((line, depth, features, size), FULL)],
+    )
+
+
+def join_attention_kernel(depth, heads, ids, *refs):
     blocks, refs = refs[: depth * GROUP], refs[depth * GROUP :]
     projections, refs = refs[:depth], refs[depth:]
-    inners, refs = refs[: depth * line], refs[depth * line :]
-    outers, refs = refs[: 2 * depth], refs[2 * depth :]
-    token, time, table, projection, inner, outer, gain, shift_out, bias, sorted_inner = refs
+    token, time, table, projection, gain, shift_out, bias = refs
     features, local = token.shape[2:]
     own = local // GROUP
-    units = inner.shape[2]
-    part = units // line
-    offsets = line_window(units, line)[1]
     entries = table.shape[2]
     at = 2 * ids[AT_COL] + ids[AT_ROW]
-    place = ids[AT_LINE]
     for layer in range(depth):
-        projection[layer] = projections[layer][...]
-        outer[layer] = outers[2 * layer][...] + outers[2 * layer + 1][...]
-        for by in range(line):
-            sorted_inner[lax.rem(place + line - by, line)] = inners[layer * line + by][...]
-        for z in range(line):
-            inner[layer, :, z * part : (z + 1) * part] = sorted_inner[
-                z, :, offsets[z] : offsets[z] + part
-            ]
-        for j in range(GROUP):
-
-            @pl.when(at == j)
-            def _(j=j, layer=layer):
+        projection[:, layer, :] = projections[layer][...]
+    for j in range(GROUP):
+
+        @pl.when(at == j)
+        def _(j=j):
+            for layer in range(depth):
                 for by in range(GROUP):
                     ref, source = blocks[layer * GROUP + by], j ^ by
                     lanes = slice(source * own, (source + 1) * own)
@@ -1051,32 +1071,26 @@
             out[layer] = total[begin : begin + 2]
 
 
-def assemble(depth, line, ids, attention, feeds, heads, local, units, width):
+def join_attention(depth, line, ids, attention, heads, local, width):
     features = width // (GROUP * line)
     vector = shape_of((depth, 2, features))
-    size = line_window(units, line)[2]
     return whole_call(
-        functools.partial(assemble_kernel, depth, line, heads // GROUP),
-        "assemble",
+        functools.partial(join_attention_kernel, depth, heads // GROUP),
+        "join_attention",
         (ids,),
         (
             *[block for layer in range(depth) for block in attention[layer][1]],
             *[attention[layer][0] for layer in range(depth)],
-            *[block for layer in range(depth) for block in feeds[layer][0]],
-            *[part for layer in range(depth) for part in feeds[layer][1]],
         ),
         [
             shape_of((depth, 3, features, local)),
             shape_of((depth, 2, features, local)),
             shape_of((depth, heads, 4 * SPAN // (GROUP * line))),
-            shape_of((depth, local // (GROUP * line), width)),
-            shape_of((depth, features, units)),
-            shape_of((depth, units // (GROUP * line), width)),
+            shape_of((local // (GROUP * line), depth, width)),
             vector,
             vector,
             vector,
         ],
-        [pltpu.VMEM((line, features, size), FULL)],
     )
 
 
@@ -1344,7 +1358,11 @@
     return lax.all_gather(half, ("line", "tensor"), tiled=True)
 
 
-def plane_steps(value, half):
+def plane_steps(value, half, slow=False):
+    if slow:
+        far = yield [swap(half, "row"), swap(half, "col"), swap_corner(half)]
+        others = yield [swap(part, "tensor") for part in far]
+        return [value, *far, *others]
     across, along = yield [swap(half, "row"), swap(half, "col")]
     corner, *others = yield [swap_corner(half), swap(across, "tensor"), swap(along, "tensor")]
     others += yield [swap(corner, "tensor")]
@@ -1479,11 +1497,12 @@
             back_partial, other, gathered_line[0] = moves.chain(back_partial, [saved[0][4]])
         else:
             back_partial, other = moves.chain(back_partial)
-        moves.start(("branch", layer), plane_steps(back_middle, half))
+        moves.start(("branch", layer), plane_steps(back_middle, half, layer == 0))
         upstream = (back_middle, back_partial, other, held)
         vectors[layer] = (feed_sums, middle_sums)
         gathered[layer] = gathered_up
     gradient_tokens, last_sums = finish(*upstream, norm_gain)
+    gathered_line[depth - 1] = saved[depth - 1][4]
     sums = [last_sums, *[pair[0] for pair in vectors], *[pair[1] for pair in vectors]]
     packed = moves.found["packed"]
     tokens_of = {}
@@ -1520,10 +1539,10 @@
         return turn, due
 
     top = depth - 1
-    turn, (gathered_line[top],) = run_attention(top, (), [saved[top][4]])
-    turn, (gathered[0],) = run_feed(top, (turn,), [gathered[0]])
-    turn, _ = run_feed(0, (turn,))
-    _, (tokens_of[top],) = run_attention(0, (turn,), [tokens_of[top]])
+    turn, _ = run_feed(top, (last_sums,))
+    turn, (gathered[0],) = run_attention(top, (turn,), [gathered[0]])
+    turn, _ = run_attention(0, (turn,))
+    _, (tokens_of[top],) = run_feed(0, (turn,), [tokens_of[top]])
     every = jnp.concatenate([part[:GROUP, :IMAGES].reshape(-1) for part in moves.found["info"]])
     embedded_every = sinusoid(every, own_feature, width)
     def deal(layer):
@@ -1546,23 +1565,26 @@
         deal(layer)
     moves.hurry(("images", 0))
     moves.finish()
-    others = [moves.found["feed", 0], moves.found["attention", depth - 1]]
-    held, others = jax.tree.flatten(others)
-    tokens_of[0], *held = gate([tokens_of[0], *held])
-    moves.found["feed", 0], moves.found["attention", depth - 1] = jax.tree.unflatten(others, held)
+    feeds = [moves.found["feed", layer] for layer in range(depth)]
+    blocks = feed_deal(depth, line, ids, [part for inner, _ in feeds for part in inner])
+    tokens_of[0], own_block, first_block, *blocks = gate(
+        [tokens_of[0], blocks[0], shift(blocks[1], line), *blocks[2:]]
+    )
+    blocks = [own_block, first_block, *[shift(block, line, by) for by, block in enumerate(blocks, 2)]]
     deal(0)
     moves.finish()
-    token, time, table, projection, inner, outer, gain, shifts, bias = assemble(
+    token, time, table, projection, gain, shifts, bias = join_attention(
         depth,
         line,
         ids,
         [moves.found["attention", layer] for layer in range(depth)],
-        [moves.found["feed", layer] for layer in range(depth)],
         heads,
         local_width,
-        units,
         width,
     )
+    projection = jnp.swapaxes(projection, 0, 1)
+    gain, *blocks = gate([gain, *blocks])
+    inner, outer = join_feed(line, ids, blocks, [part for _, outer in feeds for part in outer], units)
     return (
         output,
         gradient_tokens,

time: 421 us -> 418 us (level)
  starting transfers between devices: 68.5 us -> 58.2 us
  waiting for transfers between devices: 108 us -> 115 us
    ppermute x15 -> x12, starting transfers between devices: 21.7 us -> 15.3 us  [shift(): lax.ppermute(value, 'line', [(i, (i + by) % line) for i in range(line)])]
    ppermute x15 -> x12, waiting for transfers between devices: 9.82 us -> 14.2 us  [shift(): lax.ppermute(value, 'line', [(i, (i + by) % line) for i in range(line)])]
    unnamed x181 -> x178, local copies, waits for them, and re-layouts: 24.5 us -> 27.1 us
  transfers between devices with their start and end apart: 72 -> 69, of which waited for: 26 -> 26; matrix products, arithmetic and copies ran while one was open for 3% -> 3% of each run, Pallas kernels for 43% -> 44%
where the time goes in v4:
time: 418 us; the launch traced here: 413 us
  Pallas kernels  185 us (44%)
  waiting for transfers between devices  115 us (28%)
  starting transfers between devices  58.2 us (14%)
  local copies, waits for them, and re-layouts  31.6 us (8%)
  between operations  15.2 us (4%)
  other arithmetic  4.91 us (1%)
    pallas_call x9, Pallas kernels, plain(): pl.pallas_call(body, in_specs=[*[pl.BlockSpec(memory_space=pltpu.SMEM)] *...  82.9 us
    pallas_call x4, Pallas kernels, call(): return lambda *operands: made(*operands, *map(in_hbm, after))  71.7 us
    ppermute x42, waiting for transfers between devices, swap(): return lax.ppermute(value, axis, [(0, 1), (1, 0)])  65.5 us
    ppermute x42, starting transfers between devices, swap(): return lax.ppermute(value, axis, [(0, 1), (1, 0)])  27.5 us
    unnamed x178, local copies, waits for them, and re-layouts  27.1 us
    ppermute x2, waiting for transfers between devices, attention_deal(): lax.ppermute(projection, LINES, [(GROUP * z + j, line * j + z) for z in r...  26.8 us
    pallas_call x7, Pallas kernels, whole_call(): pl.pallas_call(kernel, in_specs=[*[pl.BlockSpec(memory_space=pltpu.SMEM)]...  25.8 us
    ppermute x12, starting transfers between devices, shift(): lax.ppermute(value, 'line', [(i, (i + by) % line) for i in range(line)])  15.3 us
  transfers between devices with their start and end apart: 69, of which 26 were waited for; matrix products, arithmetic and copies ran while one was open for 3% of the time, Pallas kernels for 44%

profile of v4, /device:TPU:2, one launch (start us, length us, event | category | flops | bytes accessed | tf_op | source)
XLA Modules:
  0.0 413.4 jit_solution(9762512618872009683)
XLA Ops:
  9.8 4.2 %convolution_bitcast_fusion.refs_7_.refs_9_ = f32[2,2,4,576]{3,2,1,0:T(4,128)S(1)} fusion(bf16[2,2,1152,576]{2,3,1,0:T(8,128)(2,1)} %param.19, f32[1152]{0:T(1024)S(1)} %fusion.11, f32[4]{0:T(128)S(1)} %convert_bitcast_fusion, pred[1152]{0:T(1024)(128)(4,1)S(1)} %iota_compare_fusion.1), kind=kOutput, calls=%fused_computation.1 | convolution fusion | flops 21247488 | bytes 5351056 | tf_op jit(solution)/shard_map/dot_general | solution.py:1415
  18.3 4.3 %expand_table.1 = (f32[16,16,512]{2,1,0:T(8,128)}, f32[16,8,128]{2,1,0:T(8,128)}) custom-call(f32[16,1024]{1,0:T(8,128)} %bitcast.24), custom_call_target="tpu_custom_call" | custom-call | tf_op jit(solution)/shard_map/expand_table/pallas_call | solution.py:136
  23.4 8.2 %attend_0.1 = (f32[256,1152]{1,0:T(8,128)}, f32[256,1152]{1,0:T(8,128)}, f32[128,1152]{1,0:T(8,128)}, bf16[3,256,576]{2,1,0:T(8,128)(2,1)}, f32[256,1152]{1,0:T(8,128)}, /*index=5*/f32[8,256,256]{2,1,0:T(8,128)}) custom-call(s32[5]{0:T(128)S(1)} %stack.22.refs_0_.ids, f32[2,2,1152]{2,1,0:T(2,128)S(1)} %copy-done, f32[2,2,1152]{2,1,0:T(2,128)S(1)} %copy-done.5, ...), custom_call_target="tpu_custom_call" | custom-call | flops 13589544960 | bytes 100270080 | tf_op jit(solution)/shard_map/attend_0/pallas_call | solution.py:295
  36.4 9.6 %feed_0.1 = (f32[256,1152]{1,0:T(8,128)}, f32[128,1152]{1,0:T(8,128)}, f32[256,2304]{1,0:T(8,128)}, f32[256,1152]{1,0:T(8,128)}) custom-call(s32[5]{0:T(128)S(1)} %stack.22.refs_0_.ids, f32[2,2,1152]{2,1,0:T(2,128)S(1)} %copy-done, f32[2,2,1152]{2,1,0:T(2,128)S(1)} %copy-done.5, f32[2,2,1152]{2,1,0:T(2,128)S(1)} %copy-done.1, ...), custom_call_target="tpu_custom_call" | custom-call | flops 27179089920 | bytes 200540160 | tf_op jit(solution)/shard_map/feed_0/pallas_call | solution.py:295
  53.7 9.3 %attend_1.1 = (f32[256,1152]{1,0:T(8,128)}, f32[256,1152]{1,0:T(8,128)}, f32[128,1152]{1,0:T(8,128)}, bf16[3,256,576]{2,1,0:T(8,128)(2,1)}, f32[256,1152]{1,0:T(8,128)}, /*index=5*/f32[8,256,256]{2,1,0:T(8,128)}) custom-call(s32[5]{0:T(128)S(1)} %stack.22.refs_0_.ids, f32[2,2,1152]{2,1,0:T(2,128)S(1)} %copy-done, f32[2,2,1152]{2,1,0:T(2,128)S(1)} %copy-done.5, ...), custom_call_target="tpu_custom_call" | custom-call | flops 13589544960 | bytes 100270080 | tf_op jit(solution)/shard_map/attend_1/pallas_call | solution.py:295
  77.6 9.5 %feed_1.1 = (f32[256,1152]{1,0:T(8,128)}, f32[128,1152]{1,0:T(8,128)}, f32[256,2304]{1,0:T(8,128)}, f32[256,1152]{1,0:T(8,128)}) custom-call(s32[5]{0:T(128)S(1)} %stack.22.refs_0_.ids, f32[2,2,1152]{2,1,0:T(2,128)S(1)} %copy-done, f32[2,2,1152]{2,1,0:T(2,128)S(1)} %copy-done.5, f32[2,2,1152]{2,1,0:T(2,128)S(1)} %copy-done.1, ...), custom_call_target="tpu_custom_call" | custom-call | flops 27179089920 | bytes 200540160 | tf_op jit(solution)/shard_map/feed_1/pallas_call | solution.py:295
  96.5 9.1 %feed_back_1.1 = (f32[256,1152]{1,0:T(8,128)}, f32[128,1152]{1,0:T(8,128)}, f32[8,1152]{1,0:T(8,128)}, f32[256,1152]{1,0:T(8,128)}) custom-call(s32[5]{0:T(128)S(1)} %stack.22.refs_0_.ids, f32[2,2,1152]{2,1,0:T(2,128)S(1)} %copy-done, bf16[256,1152]{1,0:T(8,128)(2,1)} %refs_2_.9, f32[256,2304]{1,0:T(8,128)} %get-tuple-element.245.refs_3_, ...), custom_call_target="tpu_custom_call" | custom-call | flops 27179089920 | bytes 200540160 | tf_op jit(solution)/shard_map/feed_back_1/pallas_call | solution.py:295
  105.6 3.0 collective-permute-done.18.refs_1_
  114.0 11.3 %attend_back_1.1 = (f32[256,1152]{1,0:T(8,128)}, f32[128,1152]{1,0:T(8,128)}, f32[8,1152]{1,0:T(8,128)}, f32[256,1152]{1,0:T(8,128)}) custom-call(s32[5]{0:T(128)S(1)} %stack.22.refs_0_.ids, f32[2,2,1152]{2,1,0:T(2,128)S(1)} %copy-done, f32[256,1152]{1,0:T(8,128)} %get-tuple-element.246.refs_2_, f32[256,1152]{1,0:T(8,128)} %get-tuple-element.254.refs_3_, ...), custom_call_target="tpu_custom_call" | custom-call | flops 35064381440 | bytes 123863040 | tf_op jit(solution)/shard_map/attend_back_1/pallas_call | solution.py:295
  130.3 10.2 %feed_back_0.1 = (f32[256,1152]{1,0:T(8,128)}, f32[128,1152]{1,0:T(8,128)}, f32[8,1152]{1,0:T(8,128)}, f32[256,1152]{1,0:T(8,128)}) custom-call(s32[5]{0:T(128)S(1)} %stack.22.refs_0_.ids, f32[2,2,1152]{2,1,0:T(2,128)S(1)} %copy-done, f32[256,1152]{1,0:T(8,128)} %get-tuple-element.258.refs_2_.refs_9_, f32[256,1152]{1,0:T(8,128)} %get-tuple-element.265.refs_3_, ...), custom_call_target="tpu_custom_call" | custom-call | flops 27179089920 | bytes 200540160 | tf_op jit(solution)/shard_map/feed_back_0/pallas_call | solution.py:295
  148.6 11.4 %attend_back_0.1 = (f32[256,1152]{1,0:T(8,128)}, f32[128,1152]{1,0:T(8,128)}, f32[8,1152]{1,0:T(8,128)}, f32[256,1152]{1,0:T(8,128)}) custom-call(s32[5]{0:T(128)S(1)} %stack.22.refs_0_.ids, f32[2,2,1152]{2,1,0:T(2,128)S(1)} %copy-done, f32[256,1152]{1,0:T(8,128)} %get-tuple-element.268.refs_2_, f32[256,1152]{1,0:T(8,128)} %get-tuple-element.274.refs_3_, ...), custom_call_target="tpu_custom_call" | custom-call | flops 35064381440 | bytes 123863040 | tf_op jit(solution)/shard_map/attend_back_0/pallas_call | solution.py:295
  167.3 4.2 %finish.1 = (bf16[256,1152]{1,0:T(8,128)(2,1)}, f32[8,1152]{1,0:T(8,128)}) custom-call(f32[2,2,1152]{2,1,0:T(2,128)S(1)} %copy-done, f32[256,1152]{1,0:T(8,128)} %get-tuple-element.278.refs_1_.refs_9_, f32[256,1152]{1,0:T(8,128)} %get-tuple-element.286.refs_2_, f32[256,1152]{1,0:T(8,128)} %get-tuple-element.287.refs_3_, f32[256,1152]{1,0:T(8,128)} %get-tuple-element.202.refs_4_), custom_call_target="tpu_custom_call" | custom-call | bytes 58982400 | tf_op jit(solution)/shard_map/finish/pallas_call | solution.py:295
  173.1 17.9 %feed_gradients_1.1 = (f32[2,144,1152]{2,1,0:T(8,128)}, f32[2,144,1152]{2,1,0:T(8,128)}, f32[2,4,72,640]{3,2,1,0:T(8,128)}, f32[2,4,72,640]{3,2,1,0:T(8,128)}) custom-call(s32[5]{0:T(128)S(1)} %stack.22.refs_0_.ids, f32[1024,1152]{1,0:T(8,128)} %all-gather.9.cloned.1.call-done.refs_1_, f32[1024,1152]{1,0:T(8,128)} %get-tuple-element.294.refs_2_, ...), custom_call_target="tpu_custom_call" | custom-call | flops 36238786560 | bytes 127401984 | tf_op jit(solution)/shard_map/feed_gradients_1/pallas_call | solution.py:94
  195.9 17.5 %attention_gradients_1.1 = (f32[1760,384]{1,0:T(8,128)}, f32[4,2,4,144]{3,2,1,0:T(4,128)}) custom-call(s32[5]{0:T(128)S(1)} %stack.22.refs_0_.ids, s32[4]{0:T(128)S(1)} %convert_reduce_fusion.refs_1_, f32[256,1152]{1,0:T(8,128)} %get-tuple-element.302.refs_2_, f32[128,1152]{1,0:T(8,128)} %get-tuple-element.248.refs_3_, ...), custom_call_target="tpu_custom_call" | custom-call | flops 29192355840 | bytes 88473600 | tf_op jit(solution)/shard_map/attention_gradients_1/pallas_call | solution.py:94
  213.5 9.1 %collective-permute-done.38.refs_5_ = f32[2,144,1152]{2,1,0:T(8,128)S(1)} collective-permute-done((f32[2,144,1152]{2,1,0:T(8,128)}, f32[2,144,1152]{2,1,0:T(8,128)S(1)}, u32[]{:S(2)}, u32[]{:S(2)}) %collective-permute-start.38) | collective-permute-done | bytes 1327136 | tf_op jit(solution)/shard_map/ppermute | solution.py:1350
  222.6 5.2 %collective-permute-done.39.refs_6_ = f32[2,4,72,640]{3,2,1,0:T(8,128)S(1)} collective-permute-done((f32[2,4,72,640]{3,2,1,0:T(8,128)}, f32[2,4,72,640]{3,2,1,0:T(8,128)S(1)}, u32[]{:S(2)}, u32[]{:S(2)}) %collective-permute-start.39) | collective-permute-done | bytes 1474592 | tf_op jit(solution)/shard_map/ppermute | solution.py:1350
  234.0 4.5 %feed_halve_1.1 = (f32[144,1152]{1,0:T(8,128)}, f32[144,1152]{1,0:T(8,128)}, f32[4,72,640]{2,1,0:T(8,128)}, f32[4,72,640]{2,1,0:T(8,128)}) custom-call(s32[5]{0:T(128)S(1)} %stack.22.refs_0_.ids, f32[2,144,1152]{2,1,0:T(8,128)} %get-tuple-element.309.refs_24_.outer_keep, f32[2,144,1152]{2,1,0:T(8,128)} %get-tuple-element.326.outer_half, ...), custom_call_target="tpu_custom_call" | custom-call | flops 20000000000 | bytes 66666664 | tf_op jit(solution)/shard_map/feed_halve_1/pallas_call | solution.py:871
  239.6 18.4 %attention_gradients_0.1 = (f32[1792,384]{1,0:T(8,128)}, f32[4,2,4,144]{3,2,1,0:T(4,128)}) custom-call(s32[5]{0:T(128)S(1)} %stack.22.refs_0_.ids, s32[4]{0:T(128)S(1)} %convert_reduce_fusion.refs_1_, f32[256,1152]{1,0:T(8,128)} %get-tuple-element.289.refs_2_, f32[128,1152]{1,0:T(8,128)} %get-tuple-element.220.refs_3_, ...), custom_call_target="tpu_custom_call" | custom-call | flops 29192355840 | bytes 88473600 | tf_op jit(solution)/shard_map/attention_gradients_0/pallas_call | solution.py:94
  259.1 17.8 %feed_gradients_0.1 = (f32[2,144,1152]{2,1,0:T(8,128)}, f32[2,144,1152]{2,1,0:T(8,128)}, f32[2,4,72,640]{3,2,1,0:T(8,128)}, f32[2,4,72,640]{3,2,1,0:T(8,128)}) custom-call(s32[5]{0:T(128)S(1)} %stack.22.refs_0_.ids, f32[1024,1152]{1,0:T(8,128)} %get-tuple-element.323.refs_1_, f32[1024,1152]{1,0:T(8,128)} %get-tuple-element.324.refs_2_, ...), custom_call_target="tpu_custom_call" | custom-call | flops 36238786560 | bytes 127401984 | tf_op jit(solution)/shard_map/feed_gradients_0/pallas_call | solution.py:94
  286.9 20.7 %collective-permute-done.48.outer_half = f32[2,144,1152]{2,1,0:T(8,128)S(1)} collective-permute-done((f32[2,144,1152]{2,1,0:T(8,128)}, f32[2,144,1152]{2,1,0:T(8,128)S(1)}, u32[]{:S(2)}, u32[]{:S(2)}) %collective-permute-start.48) | collective-permute-done | bytes 1327136 | tf_op jit(solution)/shard_map/ppermute | solution.py:1350
  310.7 4.6 %feed_halve_0.1 = (f32[144,1152]{1,0:T(8,128)}, f32[144,1152]{1,0:T(8,128)}, f32[4,72,640]{2,1,0:T(8,128)}, f32[4,72,640]{2,1,0:T(8,128)}) custom-call(s32[5]{0:T(128)S(1)} %stack.22.refs_0_.ids, f32[2,144,1152]{2,1,0:T(8,128)} %get-tuple-element.334.outer_keep, f32[2,144,1152]{2,1,0:T(8,128)} %copy-done.72, ...), custom_call_target="tpu_custom_call" | custom-call | flops 20000000000 | bytes 66666664 | tf_op jit(solution)/shard_map/feed_halve_0/pallas_call | solution.py:871
  318.0 13.2 %collective-permute-done.50.refs_1_ = f32[4,72,640]{2,1,0:T(8,128)S(1)} collective-permute-done((f32[4,72,640]{2,1,0:T(8,128)}, f32[4,72,640]{2,1,0:T(8,128)S(1)}, u32[]{:S(2)}, u32[]{:S(2)}) %collective-permute-start.50) | collective-permute-done | bytes 737312 | tf_op jit(solution)/shard_map/ppermute | solution.py:1350
  332.1 3.1 feed_deal.1
  342.3 4.2 %collective-permute-start.59 = (f32[36,1152]{1,0:T(8,128)}, f32[36,1152]{1,0:T(8,128)S(1)}, u32[]{:S(2)}, u32[]{:S(2)}) collective-permute-start(f32[36,1152]{1,0:T(8,128)} %get-tuple-element.366), channel_id=1, source_target_pairs={{0,0},{2,8},{4,16},{6,24},{8,2},{10,10},{12,18},{14,26},{16,4},{18... | collective-permute-start | bytes 497672 | tf_op jit(solution)/shard_map/ppermute | solution.py:993
  347.4 3.1 attention_deal_0.1
  350.4 7.3 %collective-permute-done.59.refs_9_ = f32[36,1152]{1,0:T(8,128)S(1)} collective-permute-done((f32[36,1152]{1,0:T(8,128)}, f32[36,1152]{1,0:T(8,128)S(1)}, u32[]{:S(2)}, u32[]{:S(2)}) %collective-permute-start.59) | collective-permute-done | bytes 165920 | tf_op jit(solution)/shard_map/ppermute | solution.py:993
  361.0 2.9 collective-permute-start.62
  363.9 19.6 %collective-permute-done.58.refs_8_ = f32[36,1152]{1,0:T(8,128)S(1)} collective-permute-done((f32[36,1152]{1,0:T(8,128)}, f32[36,1152]{1,0:T(8,128)S(1)}, u32[]{:S(2)}, u32[]{:S(2)}) %collective-permute-start.58) | collective-permute-done | bytes 165920 | tf_op jit(solution)/shard_map/ppermute | solution.py:993
  384.4 3.7 join_attention.1
  388.2 7.7 %collective-permute-done.60.refs_3_ = f32[2,72,640]{2,1,0:T(8,128)S(1)} collective-permute-done((f32[2,72,640]{2,1,0:T(8,128)S(1)}, f32[2,72,640]{2,1,0:T(8,128)S(1)}, u32[]{:S(2)}, u32[]{:S(2)}) %collective-permute-start.60) | collective-permute-done | bytes 368672 | tf_op jit(solution)/shard_map/ppermute | solution.py:1354
  395.9 4.9 %collective-permute-done.61.refs_4_ = f32[2,72,640]{2,1,0:T(8,128)S(1)} collective-permute-done((f32[2,72,640]{2,1,0:T(8,128)S(1)}, f32[2,72,640]{2,1,0:T(8,128)S(1)}, u32[]{:S(2)}, u32[]{:S(2)}) %collective-permute-start.61) | collective-permute-done | bytes 368672 | tf_op jit(solution)/shard_map/ppermute | solution.py:1354
  402.4 3.9 join_feed.1
  (366 shorter events, 114.5 us)
Async XLA Ops:
  7.2 58.6 %all-gather.5.cloned.1.call-start = ((), (), s32[]{:S(2)}) async-start(), calls=%async_computation.2 | async-start | bytes 5308416 | tf_op jit(solution)/shard_map/all_gather | solution.py:1358
  9.1 116.2 %all-gather.7.cloned.1.call-start = ((), (), s32[]{:S(2)}) async-start(), calls=%async_computation.3 | async-start | bytes 5308416 | tf_op jit(solution)/shard_map/all_gather | solution.py:1358
  14.7 16.9 %collective-permute-start = (f32[24,576]{1,0:T(8,128)S(1)}, f32[24,576]{1,0:T(8,128)S(1)}, u32[]{:S(2)}, u32[]{:S(2)}) collective-permute-start(f32[24,576]{1,0:T(8,128)S(1)} %select_maximum_fusion.refs_18_), channel_id=1, source_target_pairs={{0,2},{2,0},{1,3},{3,1},{4,6},{6,4},{5,7},{7,5},{8,10},{10,8},{9,1... | collective-permute-start | bytes 165896 | tf_op jit(solution)/shard_map/ppermute | solution.py:1350
  67.0 106.1 %all-gather.9.cloned.1.call-start = ((), (), s32[]{:S(2)}) async-start(), calls=%async_computation.4 | async-start | bytes 5308416 | tf_op jit(solution)/shard_map/all_gather | solution.py:1358
  109.8 118.1 %all-gather.11.cloned.1.call-start = ((), (), s32[]{:S(2)}) async-start(), calls=%async_computation.5 | async-start | bytes 5308416 | tf_op jit(solution)/shard_map/all_gather | solution.py:1358
  146.2 138.5 %reduce-scatter.7.cloned.1.call-start = ((), (), s32[]{:S(2)}) async-start(), calls=%async_computation.7 | async-start | bytes 3379200
  162.8 29.9 %collective-permute-start.32 = (f32[128,1152]{1,0:T(8,128)}, f32[128,1152]{1,0:T(8,128)S(1)}, u32[]{:S(2)}, u32[]{:S(2)}) collective-permute-start(f32[128,1152]{1,0:T(8,128)} %get-tuple-element.298), channel_id=1, source_target_pairs={{0,2},{2,0},{1,3},{3,1},{4,6},{6,4},{5,7},{7,5},{8,10},{10,8},{9,1... | collective-permute-start | bytes 1769480 | tf_op jit(solution)/shard_map/ppermute | solution.py:1350
  164.3 29.7 %collective-permute-start.33 = (f32[128,1152]{1,0:T(8,128)}, f32[128,1152]{1,0:T(8,128)}, u32[]{:S(2)}, u32[]{:S(2)}) collective-permute-start(f32[128,1152]{1,0:T(8,128)} %get-tuple-element.298), channel_id=1, source_target_pairs={{0,4},{4,0},{1,5},{5,1},{2,6},{6,2},{3,7},{7,3},{8,12},{12,8},{9,1... | collective-permute-start | bytes 1769480 | tf_op jit(solution)/shard_map/ppermute | solution.py:1350
  165.6 28.4 %collective-permute-start.34 = (f32[128,1152]{1,0:T(8,128)}, f32[128,1152]{1,0:T(8,128)}, u32[]{:S(2)}, u32[]{:S(2)}) collective-permute-start(f32[128,1152]{1,0:T(8,128)} %get-tuple-element.298), channel_id=1, source_target_pairs={{0,6},{6,0},{2,4},{4,2},{1,7},{7,1},{3,5},{5,3},{8,14},{14,8},{10,... | collective-permute-start | bytes 1769480 | tf_op jit(solution)/shard_map/ppermute | solution.py:1373
  167.3 26.7 %collective-permute-start.31 = (f32[128,1152]{1,0:T(8,128)}, f32[128,1152]{1,0:T(8,128)S(1)}, u32[]{:S(2)}, u32[]{:S(2)}) collective-permute-start(f32[128,1152]{1,0:T(8,128)} %get-tuple-element.297.refs_12_), channel_id=1, source_target_pairs={{0,1},{1,0},{2,3},{3,2},{4,5},{5,4},{6,7},{7,6},{8,9},{9,8},{10,11... | collective-permute-start | bytes 1769480 | tf_op jit(solution)/shard_map/ppermute | solution.py:1350
  191.1 31.5 %collective-permute-start.38 = (f32[2,144,1152]{2,1,0:T(8,128)}, f32[2,144,1152]{2,1,0:T(8,128)S(1)}, u32[]{:S(2)}, u32[]{:S(2)}) collective-permute-start(f32[2,144,1152]{2,1,0:T(8,128)} %get-tuple-element.312), channel_id=1, source_target_pairs={{0,4},{4,0},{1,5},{5,1},{2,6},{6,2},{3,7},{7,3},{8,12},{12,8},{9,1... | collective-permute-start | bytes 3981320 | tf_op jit(solution)/shard_map/ppermute | solution.py:1350
  193.4 34.4 %collective-permute-start.39 = (f32[2,4,72,640]{3,2,1,0:T(8,128)}, f32[2,4,72,640]{3,2,1,0:T(8,128)S(1)}, u32[]{:S(2)}, u32[]{:S(2)}) collective-permute-start(f32[2,4,72,640]{3,2,1,0:T(8,128)} %get-tuple-element.313), channel_id=1, source_target_pairs={{0,2},{2,0},{1,3},{3,1},{4,6},{6,4},{5,7},{7,5},{8,10},{10,8},{9,1... | collective-permute-start | bytes 4423688 | tf_op jit(solution)/shard_map/ppermute | solution.py:1350
  194.8 18.7 %collective-permute-start.35 = (f32[128,1152]{1,0:T(8,128)}, f32[128,1152]{1,0:T(8,128)}, u32[]{:S(2)}, u32[]{:S(2)}) collective-permute-start(f32[128,1152]{1,0:T(8,128)} %get-tuple-element.299.refs_10_), channel_id=1, source_target_pairs={{0,1},{1,0},{2,3},{3,2},{4,5},{5,4},{6,7},{7,6},{8,9},{9,8},{10,11... | collective-permute-start | bytes 1769480 | tf_op jit(solution)/shard_map/ppermute | solution.py:1350
  194.8 18.7 %collective-permute-start.36 = (f32[128,1152]{1,0:T(8,128)}, f32[128,1152]{1,0:T(8,128)}, u32[]{:S(2)}, u32[]{:S(2)}) collective-permute-start(f32[128,1152]{1,0:T(8,128)} %get-tuple-element.300.refs_11_), channel_id=1, source_target_pairs={{0,1},{1,0},{2,3},{3,2},{4,5},{5,4},{6,7},{7,6},{8,9},{9,8},{10,11... | collective-permute-start | bytes 1769480 | tf_op jit(solution)/shard_map/ppermute | solution.py:1350
  195.4 18.2 %collective-permute-start.37 = (f32[128,1152]{1,0:T(8,128)}, f32[128,1152]{1,0:T(8,128)}, u32[]{:S(2)}, u32[]{:S(2)}) collective-permute-start(f32[128,1152]{1,0:T(8,128)} %get-tuple-element.301.refs_12_), channel_id=1, source_target_pairs={{0,1},{1,0},{2,3},{3,2},{4,5},{5,4},{6,7},{7,6},{8,9},{9,8},{10,11... | collective-permute-start | bytes 1769480 | tf_op jit(solution)/shard_map/ppermute | solution.py:1350
  213.5 133.2 %reduce-scatter.5.cloned.1.call-start = ((), (), s32[]{:S(2)}) async-start(), calls=%async_computation.6 | async-start | bytes 3440640 | tf_op jit(solution)/shard_map/reduce_scatter | solution.py:1536
  229.7 28.2 %collective-permute-start.42 = (f32[32,144]{1,0:T(8,128)S(1)}, f32[32,144]{1,0:T(8,128)S(1)}, u32[]{:S(2)}, u32[]{:S(2)}) collective-permute-start(f32[32,144]{1,0:T(8,128)S(1)} %reshape.118.refs_0_), channel_id=1, source_target_pairs={{0,8},{8,16},{16,24},{24,0},{1,9},{9,17},{17,25},{25,1},{2,10},{10... | collective-permute-start | bytes 55304 | tf_op jit(solution)/shard_map/ppermute | solution.py:1354
  229.8 28.2 %collective-permute-start.43 = (f32[32,144]{1,0:T(8,128)S(1)}, f32[32,144]{1,0:T(8,128)S(1)}, u32[]{:S(2)}, u32[]{:S(2)}) collective-permute-start(f32[32,144]{1,0:T(8,128)S(1)} %reshape.118.refs_0_), channel_id=1, source_target_pairs={{0,16},{8,24},{16,0},{24,8},{1,17},{9,25},{17,1},{25,9},{2,18},{10... | collective-permute-start | bytes 55304 | tf_op jit(solution)/shard_map/ppermute | solution.py:1354
  231.5 26.6 %collective-permute-start.44 = (f32[32,144]{1,0:T(8,128)S(1)}, f32[32,144]{1,0:T(8,128)S(1)}, u32[]{:S(2)}, u32[]{:S(2)}) collective-permute-start(f32[32,144]{1,0:T(8,128)S(1)} %reshape.118.refs_0_), channel_id=1, source_target_pairs={{0,24},{8,0},{16,8},{24,16},{1,25},{9,1},{17,9},{25,17},{2,26},{10... | collective-permute-start | bytes 55304 | tf_op jit(solution)/shard_map/ppermute | solution.py:1354
  238.5 19.6 %collective-permute-start.40 = (f32[144,1152]{1,0:T(8,128)}, f32[144,1152]{1,0:T(8,128)S(1)}, u32[]{:S(2)}, u32[]{:S(2)}) collective-permute-start(f32[144,1152]{1,0:T(8,128)} %get-tuple-element.329), channel_id=1, source_target_pairs={{0,2},{2,0},{1,3},{3,1},{4,6},{6,4},{5,7},{7,5},{8,10},{10,8},{9,1... | collective-permute-start | bytes 1990664 | tf_op jit(solution)/shard_map/ppermute | solution.py:1350
  239.0 19.1 %collective-permute-start.41 = (f32[4,72,640]{2,1,0:T(8,128)}, f32[4,72,640]{2,1,0:T(8,128)S(1)}, u32[]{:S(2)}, u32[]{:S(2)}) collective-permute-start(f32[4,72,640]{2,1,0:T(8,128)} %get-tuple-element.330), channel_id=1, source_target_pairs={{0,4},{4,0},{1,5},{5,1},{2,6},{6,2},{3,7},{7,3},{8,12},{12,8},{9,1... | collective-permute-start | bytes 2211848 | tf_op jit(solution)/shard_map/ppermute | solution.py:1350
  276.9 32.7 %collective-permute-start.49 = (f32[2,4,72,640]{3,2,1,0:T(8,128)}, f32[2,4,72,640]{3,2,1,0:T(8,128)S(1)}, u32[]{:S(2)}, u32[]{:S(2)}) collective-permute-start(f32[2,4,72,640]{3,2,1,0:T(8,128)} %get-tuple-element.337), channel_id=1, source_target_pairs={{0,2},{2,0},{1,3},{3,1},{4,6},{6,4},{5,7},{7,5},{8,10},{10,8},{9,1... | collective-permute-start | bytes 4423688 | tf_op jit(solution)/shard_map/ppermute | solution.py:1350
  278.4 29.2 %collective-permute-start.48 = (f32[2,144,1152]{2,1,0:T(8,128)}, f32[2,144,1152]{2,1,0:T(8,128)S(1)}, u32[]{:S(2)}, u32[]{:S(2)}) collective-permute-start(f32[2,144,1152]{2,1,0:T(8,128)} %get-tuple-element.335), channel_id=1, source_target_pairs={{0,4},{4,0},{1,5},{5,1},{2,6},{6,2},{3,7},{7,3},{8,12},{12,8},{9,1... | collective-permute-start | bytes 3981320 | tf_op jit(solution)/shard_map/ppermute | solution.py:1350
  338.9 18.9 %collective-permute-start.55 = (f32[80,720]{1,0:T(8,128)}, f32[80,720]{1,0:T(8,128)S(1)}, u32[]{:S(2)}, u32[]{:S(2)}) collective-permute-start(f32[80,720]{1,0:T(8,128)} %get-tuple-element.362), channel_id=1, source_target_pairs={{0,2},{2,0},{1,3},{3,1},{4,6},{6,4},{5,7},{7,5},{8,10},{10,8},{9,1... | collective-permute-start | bytes 691208 | tf_op jit(solution)/shard_map/ppermute | solution.py:1350
  340.3 17.5 %collective-permute-start.56 = (f32[80,720]{1,0:T(8,128)}, f32[80,720]{1,0:T(8,128)S(1)}, u32[]{:S(2)}, u32[]{:S(2)}) collective-permute-start(f32[80,720]{1,0:T(8,128)} %get-tuple-element.363), channel_id=1, source_target_pairs={{0,4},{4,0},{1,5},{5,1},{2,6},{6,2},{3,7},{7,3},{8,12},{12,8},{9,1... | collective-permute-start | bytes 691208 | tf_op jit(solution)/shard_map/ppermute | solution.py:1350
  342.0 18.9 %collective-permute-start.57 = (f32[80,720]{1,0:T(8,128)}, f32[80,720]{1,0:T(8,128)S(1)}, u32[]{:S(2)}, u32[]{:S(2)}) collective-permute-start(f32[80,720]{1,0:T(8,128)} %get-tuple-element.364), channel_id=1, source_target_pairs={{0,6},{6,0},{2,4},{4,2},{1,7},{7,1},{3,5},{5,3},{8,14},{14,8},{10,... | collective-permute-start | bytes 691208 | tf_op jit(solution)/shard_map/ppermute | solution.py:1373
  350.4 33.0 %collective-permute-start.52 = (f32[96,720]{1,0:T(8,128)}, f32[96,720]{1,0:T(8,128)S(1)}, u32[]{:S(2)}, u32[]{:S(2)}) collective-permute-start(f32[96,720]{1,0:T(8,128)} %get-tuple-element.354), channel_id=1, source_target_pairs={{0,2},{2,0},{1,3},{3,1},{4,6},{6,4},{5,7},{7,5},{8,10},{10,8},{9,1... | collective-permute-start | bytes 829448 | tf_op jit(solution)/shard_map/ppermute | solution.py:1350
  357.7 25.9 %collective-permute-start.53 = (f32[96,720]{1,0:T(8,128)}, f32[96,720]{1,0:T(8,128)S(1)}, u32[]{:S(2)}, u32[]{:S(2)}) collective-permute-start(f32[96,720]{1,0:T(8,128)} %get-tuple-element.355), channel_id=1, source_target_pairs={{0,4},{4,0},{1,5},{5,1},{2,6},{6,2},{3,7},{7,3},{8,12},{12,8},{9,1... | collective-permute-start | bytes 829448 | tf_op jit(solution)/shard_map/ppermute | solution.py:1350
  357.7 25.9 %collective-permute-start.54 = (f32[96,720]{1,0:T(8,128)}, f32[96,720]{1,0:T(8,128)S(1)}, u32[]{:S(2)}, u32[]{:S(2)}) collective-permute-start(f32[96,720]{1,0:T(8,128)} %get-tuple-element.356), channel_id=1, source_target_pairs={{0,6},{6,0},{2,4},{4,2},{1,7},{7,1},{3,5},{5,3},{8,14},{14,8},{10,... | collective-permute-start | bytes 829448 | tf_op jit(solution)/shard_map/ppermute | solution.py:1373
  357.8 25.6 %collective-permute-start.58 = (f32[36,1152]{1,0:T(8,128)}, f32[36,1152]{1,0:T(8,128)S(1)}, u32[]{:S(2)}, u32[]{:S(2)}) collective-permute-start(f32[36,1152]{1,0:T(8,128)} %get-tuple-element.365), channel_id=1, source_target_pairs={{0,0},{2,8},{4,16},{6,24},{8,2},{10,10},{12,18},{14,26},{16,4},{18... | collective-permute-start | bytes 497672 | tf_op jit(solution)/shard_map/ppermute | solution.py:993
  361.0 40.6 %collective-permute-start.62 = (f32[144,1152]{1,0:T(8,128)S(1)}, f32[144,1152]{1,0:T(8,128)S(1)}, u32[]{:S(2)}, u32[]{:S(2)}) collective-permute-start(f32[144,1152]{1,0:T(8,128)S(1)} %copy-done.74), channel_id=1, source_target_pairs={{0,2},{2,0},{1,3},{3,1},{4,6},{6,4},{5,7},{7,5},{8,10},{10,8},{9,1... | collective-permute-start | bytes 1990664 | tf_op jit(solution)/shard_map/ppermute | solution.py:1350
  383.5 17.3 %collective-permute-start.61 = (f32[2,72,640]{2,1,0:T(8,128)S(1)}, f32[2,72,640]{2,1,0:T(8,128)S(1)}, u32[]{:S(2)}, u32[]{:S(2)}) collective-permute-start(f32[2,72,640]{2,1,0:T(8,128)S(1)} %copy-done.45), channel_id=1, source_target_pairs={{0,24},{8,0},{16,8},{24,16},{1,25},{9,1},{17,9},{25,17},{2,26},{10... | collective-permute-start | bytes 1105928 | tf_op jit(solution)/shard_map/ppermute | solution.py:1354
  (126 other events, 779.9 us)
Sparse Core Ops, SparseCore 0:
  9.7 52.9 all-gather.4
  67.1 53.1 all-gather.6
  122.6 50.5 all-gather.8
  174.6 50.5 all-gather.10
  227.3 52.6 reduce-scatter.6
  284.8 51.9 reduce-scatter.4

commit v5 on v4

--- a/solution.py
+++ b/solution.py
@@ -1567,10 +1567,14 @@
     moves.finish()
     feeds = [moves.found["feed", layer] for layer in range(depth)]
     blocks = feed_deal(depth, line, ids, [part for inner, _ in feeds for part in inner])
-    tokens_of[0], own_block, first_block, *blocks = gate(
-        [tokens_of[0], blocks[0], shift(blocks[1], line), *blocks[2:]]
-    )
-    blocks = [own_block, first_block, *[shift(block, line, by) for by, block in enumerate(blocks, 2)]]
+    early = (1, line - 1)
+    moved = {by: shift(blocks[by], line, by) for by in range(1, line) if by in early}
+    tokens_of[0], *held = gate(
+        [tokens_of[0], *[moved.get(by, block) for by, block in enumerate(blocks)]]
+    )
+    blocks = [
+        block if by == 0 or by in early else shift(block, line, by) for by, block in enumerate(held)
+    ]
     deal(0)
     moves.finish()
     token, time, table, projection, gain, shifts, bias = join_attention(

time: 418 us -> 416 us (level)
  waiting for transfers between devices: 115 us -> 90.8 us
  starting transfers between devices: 58.2 us -> 78.5 us
    ppermute x2, waiting for transfers between devices: 26.8 us -> 7.43 us  [attention_deal(): lax.ppermute(projection, LINES, [(GROUP * z + j, line * j + z) for z in r...]
    ppermute x12, starting transfers between devices: 15.3 us -> 27 us  [shift(): lax.ppermute(value, 'line', [(i, (i + by) % line) for i in range(line)])]
    ppermute x42, starting transfers between devices: 27.5 us -> 35.2 us  [swap(): return lax.ppermute(value, axis, [(0, 1), (1, 0)])]
    unnamed x178 -> x174, local copies, waits for them, and re-layouts: 27.1 us -> 27.1 us
  transfers between devices with their start and end apart: 69 -> 69, of which waited for: 26 -> 25; matrix products, arithmetic and copies ran while one was open for 3% -> 3% of each run, Pallas kernels for 44% -> 44%
where the time goes in v5:
time: 416 us; the launch traced here: 410 us
  Pallas kernels  185 us (44%)
  waiting for transfers between devices  90.8 us (22%)
  starting transfers between devices  78.5 us (19%)
  local copies, waits for them, and re-layouts  31.7 us (8%)
  between operations  15.2 us (4%)
  other arithmetic  4.91 us (1%)
    pallas_call x9, Pallas kernels, plain(): pl.pallas_call(body, in_specs=[*[pl.BlockSpec(memory_space=pltpu.SMEM)] *...  82.9 us
    pallas_call x4, Pallas kernels, call(): return lambda *operands: made(*operands, *map(in_hbm, after))  71.7 us
    ppermute x42, waiting for transfers between devices, swap(): return lax.ppermute(value, axis, [(0, 1), (1, 0)])  65.1 us
    ppermute x42, starting transfers between devices, swap(): return lax.ppermute(value, axis, [(0, 1), (1, 0)])  35.2 us
    unnamed x174, local copies, waits for them, and re-layouts  27.1 us
    ppermute x12, starting transfers between devices, shift(): lax.ppermute(value, 'line', [(i, (i + by) % line) for i in range(line)])  27 us
    pallas_call x7, Pallas kernels, whole_call(): pl.pallas_call(kernel, in_specs=[*[pl.BlockSpec(memory_space=pltpu.SMEM)]...  25.8 us
    ppermute x7, starting transfers between devices, swap_corner(): return lax.ppermute(value, ('col', 'row'), [(0, 3), (3, 0), (1, 2), (2, 1)])  10.7 us
  transfers between devices with their start and end apart: 69, of which 25 were waited for; matrix products, arithmetic and copies ran while one was open for 3% of the time, Pallas kernels for 44%

profile of v5, /device:TPU:2, one launch (start us, length us, event | category | flops | bytes accessed | tf_op | source)
XLA Modules:
  0.0 409.9 jit_solution(17965381661573265783)
XLA Ops:
  9.8 4.2 %convolution_bitcast_fusion.refs_7_.refs_9_ = f32[2,2,4,576]{3,2,1,0:T(4,128)S(1)} fusion(bf16[2,2,1152,576]{2,3,1,0:T(8,128)(2,1)} %param.19, f32[1152]{0:T(1024)S(1)} %fusion.11, f32[4]{0:T(128)S(1)} %convert_bitcast_fusion, pred[1152]{0:T(1024)(128)(4,1)S(1)} %iota_compare_fusion.1), kind=kOutput, calls=%fused_computation.1 | convolution fusion | flops 21247488 | bytes 5351056 | tf_op jit(solution)/shard_map/dot_general | solution.py:1415
  18.3 4.3 %expand_table.1 = (f32[16,16,512]{2,1,0:T(8,128)}, f32[16,8,128]{2,1,0:T(8,128)}) custom-call(f32[16,1024]{1,0:T(8,128)} %bitcast.24), custom_call_target="tpu_custom_call" | custom-call | tf_op jit(solution)/shard_map/expand_table/pallas_call | solution.py:136
  23.4 8.2 %attend_0.1 = (f32[256,1152]{1,0:T(8,128)}, f32[256,1152]{1,0:T(8,128)}, f32[128,1152]{1,0:T(8,128)}, bf16[3,256,576]{2,1,0:T(8,128)(2,1)}, f32[256,1152]{1,0:T(8,128)}, /*index=5*/f32[8,256,256]{2,1,0:T(8,128)}) custom-call(s32[5]{0:T(128)S(1)} %stack.22.refs_0_.ids, f32[2,2,1152]{2,1,0:T(2,128)S(1)} %copy-done, f32[2,2,1152]{2,1,0:T(2,128)S(1)} %copy-done.5, ...), custom_call_target="tpu_custom_call" | custom-call | flops 13589544960 | bytes 100270080 | tf_op jit(solution)/shard_map/attend_0/pallas_call | solution.py:295
  36.4 9.6 %feed_0.1 = (f32[256,1152]{1,0:T(8,128)}, f32[128,1152]{1,0:T(8,128)}, f32[256,2304]{1,0:T(8,128)}, f32[256,1152]{1,0:T(8,128)}) custom-call(s32[5]{0:T(128)S(1)} %stack.22.refs_0_.ids, f32[2,2,1152]{2,1,0:T(2,128)S(1)} %copy-done, f32[2,2,1152]{2,1,0:T(2,128)S(1)} %copy-done.5, f32[2,2,1152]{2,1,0:T(2,128)S(1)} %copy-done.1, ...), custom_call_target="tpu_custom_call" | custom-call | flops 27179089920 | bytes 200540160 | tf_op jit(solution)/shard_map/feed_0/pallas_call | solution.py:295
  53.7 9.3 %attend_1.1 = (f32[256,1152]{1,0:T(8,128)}, f32[256,1152]{1,0:T(8,128)}, f32[128,1152]{1,0:T(8,128)}, bf16[3,256,576]{2,1,0:T(8,128)(2,1)}, f32[256,1152]{1,0:T(8,128)}, /*index=5*/f32[8,256,256]{2,1,0:T(8,128)}) custom-call(s32[5]{0:T(128)S(1)} %stack.22.refs_0_.ids, f32[2,2,1152]{2,1,0:T(2,128)S(1)} %copy-done, f32[2,2,1152]{2,1,0:T(2,128)S(1)} %copy-done.5, ...), custom_call_target="tpu_custom_call" | custom-call | flops 13589544960 | bytes 100270080 | tf_op jit(solution)/shard_map/attend_1/pallas_call | solution.py:295
  77.6 9.5 %feed_1.1 = (f32[256,1152]{1,0:T(8,128)}, f32[128,1152]{1,0:T(8,128)}, f32[256,2304]{1,0:T(8,128)}, f32[256,1152]{1,0:T(8,128)}) custom-call(s32[5]{0:T(128)S(1)} %stack.22.refs_0_.ids, f32[2,2,1152]{2,1,0:T(2,128)S(1)} %copy-done, f32[2,2,1152]{2,1,0:T(2,128)S(1)} %copy-done.5, f32[2,2,1152]{2,1,0:T(2,128)S(1)} %copy-done.1, ...), custom_call_target="tpu_custom_call" | custom-call | flops 27179089920 | bytes 200540160 | tf_op jit(solution)/shard_map/feed_1/pallas_call | solution.py:295
  96.5 9.0 %feed_back_1.1 = (f32[256,1152]{1,0:T(8,128)}, f32[128,1152]{1,0:T(8,128)}, f32[8,1152]{1,0:T(8,128)}, f32[256,1152]{1,0:T(8,128)}) custom-call(s32[5]{0:T(128)S(1)} %stack.22.refs_0_.ids, f32[2,2,1152]{2,1,0:T(2,128)S(1)} %copy-done, bf16[256,1152]{1,0:T(8,128)(2,1)} %refs_2_.9, f32[256,2304]{1,0:T(8,128)} %get-tuple-element.245.refs_3_, ...), custom_call_target="tpu_custom_call" | custom-call | flops 27179089920 | bytes 200540160 | tf_op jit(solution)/shard_map/feed_back_1/pallas_call | solution.py:295
  105.6 3.0 collective-permute-done.18.refs_1_
  114.0 11.3 %attend_back_1.1 = (f32[256,1152]{1,0:T(8,128)}, f32[128,1152]{1,0:T(8,128)}, f32[8,1152]{1,0:T(8,128)}, f32[256,1152]{1,0:T(8,128)}) custom-call(s32[5]{0:T(128)S(1)} %stack.22.refs_0_.ids, f32[2,2,1152]{2,1,0:T(2,128)S(1)} %copy-done, f32[256,1152]{1,0:T(8,128)} %get-tuple-element.246.refs_2_, f32[256,1152]{1,0:T(8,128)} %get-tuple-element.254.refs_3_, ...), custom_call_target="tpu_custom_call" | custom-call | flops 35064381440 | bytes 123863040 | tf_op jit(solution)/shard_map/attend_back_1/pallas_call | solution.py:295
  130.3 10.2 %feed_back_0.1 = (f32[256,1152]{1,0:T(8,128)}, f32[128,1152]{1,0:T(8,128)}, f32[8,1152]{1,0:T(8,128)}, f32[256,1152]{1,0:T(8,128)}) custom-call(s32[5]{0:T(128)S(1)} %stack.22.refs_0_.ids, f32[2,2,1152]{2,1,0:T(2,128)S(1)} %copy-done, f32[256,1152]{1,0:T(8,128)} %get-tuple-element.258.refs_2_.refs_9_, f32[256,1152]{1,0:T(8,128)} %get-tuple-element.265.refs_3_, ...), custom_call_target="tpu_custom_call" | custom-call | flops 27179089920 | bytes 200540160 | tf_op jit(solution)/shard_map/feed_back_0/pallas_call | solution.py:295
  148.6 11.4 %attend_back_0.1 = (f32[256,1152]{1,0:T(8,128)}, f32[128,1152]{1,0:T(8,128)}, f32[8,1152]{1,0:T(8,128)}, f32[256,1152]{1,0:T(8,128)}) custom-call(s32[5]{0:T(128)S(1)} %stack.22.refs_0_.ids, f32[2,2,1152]{2,1,0:T(2,128)S(1)} %copy-done, f32[256,1152]{1,0:T(8,128)} %get-tuple-element.268.refs_2_, f32[256,1152]{1,0:T(8,128)} %get-tuple-element.274.refs_3_, ...), custom_call_target="tpu_custom_call" | custom-call | flops 35064381440 | bytes 123863040 | tf_op jit(solution)/shard_map/attend_back_0/pallas_call | solution.py:295
  167.3 4.2 %finish.1 = (bf16[256,1152]{1,0:T(8,128)(2,1)}, f32[8,1152]{1,0:T(8,128)}) custom-call(f32[2,2,1152]{2,1,0:T(2,128)S(1)} %copy-done, f32[256,1152]{1,0:T(8,128)} %get-tuple-element.278.refs_1_.refs_9_, f32[256,1152]{1,0:T(8,128)} %get-tuple-element.286.refs_2_, f32[256,1152]{1,0:T(8,128)} %get-tuple-element.287.refs_3_, f32[256,1152]{1,0:T(8,128)} %get-tuple-element.202.refs_4_), custom_call_target="tpu_custom_call" | custom-call | bytes 58982400 | tf_op jit(solution)/shard_map/finish/pallas_call | solution.py:295
  173.2 17.9 %feed_gradients_1.1 = (f32[2,144,1152]{2,1,0:T(8,128)}, f32[2,144,1152]{2,1,0:T(8,128)}, f32[2,4,72,640]{3,2,1,0:T(8,128)}, f32[2,4,72,640]{3,2,1,0:T(8,128)}) custom-call(s32[5]{0:T(128)S(1)} %stack.22.refs_0_.ids, f32[1024,1152]{1,0:T(8,128)} %all-gather.9.cloned.1.call-done.refs_1_, f32[1024,1152]{1,0:T(8,128)} %get-tuple-element.294.refs_2_, ...), custom_call_target="tpu_custom_call" | custom-call | flops 36238786560 | bytes 127401984 | tf_op jit(solution)/shard_map/feed_gradients_1/pallas_call | solution.py:94
  195.9 17.6 %attention_gradients_1.1 = (f32[1760,384]{1,0:T(8,128)}, f32[4,2,4,144]{3,2,1,0:T(4,128)}) custom-call(s32[5]{0:T(128)S(1)} %stack.22.refs_0_.ids, s32[4]{0:T(128)S(1)} %convert_reduce_fusion.refs_1_, f32[256,1152]{1,0:T(8,128)} %get-tuple-element.302.refs_2_, f32[128,1152]{1,0:T(8,128)} %get-tuple-element.248.refs_3_, ...), custom_call_target="tpu_custom_call" | custom-call | flops 29192355840 | bytes 88473600 | tf_op jit(solution)/shard_map/attention_gradients_1/pallas_call | solution.py:94
  213.6 9.1 %collective-permute-done.38.refs_5_ = f32[2,144,1152]{2,1,0:T(8,128)S(1)} collective-permute-done((f32[2,144,1152]{2,1,0:T(8,128)}, f32[2,144,1152]{2,1,0:T(8,128)S(1)}, u32[]{:S(2)}, u32[]{:S(2)}) %collective-permute-start.38) | collective-permute-done | bytes 1327136 | tf_op jit(solution)/shard_map/ppermute | solution.py:1350
  222.7 5.2 %collective-permute-done.39.refs_6_ = f32[2,4,72,640]{3,2,1,0:T(8,128)S(1)} collective-permute-done((f32[2,4,72,640]{3,2,1,0:T(8,128)}, f32[2,4,72,640]{3,2,1,0:T(8,128)S(1)}, u32[]{:S(2)}, u32[]{:S(2)}) %collective-permute-start.39) | collective-permute-done | bytes 1474592 | tf_op jit(solution)/shard_map/ppermute | solution.py:1350
  234.0 4.5 %feed_halve_1.1 = (f32[144,1152]{1,0:T(8,128)}, f32[144,1152]{1,0:T(8,128)}, f32[4,72,640]{2,1,0:T(8,128)}, f32[4,72,640]{2,1,0:T(8,128)}) custom-call(s32[5]{0:T(128)S(1)} %stack.22.refs_0_.ids, f32[2,144,1152]{2,1,0:T(8,128)} %get-tuple-element.309.refs_24_.outer_keep, f32[2,144,1152]{2,1,0:T(8,128)} %get-tuple-element.326.outer_half, ...), custom_call_target="tpu_custom_call" | custom-call | flops 20000000000 | bytes 66666664 | tf_op jit(solution)/shard_map/feed_halve_1/pallas_call | solution.py:871
  239.7 18.4 %attention_gradients_0.1 = (f32[1792,384]{1,0:T(8,128)}, f32[4,2,4,144]{3,2,1,0:T(4,128)}) custom-call(s32[5]{0:T(128)S(1)} %stack.22.refs_0_.ids, s32[4]{0:T(128)S(1)} %convert_reduce_fusion.refs_1_, f32[256,1152]{1,0:T(8,128)} %get-tuple-element.289.refs_2_, f32[128,1152]{1,0:T(8,128)} %get-tuple-element.220.refs_3_, ...), custom_call_target="tpu_custom_call" | custom-call | flops 29192355840 | bytes 88473600 | tf_op jit(solution)/shard_map/attention_gradients_0/pallas_call | solution.py:94
  259.2 17.8 %feed_gradients_0.1 = (f32[2,144,1152]{2,1,0:T(8,128)}, f32[2,144,1152]{2,1,0:T(8,128)}, f32[2,4,72,640]{3,2,1,0:T(8,128)}, f32[2,4,72,640]{3,2,1,0:T(8,128)}) custom-call(s32[5]{0:T(128)S(1)} %stack.22.refs_0_.ids, f32[1024,1152]{1,0:T(8,128)} %get-tuple-element.323.refs_1_, f32[1024,1152]{1,0:T(8,128)} %get-tuple-element.324.refs_2_, ...), custom_call_target="tpu_custom_call" | custom-call | flops 36238786560 | bytes 127401984 | tf_op jit(solution)/shard_map/feed_gradients_0/pallas_call | solution.py:94
  286.9 20.8 %collective-permute-done.48.outer_half = f32[2,144,1152]{2,1,0:T(8,128)} collective-permute-done((f32[2,144,1152]{2,1,0:T(8,128)}, f32[2,144,1152]{2,1,0:T(8,128)}, u32[]{:S(2)}, u32[]{:S(2)}) %collective-permute-start.48) | collective-permute-done | bytes 1327136 | tf_op jit(solution)/shard_map/ppermute | solution.py:1350
  310.9 4.5 %feed_halve_0.1 = (f32[144,1152]{1,0:T(8,128)}, f32[144,1152]{1,0:T(8,128)}, f32[4,72,640]{2,1,0:T(8,128)}, f32[4,72,640]{2,1,0:T(8,128)}) custom-call(s32[5]{0:T(128)S(1)} %stack.22.refs_0_.ids, f32[2,144,1152]{2,1,0:T(8,128)} %get-tuple-element.334.outer_keep, f32[2,144,1152]{2,1,0:T(8,128)} %collective-permute-done.48.outer_half, ...), custom_call_target="tpu_custom_call" | custom-call | flops 20000000000 | bytes 66666664 | tf_op jit(solution)/shard_map/feed_halve_0/pallas_call | solution.py:871
  318.1 13.3 %collective-permute-done.50.refs_1_ = f32[4,72,640]{2,1,0:T(8,128)S(1)} collective-permute-done((f32[4,72,640]{2,1,0:T(8,128)}, f32[4,72,640]{2,1,0:T(8,128)S(1)}, u32[]{:S(2)}, u32[]{:S(2)}) %collective-permute-start.50) | collective-permute-done | bytes 737312 | tf_op jit(solution)/shard_map/ppermute | solution.py:1350
  332.2 3.1 feed_deal.1
  335.8 3.5 collective-permute-start.52
  345.7 3.2 collective-permute-done.51.refs_2_
  352.2 3.1 attention_deal_0.1
  355.2 10.5 %collective-permute-start.53 = (f32[96,720]{1,0:T(8,128)}, f32[96,720]{1,0:T(8,128)S(1)}, u32[]{:S(2)}, u32[]{:S(2)}) collective-permute-start(f32[96,720]{1,0:T(8,128)} %get-tuple-element.354), channel_id=1, source_target_pairs={{0,2},{2,0},{1,3},{3,1},{4,6},{6,4},{5,7},{7,5},{8,10},{10,8},{9,1... | collective-permute-start | bytes 829448 | tf_op jit(solution)/shard_map/ppermute | solution.py:1350
  371.9 7.4 %collective-permute-done.59.refs_8_ = f32[36,1152]{1,0:T(8,128)S(1)} collective-permute-done((f32[36,1152]{1,0:T(8,128)}, f32[36,1152]{1,0:T(8,128)S(1)}, u32[]{:S(2)}, u32[]{:S(2)}) %collective-permute-start.59) | collective-permute-done | bytes 165920 | tf_op jit(solution)/shard_map/ppermute | solution.py:993
  379.3 8.6 %collective-permute-start.61 = (f32[2,72,640]{2,1,0:T(8,128)S(1)}, f32[2,72,640]{2,1,0:T(8,128)S(1)}, u32[]{:S(2)}, u32[]{:S(2)}) collective-permute-start(f32[2,72,640]{2,1,0:T(8,128)S(1)} %copy-done.45), channel_id=1, source_target_pairs={{0,16},{8,24},{16,0},{24,8},{1,17},{9,25},{17,1},{25,9},{2,18},{10... | collective-permute-start | bytes 1105928 | tf_op jit(solution)/shard_map/ppermute | solution.py:1354
  388.9 3.7 join_attention.1
  392.6 4.8 %collective-permute-done.61.refs_3_ = f32[2,72,640]{2,1,0:T(8,128)S(1)} collective-permute-done((f32[2,72,640]{2,1,0:T(8,128)S(1)}, f32[2,72,640]{2,1,0:T(8,128)S(1)}, u32[]{:S(2)}, u32[]{:S(2)}) %collective-permute-start.61) | collective-permute-done | bytes 368672 | tf_op jit(solution)/shard_map/ppermute | solution.py:1354
  399.0 3.9 join_feed.1
  (362 shorter events, 119.5 us)
Async XLA Ops:
  7.2 58.6 %all-gather.5.cloned.1.call-start = ((), (), s32[]{:S(2)}) async-start(), calls=%async_computation.2 | async-start | bytes 5308416 | tf_op jit(solution)/shard_map/all_gather | solution.py:1358
  9.1 116.2 %all-gather.7.cloned.1.call-start = ((), (), s32[]{:S(2)}) async-start(), calls=%async_computation.3 | async-start | bytes 5308416 | tf_op jit(solution)/shard_map/all_gather | solution.py:1358
  14.7 16.9 %collective-permute-start = (f32[24,576]{1,0:T(8,128)S(1)}, f32[24,576]{1,0:T(8,128)S(1)}, u32[]{:S(2)}, u32[]{:S(2)}) collective-permute-start(f32[24,576]{1,0:T(8,128)S(1)} %select_maximum_fusion.refs_18_), channel_id=1, source_target_pairs={{0,2},{2,0},{1,3},{3,1},{4,6},{6,4},{5,7},{7,5},{8,10},{10,8},{9,1... | collective-permute-start | bytes 165896 | tf_op jit(solution)/shard_map/ppermute | solution.py:1350
  14.8 16.8 %collective-permute-start.1 = (f32[24,576]{1,0:T(8,128)S(1)}, f32[24,576]{1,0:T(8,128)S(1)}, u32[]{:S(2)}, u32[]{:S(2)}) collective-permute-start(f32[24,576]{1,0:T(8,128)S(1)} %select_maximum_fusion.refs_18_), channel_id=1, source_target_pairs={{0,4},{4,0},{1,5},{5,1},{2,6},{6,2},{3,7},{7,3},{8,12},{12,8},{9,1... | collective-permute-start | bytes 165896 | tf_op jit(solution)/shard_map/ppermute | solution.py:1350
  67.0 106.2 %all-gather.9.cloned.1.call-start = ((), (), s32[]{:S(2)}) async-start(), calls=%async_computation.4 | async-start | bytes 5308416 | tf_op jit(solution)/shard_map/all_gather | solution.py:1358
  109.8 118.1 %all-gather.11.cloned.1.call-start = ((), (), s32[]{:S(2)}) async-start(), calls=%async_computation.5 | async-start | bytes 5308416 | tf_op jit(solution)/shard_map/all_gather | solution.py:1358
  146.2 138.5 %reduce-scatter.7.cloned.1.call-start = ((), (), s32[]{:S(2)}) async-start(), calls=%async_computation.7 | async-start | bytes 3379200
  162.8 29.9 %collective-permute-start.32 = (f32[128,1152]{1,0:T(8,128)}, f32[128,1152]{1,0:T(8,128)S(1)}, u32[]{:S(2)}, u32[]{:S(2)}) collective-permute-start(f32[128,1152]{1,0:T(8,128)} %get-tuple-element.298), channel_id=1, source_target_pairs={{0,2},{2,0},{1,3},{3,1},{4,6},{6,4},{5,7},{7,5},{8,10},{10,8},{9,1... | collective-permute-start | bytes 1769480 | tf_op jit(solution)/shard_map/ppermute | solution.py:1350
  164.3 29.7 %collective-permute-start.33 = (f32[128,1152]{1,0:T(8,128)}, f32[128,1152]{1,0:T(8,128)}, u32[]{:S(2)}, u32[]{:S(2)}) collective-permute-start(f32[128,1152]{1,0:T(8,128)} %get-tuple-element.298), channel_id=1, source_target_pairs={{0,4},{4,0},{1,5},{5,1},{2,6},{6,2},{3,7},{7,3},{8,12},{12,8},{9,1... | collective-permute-start | bytes 1769480 | tf_op jit(solution)/shard_map/ppermute | solution.py:1350
  165.6 28.5 %collective-permute-start.34 = (f32[128,1152]{1,0:T(8,128)}, f32[128,1152]{1,0:T(8,128)}, u32[]{:S(2)}, u32[]{:S(2)}) collective-permute-start(f32[128,1152]{1,0:T(8,128)} %get-tuple-element.298), channel_id=1, source_target_pairs={{0,6},{6,0},{2,4},{4,2},{1,7},{7,1},{3,5},{5,3},{8,14},{14,8},{10,... | collective-permute-start | bytes 1769480 | tf_op jit(solution)/shard_map/ppermute | solution.py:1373
  167.3 26.7 %collective-permute-start.31 = (f32[128,1152]{1,0:T(8,128)}, f32[128,1152]{1,0:T(8,128)S(1)}, u32[]{:S(2)}, u32[]{:S(2)}) collective-permute-start(f32[128,1152]{1,0:T(8,128)} %get-tuple-element.297.refs_12_), channel_id=1, source_target_pairs={{0,1},{1,0},{2,3},{3,2},{4,5},{5,4},{6,7},{7,6},{8,9},{9,8},{10,11... | collective-permute-start | bytes 1769480 | tf_op jit(solution)/shard_map/ppermute | solution.py:1350
  191.1 31.5 %collective-permute-start.38 = (f32[2,144,1152]{2,1,0:T(8,128)}, f32[2,144,1152]{2,1,0:T(8,128)S(1)}, u32[]{:S(2)}, u32[]{:S(2)}) collective-permute-start(f32[2,144,1152]{2,1,0:T(8,128)} %get-tuple-element.312), channel_id=1, source_target_pairs={{0,4},{4,0},{1,5},{5,1},{2,6},{6,2},{3,7},{7,3},{8,12},{12,8},{9,1... | collective-permute-start | bytes 3981320 | tf_op jit(solution)/shard_map/ppermute | solution.py:1350
  193.5 34.4 %collective-permute-start.39 = (f32[2,4,72,640]{3,2,1,0:T(8,128)}, f32[2,4,72,640]{3,2,1,0:T(8,128)S(1)}, u32[]{:S(2)}, u32[]{:S(2)}) collective-permute-start(f32[2,4,72,640]{3,2,1,0:T(8,128)} %get-tuple-element.313), channel_id=1, source_target_pairs={{0,2},{2,0},{1,3},{3,1},{4,6},{6,4},{5,7},{7,5},{8,10},{10,8},{9,1... | collective-permute-start | bytes 4423688 | tf_op jit(solution)/shard_map/ppermute | solution.py:1350
  194.9 18.7 %collective-permute-start.35 = (f32[128,1152]{1,0:T(8,128)}, f32[128,1152]{1,0:T(8,128)}, u32[]{:S(2)}, u32[]{:S(2)}) collective-permute-start(f32[128,1152]{1,0:T(8,128)} %get-tuple-element.299.refs_10_), channel_id=1, source_target_pairs={{0,1},{1,0},{2,3},{3,2},{4,5},{5,4},{6,7},{7,6},{8,9},{9,8},{10,11... | collective-permute-start | bytes 1769480 | tf_op jit(solution)/shard_map/ppermute | solution.py:1350
  194.9 18.7 %collective-permute-start.36 = (f32[128,1152]{1,0:T(8,128)}, f32[128,1152]{1,0:T(8,128)}, u32[]{:S(2)}, u32[]{:S(2)}) collective-permute-start(f32[128,1152]{1,0:T(8,128)} %get-tuple-element.300.refs_11_), channel_id=1, source_target_pairs={{0,1},{1,0},{2,3},{3,2},{4,5},{5,4},{6,7},{7,6},{8,9},{9,8},{10,11... | collective-permute-start | bytes 1769480 | tf_op jit(solution)/shard_map/ppermute | solution.py:1350
  195.4 18.2 %collective-permute-start.37 = (f32[128,1152]{1,0:T(8,128)}, f32[128,1152]{1,0:T(8,128)}, u32[]{:S(2)}, u32[]{:S(2)}) collective-permute-start(f32[128,1152]{1,0:T(8,128)} %get-tuple-element.301.refs_12_), channel_id=1, source_target_pairs={{0,1},{1,0},{2,3},{3,2},{4,5},{5,4},{6,7},{7,6},{8,9},{9,8},{10,11... | collective-permute-start | bytes 1769480 | tf_op jit(solution)/shard_map/ppermute | solution.py:1350
  213.5 137.9 %reduce-scatter.5.cloned.1.call-start = ((), (), s32[]{:S(2)}) async-start(), calls=%async_computation.6 | async-start | bytes 3440640 | tf_op jit(solution)/shard_map/reduce_scatter | solution.py:1536
  229.8 28.3 %collective-permute-start.42 = (f32[32,144]{1,0:T(8,128)S(1)}, f32[32,144]{1,0:T(8,128)S(1)}, u32[]{:S(2)}, u32[]{:S(2)}) collective-permute-start(f32[32,144]{1,0:T(8,128)S(1)} %reshape.118.refs_0_), channel_id=1, source_target_pairs={{0,8},{8,16},{16,24},{24,0},{1,9},{9,17},{17,25},{25,1},{2,10},{10... | collective-permute-start | bytes 55304 | tf_op jit(solution)/shard_map/ppermute | solution.py:1354
  229.8 28.3 %collective-permute-start.43 = (f32[32,144]{1,0:T(8,128)S(1)}, f32[32,144]{1,0:T(8,128)S(1)}, u32[]{:S(2)}, u32[]{:S(2)}) collective-permute-start(f32[32,144]{1,0:T(8,128)S(1)} %reshape.118.refs_0_), channel_id=1, source_target_pairs={{0,16},{8,24},{16,0},{24,8},{1,17},{9,25},{17,1},{25,9},{2,18},{10... | collective-permute-start | bytes 55304 | tf_op jit(solution)/shard_map/ppermute | solution.py:1354
  231.5 26.6 %collective-permute-start.44 = (f32[32,144]{1,0:T(8,128)S(1)}, f32[32,144]{1,0:T(8,128)S(1)}, u32[]{:S(2)}, u32[]{:S(2)}) collective-permute-start(f32[32,144]{1,0:T(8,128)S(1)} %reshape.118.refs_0_), channel_id=1, source_target_pairs={{0,24},{8,0},{16,8},{24,16},{1,25},{9,1},{17,9},{25,17},{2,26},{10... | collective-permute-start | bytes 55304 | tf_op jit(solution)/shard_map/ppermute | solution.py:1354
  238.5 19.6 %collective-permute-start.40 = (f32[144,1152]{1,0:T(8,128)}, f32[144,1152]{1,0:T(8,128)S(1)}, u32[]{:S(2)}, u32[]{:S(2)}) collective-permute-start(f32[144,1152]{1,0:T(8,128)} %get-tuple-element.329), channel_id=1, source_target_pairs={{0,2},{2,0},{1,3},{3,1},{4,6},{6,4},{5,7},{7,5},{8,10},{10,8},{9,1... | collective-permute-start | bytes 1990664 | tf_op jit(solution)/shard_map/ppermute | solution.py:1350
  239.0 19.1 %collective-permute-start.41 = (f32[4,72,640]{2,1,0:T(8,128)}, f32[4,72,640]{2,1,0:T(8,128)S(1)}, u32[]{:S(2)}, u32[]{:S(2)}) collective-permute-start(f32[4,72,640]{2,1,0:T(8,128)} %get-tuple-element.330), channel_id=1, source_target_pairs={{0,4},{4,0},{1,5},{5,1},{2,6},{6,2},{3,7},{7,3},{8,12},{12,8},{9,1... | collective-permute-start | bytes 2211848 | tf_op jit(solution)/shard_map/ppermute | solution.py:1350
  277.0 32.7 %collective-permute-start.49 = (f32[2,4,72,640]{3,2,1,0:T(8,128)}, f32[2,4,72,640]{3,2,1,0:T(8,128)S(1)}, u32[]{:S(2)}, u32[]{:S(2)}) collective-permute-start(f32[2,4,72,640]{3,2,1,0:T(8,128)} %get-tuple-element.337), channel_id=1, source_target_pairs={{0,2},{2,0},{1,3},{3,1},{4,6},{6,4},{5,7},{7,5},{8,10},{10,8},{9,1... | collective-permute-start | bytes 4423688 | tf_op jit(solution)/shard_map/ppermute | solution.py:1350
  278.4 29.3 %collective-permute-start.48 = (f32[2,144,1152]{2,1,0:T(8,128)}, f32[2,144,1152]{2,1,0:T(8,128)}, u32[]{:S(2)}, u32[]{:S(2)}) collective-permute-start(f32[2,144,1152]{2,1,0:T(8,128)} %get-tuple-element.335), channel_id=1, source_target_pairs={{0,4},{4,0},{1,5},{5,1},{2,6},{6,2},{3,7},{7,3},{8,12},{12,8},{9,1... | collective-permute-start | bytes 3981320 | tf_op jit(solution)/shard_map/ppermute | solution.py:1350
  342.2 23.5 %collective-permute-start.56 = (f32[80,720]{1,0:T(8,128)}, f32[80,720]{1,0:T(8,128)S(1)}, u32[]{:S(2)}, u32[]{:S(2)}) collective-permute-start(f32[80,720]{1,0:T(8,128)} %get-tuple-element.362), channel_id=1, source_target_pairs={{0,2},{2,0},{1,3},{3,1},{4,6},{6,4},{5,7},{7,5},{8,10},{10,8},{9,1... | collective-permute-start | bytes 691208 | tf_op jit(solution)/shard_map/ppermute | solution.py:1350
  343.6 23.7 %collective-permute-start.57 = (f32[80,720]{1,0:T(8,128)}, f32[80,720]{1,0:T(8,128)S(1)}, u32[]{:S(2)}, u32[]{:S(2)}) collective-permute-start(f32[80,720]{1,0:T(8,128)} %get-tuple-element.363), channel_id=1, source_target_pairs={{0,4},{4,0},{1,5},{5,1},{2,6},{6,2},{3,7},{7,3},{8,12},{12,8},{9,1... | collective-permute-start | bytes 691208 | tf_op jit(solution)/shard_map/ppermute | solution.py:1350
  344.6 26.5 %collective-permute-start.58 = (f32[80,720]{1,0:T(8,128)}, f32[80,720]{1,0:T(8,128)S(1)}, u32[]{:S(2)}, u32[]{:S(2)}) collective-permute-start(f32[80,720]{1,0:T(8,128)} %get-tuple-element.364), channel_id=1, source_target_pairs={{0,6},{6,0},{2,4},{4,2},{1,7},{7,1},{3,5},{5,3},{8,14},{14,8},{10,... | collective-permute-start | bytes 691208 | tf_op jit(solution)/shard_map/ppermute | solution.py:1373
  355.2 32.7 %collective-permute-start.53 = (f32[96,720]{1,0:T(8,128)}, f32[96,720]{1,0:T(8,128)S(1)}, u32[]{:S(2)}, u32[]{:S(2)}) collective-permute-start(f32[96,720]{1,0:T(8,128)} %get-tuple-element.354), channel_id=1, source_target_pairs={{0,2},{2,0},{1,3},{3,1},{4,6},{6,4},{5,7},{7,5},{8,10},{10,8},{9,1... | collective-permute-start | bytes 829448 | tf_op jit(solution)/shard_map/ppermute | solution.py:1350
  365.7 22.3 %collective-permute-start.54 = (f32[96,720]{1,0:T(8,128)}, f32[96,720]{1,0:T(8,128)S(1)}, u32[]{:S(2)}, u32[]{:S(2)}) collective-permute-start(f32[96,720]{1,0:T(8,128)} %get-tuple-element.355), channel_id=1, source_target_pairs={{0,4},{4,0},{1,5},{5,1},{2,6},{6,2},{3,7},{7,3},{8,12},{12,8},{9,1... | collective-permute-start | bytes 829448 | tf_op jit(solution)/shard_map/ppermute | solution.py:1350
  365.7 22.2 %collective-permute-start.55 = (f32[96,720]{1,0:T(8,128)}, f32[96,720]{1,0:T(8,128)S(1)}, u32[]{:S(2)}, u32[]{:S(2)}) collective-permute-start(f32[96,720]{1,0:T(8,128)} %get-tuple-element.356), channel_id=1, source_target_pairs={{0,6},{6,0},{2,4},{4,2},{1,7},{7,1},{3,5},{5,3},{8,14},{14,8},{10,... | collective-permute-start | bytes 829448 | tf_op jit(solution)/shard_map/ppermute | solution.py:1373
  371.2 27.0 %collective-permute-start.62 = (f32[144,1152]{1,0:T(8,128)S(1)}, f32[144,1152]{1,0:T(8,128)S(1)}, u32[]{:S(2)}, u32[]{:S(2)}) collective-permute-start(f32[144,1152]{1,0:T(8,128)S(1)} %copy-done.72), channel_id=1, source_target_pairs={{0,2},{2,0},{1,3},{3,1},{4,6},{6,4},{5,7},{7,5},{8,10},{10,8},{9,1... | collective-permute-start | bytes 1990664 | tf_op jit(solution)/shard_map/ppermute | solution.py:1350
  379.3 18.1 %collective-permute-start.61 = (f32[2,72,640]{2,1,0:T(8,128)S(1)}, f32[2,72,640]{2,1,0:T(8,128)S(1)}, u32[]{:S(2)}, u32[]{:S(2)}) collective-permute-start(f32[2,72,640]{2,1,0:T(8,128)S(1)} %copy-done.45), channel_id=1, source_target_pairs={{0,16},{8,24},{16,0},{24,8},{1,17},{9,25},{17,1},{25,9},{2,18},{10... | collective-permute-start | bytes 1105928 | tf_op jit(solution)/shard_map/ppermute | solution.py:1354
  (124 other events, 762.8 us)
Sparse Core Ops, SparseCore 0:
  9.7 52.9 all-gather.4
  67.1 53.2 all-gather.6
  122.6 50.5 all-gather.8
  174.7 50.5 all-gather.10
  227.4 52.6 reduce-scatter.6
  284.8 52.0 reduce-scatter.4
